TPU v7x, 32 devices: a whole 2x2x4 slice. The times are simulated.
32 devices in a mesh: scen: 2 (over y), tm: 4 (over z), bus: 4 (over x, core).
Axes of the slice: x: 2, y: 2, z: 4, core: 2. Of those that a mesh axis runs over, the one named last changes fastest.
Arguments:
- gen_start: float32 [512, 2560], P(('scen', 'tm'), 'bus'), parts along dimension 0, may hold values from 0 to 1
- charge_start: float32 [512, 1024], P(('scen', 'tm'), 'bus'), parts along dimension 0, may hold values from -3 to 3
- load: bfloat16 [512, 17920], P(('scen', 'tm'), 'bus'), parts along dimension 0, may hold values from 0 to 0.19921875
- ptdf_tiles: bfloat16 [464, 128, 128], P('bus'), may hold values from -0.5 to 0.5
- tile_row: int32 [464], P('bus'), may hold values from 0 to 79
- tile_col: int32 [464], P('bus'), may hold values from 0 to 34
- gen_bus: int32 [2560], P('bus'), may hold values from 0 to 4479
- stor_bus: int32 [1024], P('bus'), may hold values from 0 to 4479
- gen_cost: float32 [2560], P('bus'), may hold values from 0 to 1
- gen_max: float32 [2560], P('bus'), may hold values from 0.5 to 3
- ramp_limit: float32 [2560], P('bus'), may hold values from 0.05 to 0.5
- stor_power: float32 [1024], P('bus'), may hold values from 0.3 to 2
- stor_loss: float32 [1024], P('bus'), may hold values from 0.02 to 0.3
- stor_cap: float32 [1024], P('bus'), may hold values from 0.5 to 3
- flow_limit: float32 [10240], replicated, may hold values from 0.5 to 2
Outputs:
- gen_next: float32 [512, 2560], P(('scen', 'tm'), 'bus'), parts along dimension 0
- charge_next: float32 [512, 1024], P(('scen', 'tm'), 'bus'), parts along dimension 0
- line_dual: float32 [512, 10240], P(('scen', 'tm'), 'bus'), parts along dimension 0
There are 2 independent parts, one for each index of `scen`. A program takes and returns all parts, laid end to end along the dimension named above; an argument that names none is the same for every part. Nothing has to cross between parts.
Inputs may be any that keep to these rules, and one draw needn't show every extreme that they name: Stored tile k lies in line tile tile_row[k] of the 80; pairs of tile_row and tile_col may repeat, and repeated tiles add. Stored tile k covers the buses 128 * tile_col[k] to 128 * tile_col[k] + 127 of the block (k // 116). `gen_bus`: A bus index within the block of generator i, which is block i // 640. `stor_bus`: A bus index within the block of storage unit s, which is block s // 256.
All inputs are finite; a program needn't handle non-finite values.
Results may differ from a plain program's by a relative error of at most 0.028.
Values may be sent and summed in bfloat16 or wider, within the bound.
No kernel may reach another device: no remote copies, remote signals or barrier semaphores. Data moves between devices by JAX's collectives and lax.ppermute only.
A program may use at most 128 MiB of HBM per device.

v0:
```python
import functools

import jax
import jax.numpy as jnp
from jax import lax
from jax.experimental import pallas as pl
from jax.experimental.pallas import tpu as pltpu
from jax.sharding import PartitionSpec as P

ITERS = 3
TAU = 0.5
SIGMA = 0.5
LANE = 128
LARGE, SMALL = 32, 8
KEPT = 160
F32 = jnp.float32
BF16 = jnp.bfloat16

NN = (((1,), (0,)), ((), ()))
NT = (((1,), (1,)), ((), ()))


def mxu(a, b, dims):
    return lax.dot_general(a, b, dims, preferred_element_type=F32)


def smem():
    return pl.BlockSpec(memory_space=pltpu.SMEM)


def vmem():
    return pl.BlockSpec(memory_space=pltpu.VMEM)


def hbm():
    return pl.BlockSpec(memory_space=pl.ANY)


def params(mib):
    return pltpu.CompilerParams(vmem_limit_bytes=mib * 1024 * 1024)


def cost(us):
    return pl.CostEstimate(flops=0, bytes_accessed=int(us * 3.0e6), transcendentals=0)


def lanes(at):
    return pl.ds(pl.multiple_of(at * LANE, LANE), LANE)


ROW, BLOCK, TILE, COLUMN, FIRST, START = range(6)


def plan_kernel(
    chunks, quarter_tiles,
    mine, gen_bus, stor_bus, tile_row, tile_col,
    place, sorted_bus, ents,
    tiles,
):
    units = place.shape[0]
    blocks = units // LANE
    kt = tile_row.shape[1]
    square = (LANE, LANE)
    sub = lax.broadcasted_iota(jnp.int32, square, 0).astype(F32)
    lane = lax.broadcasted_iota(jnp.int32, square, 1).astype(F32)
    eye = sub == lane

    def column(row):
        return jnp.sum(jnp.where(eye, jnp.broadcast_to(row, square), 0.0), axis=1, keepdims=True)

    def over_sub(mask, values):
        return jnp.sum(jnp.where(mask, values, 0.0), axis=0, keepdims=True)

    def over_lane(mask, values):
        return jnp.sum(jnp.where(mask, values, 0.0), axis=1, keepdims=True)

    bus = jnp.concatenate([gen_bus[...], stor_bus[...]], axis=1).astype(F32)
    unit = lax.broadcasted_iota(jnp.int32, (1, units), 1).astype(F32)
    key = bus * units + unit
    ordered = jnp.zeros((1, units), F32)
    starts = jnp.zeros((1, LANE), F32)
    stops = jnp.zeros((1, LANE), F32)
    for b in range(blocks):
        here = column(bus[:, b * LANE : (b + 1) * LANE])
        rank = over_lane(key < here * units + (sub[:, :1] + float(b * LANE)), 1.0)
        mine_at = rank == unit
        place[b * LANE : (b + 1) * LANE] = jnp.where(mine_at, 1.0, 0.0).astype(BF16)
        ordered += over_sub(mine_at, here)
        starts += over_sub(here < lane * LANE, 1.0)
        stops += over_sub(here < (lane + 1.0) * LANE, 1.0)
    for b in range(blocks):
        sorted_bus[b] = jnp.broadcast_to(column(ordered[:, b * LANE : (b + 1) * LANE]), square)

    tiles[...] = jnp.zeros_like(tiles)
    tiles[0:1, :kt] = tile_row[...]
    tiles[1:2, :kt] = tile_col[...]
    row, col = tiles[0:1], tiles[1:2].astype(F32)
    chunk = jnp.zeros_like(row)
    for d in range(1, chunks):
        chunk = chunk + (row >= d * quarter_tiles).astype(jnp.int32)
    relative = (((chunk ^ mine[0]) - chunk) * quarter_tiles + row).astype(F32)
    number = lane[:1]
    tile_key = jnp.where(number < kt, relative, float(chunks * quarter_tiles)) * LANE + number
    rank = over_sub(column(tile_key) < tile_key, 1.0)
    sorting = rank == sub
    relative, col, tile = (over_lane(sorting, x) for x in (relative, col, number))
    first, last = over_lane(lane == col, starts), over_lane(lane == col, stops)
    block = jnp.minimum(jnp.floor(first * (1.0 / LANE)), float(blocks - 1))
    until = jnp.floor((last - 1.0) * (1.0 / LANE))
    count = jnp.where(last > first, until - block + 1.0, 1.0)
    count = jnp.where(sub[:, :1] < kt, count, 0.0)
    at = over_lane(lane < sub, over_sub(eye, count))
    entry = lax.broadcasted_iota(jnp.int32, (1, ents.shape[1]), 1).astype(F32)
    inside = (at <= entry) & (entry < at + count)
    ents[...] = jnp.zeros_like(ents)
    for name, values in (
        (ROW, relative),
        (BLOCK, block - at + entry),
        (TILE, tile),
        (COLUMN, col),
        (FIRST, (entry == at).astype(F32)),
    ):
        ents[name : name + 1] = over_sub(inside, values).astype(jnp.int32)
    ents[START : START + 1, :LANE] = over_sub(relative < lane * quarter_tiles, count).astype(
        jnp.int32
    )


def sweep(lo, hi, body):
    hi = jnp.maximum(lo, hi)
    long = (hi - lo) // LARGE

    def group(n, _):
        for u in range(LARGE):
            body(lo + n * LARGE + u, None)
        return 0

    lax.fori_loop(0, long, group, 0)
    rest = lo + long * LARGE

    def short(n, _):
        for u in range(SMALL):
            e = rest + n * SMALL + u
            body(e, e < hi)
        return 0

    lax.fori_loop(0, (hi - rest + SMALL - 1) // SMALL, short, 0)


def sweep_held(lo, hi, compact, spill, stage, sem, body):
    kept = compact.shape[0] - SMALL
    sweep(lo, jnp.minimum(hi, kept), lambda e, live: body(e, live, compact.at[e]))

    def fetched(e, _):
        copy = pltpu.make_async_copy(spill.at[e - kept], stage, sem)
        copy.start()
        copy.wait()
        body(e, None, stage)
        return 0

    lax.fori_loop(jnp.maximum(lo, kept), hi, fetched, 0)


def pick(live, value, other):
    return value if live is None else jnp.where(live, value, other)


def build(ents, sorted_bus, load, tiles, compact, spill, base, load_sum, stage, sem, found):
    kept = compact.shape[0] - SMALL
    hours = load.shape[0]
    spare = base.shape[1] // LANE - 1
    base[...] = jnp.zeros_like(base)
    lane = lax.broadcasted_iota(jnp.int32, (LANE, LANE), 1)

    def restricted(e, live):
        col = pick(live, ents[COLUMN, e], 0)
        row = jnp.where(pick(live, ents[FIRST, e], 0) == 1, ents[ROW, e], spare)
        bus = sorted_bus[pick(live, ents[BLOCK, e], 0)]
        hot = jnp.where(bus == (lane + col * LANE).astype(F32), 1.0, 0.0).astype(BF16)
        left = jnp.concatenate([load[:, lanes(col)], hot], axis=0)
        both = mxu(left, tiles[pick(live, ents[TILE, e], 0)], NT)
        base[:, lanes(row)] -= both[:hours]
        return both[hours:].astype(BF16)

    def keep(e, live):
        compact[e] = restricted(e, live)

    def put_out(e, _):
        stage[...] = restricted(e, None)
        copy = pltpu.make_async_copy(stage, spill.at[e - kept], sem)
        copy.start()
        copy.wait()
        return 0

    sweep(jnp.int32(0), jnp.minimum(found, kept), keep)
    lax.fori_loop(jnp.int32(kept), found, put_out, 0)
    total = load[:, :LANE].astype(F32)
    for c in range(1, load.shape[1] // LANE):
        total += load[:, c * LANE : (c + 1) * LANE].astype(F32)
    load_sum[...] = jnp.sum(total, axis=1, keepdims=True)


def add_flows(ents, compact, spill, stage, sem, picked, base, total, cap, chunks, quarter_tiles, first, last, outs):
    origin, width = first * quarter_tiles, (last - first) * quarter_tiles
    total[:, : width * LANE] = base[:, origin * LANE : (origin + width) * LANE]
    spare, blocks = width, picked.shape[0] - 1

    def entry(e, live, matrix):
        row = pick(live, ents[ROW, e] - origin, spare)
        m = pick(live, ents[BLOCK, e], blocks)
        total[:, lanes(row)] += mxu(picked[m], matrix[...], NN)

    lo, hi = ents[START, first], ents[START, last]
    sweep_held(lo, hi, compact, spill, stage, sem, entry)
    for d in range(last - first):
        at = d * quarter_tiles
        outs[d][...] = total[:, at * LANE : (at + quarter_tiles) * LANE].astype(BF16)


def add_prices(
    ents, compact, spill, stage, sem, bars, lines, total, cap, quarter_tiles, first, last
):
    half = (quarter_tiles + 1) // 2
    origin = first * quarter_tiles
    for d in range(last - first):
        at = d * quarter_tiles
        lines[:, at * LANE : (at + half) * LANE] = bars[2 * d][:, : half * LANE]
        lines[:, (at + half) * LANE : (at + quarter_tiles) * LANE] = bars[2 * d + 1][...]
    spare, blocks = (last - first) * quarter_tiles, total.shape[0] - 2

    def entry(e, live, matrix):
        row = pick(live, ents[ROW, e] - origin, spare)
        m = pick(live, ents[BLOCK, e], blocks)
        total[m] += mxu(lines[:, lanes(row)], matrix[...], NT)

    lo, hi = ents[START, first], ents[START, last]
    sweep_held(lo, hi, compact, spill, stage, sem, entry)
    for d in range(last - first):
        total[blocks + 1] += bars[2 * d][:, half * LANE :].astype(F32)


def choose(g, p, place, picked):
    x = jnp.concatenate([g.astype(BF16), (-p).astype(BF16)], axis=1)
    chosen = mxu(x, place[...], NN).astype(BF16)
    for m in range(picked.shape[0] - 1):
        picked[m] = chosen[:, m * LANE : (m + 1) * LANE]


def send_hours(g, p, sent):
    hours, stores = p.shape
    gens = g.shape[1]
    sent[:hours] = p
    sent[hours:] = jnp.zeros_like(sent[hours:])
    each = -(-gens // stores)
    for i, row in enumerate((g[:1], g[hours - 1 :])):
        for j in range(each):
            piece = row[:, j * stores : min((j + 1) * stores, gens)]
            sent[hours + i * each + j : hours + i * each + j + 1, : piece.shape[1]] = piece


def own_balance(g, p, load_sum, balance):
    value = jnp.sum(g, axis=1, keepdims=True) - jnp.sum(p, axis=1, keepdims=True) - load_sum[...]
    lane = lax.broadcasted_iota(jnp.int32, balance.shape, 1)
    high = value.astype(BF16).astype(F32)
    middle = (value - high).astype(BF16).astype(F32)
    low = value - high - middle
    balance[...] = jnp.where(
        lane == 0, high, jnp.where(lane == 1, middle, jnp.where(lane == 2, low, 0.0))
    ).astype(BF16)


def first_kernel(
    cap, chunks, quarter_tiles,
    ents, sorted_bus, load, tiles, place, generation, charging,
    compact, spill, base, load_sum, *rest,
):
    upper = chunks - chunks // 2
    outs = rest[:upper]
    balance, sent, picked, stage, sem, total = rest[upper:]
    g, p = generation[...], charging[...]
    send_hours(g, p, sent)
    choose(g, p, place, picked)
    found = ents[START, chunks]
    build(ents, sorted_bus, load, tiles, compact, spill, base, load_sum, stage, sem, found)
    own_balance(g, p, load_sum, balance)
    add_flows(
        ents, compact, spill, stage, sem, picked, base, total,
        cap, chunks, quarter_tiles, chunks // 2, chunks, outs,
    )


def lower_kernel(
    cap, chunks, quarter_tiles, first, last,
    ents, compact, spill, base, picked,
    *rest,
):
    outs = rest[: last - first]
    stage, sem, total = rest[last - first :]
    add_flows(
        ents, compact, spill, stage, sem, picked, base, total,
        cap, chunks, quarter_tiles, first, last, outs,
    )


def price_kernel(cap, quarter_tiles, first, last, fresh, ents, compact, spill, *rest):
    count = 2 * (last - first)
    bars, rest = rest[:count], rest[count:]
    if fresh:
        total, stage, sem, lines = rest
        total[...] = jnp.zeros_like(total)
    else:
        before, total, stage, sem, lines = rest
        total[...] = before[...]
    add_prices(
        ents, compact, spill, stage, sem, bars, lines, total, cap, quarter_tiles, first, last
    )


def step_kernel(
    cap, chunks, quarter_tiles, balance_step, final,
    ents, compact, spill, place, before, generation, charging, fixed_g, fixed_p, balance_dual,
    limits, base, load_sum, *rest,
):
    start = chunks - chunks // 4
    count = 2 * (chunks - start)
    bars, rest = rest[:count], rest[count:]
    if final:
        next_g, next_p, stage, sem, lines, prices = rest
    else:
        next_g, next_p, next_balance, *rest = rest
        outs, rest = rest[: chunks - chunks // 2], rest[chunks - chunks // 2 :]
        balance, sent, picked, stage, sem, lines, prices, total = rest
    prices[...] = before[...]
    add_prices(
        ents, compact, spill, stage, sem, bars, lines, prices, cap, quarter_tiles, start, chunks
    )
    hours, gens = generation.shape
    blocks = prices.shape[0] - 2
    price = jnp.concatenate([prices[m] for m in range(blocks)], axis=1)
    high = price.astype(BF16)
    low = (price - high.astype(F32)).astype(BF16)
    price = mxu(jnp.concatenate([high, low], axis=0), place[...], NT)
    price = price[:hours] + price[hours:]
    old = balance_dual[...]
    new = old + balance_step * jnp.sum(prices[blocks + 1], axis=1, keepdims=True)
    bb = 2.0 * new - old
    g = generation[...] - TAU * (bb + price[:, :gens] + fixed_g[...])
    bound = limits[1:2]
    g = jnp.minimum(jnp.maximum(g, 0.0), bound[:, :gens])
    p = charging[...] - TAU * (fixed_p[...] - bb - price[:, gens:])
    p = jnp.minimum(jnp.maximum(p, -bound[:, gens:]), bound[:, gens:])
    next_g[...] = g
    next_p[...] = p
    if not final:
        next_balance[...] = new
        send_hours(g, p, sent)
        own_balance(g, p, load_sum, balance)
        choose(g, p, place, picked)
        add_flows(
            ents, compact, spill, stage, sem, picked, base, total,
            cap, chunks, quarter_tiles, chunks // 2, chunks, outs,
        )


def hourly_kernel(
    years, hours, order,
    where, generation, limits, ramp_dual, state_dual,
    *rest,
):
    heard, rest = rest[:years], rest[years:]
    fixed_g, fixed_p, ramp_out, state_out, everyone, wide, local, bars = rest
    gens = generation.shape[1]
    units = limits.shape[1] - gens
    cost, ramp_limit = limits[0:1, :gens], limits[2:3, :gens]
    cap, keep = limits[2:3, gens:], limits[3:4, gens:]
    each = -(-gens // units)
    me = where[0]
    before = lax.rem(me + years - 1, years)
    after = lax.rem(me + 1, years)
    for j in range(years):
        everyone[me ^ order[j]] = heard[j][...]
    wide[8 : 8 + hours] = generation[...]
    for j in range(each):
        span = min(units, gens - j * units)
        to = slice(j * units, j * units + span)
        at = hours + each + j
        wide[7:8, to] = everyone[before, at : at + 1, :span]
        at = hours + j
        wide[8 + hours : 9 + hours, to] = everyone[after, at : at + 1, :span]
    ramps = wide[8 : 16 + hours] - wide[7 : 15 + hours]
    old = ramp_dual[...]
    shift = old + SIGMA * ramps
    limit = SIGMA * ramp_limit
    new = shift - jnp.minimum(jnp.maximum(shift, -limit), limit)
    ramp_out[...] = new
    wide[0 : 8 + hours] = 2.0 * new - old
    fixed_g[...] = cost + wide[0:hours] - wide[1 : 1 + hours]

    step = lax.broadcasted_iota(jnp.int32, (8, units), 0)
    rise = jnp.exp((step + 1).astype(F32) * keep)
    fall = jnp.exp((8 - step).astype(F32) * keep)
    one, two, four, eight = (jnp.exp(k * keep) for k in (1.0, 2.0, 4.0, 8.0))
    closing = 1.0 / (1.0 - jnp.exp(float(years * hours) * keep))
    count = years * hours // 8
    per = hours // 8

    def within(n, _):
        y = everyone[n // per, pl.ds(pl.multiple_of((n % per) * 8, 8), 8), :]
        for by, factor in ((1, one), (2, two), (4, four)):
            y = y + jnp.where(step >= by, factor * pltpu.roll(y, by, 0), 0.0)
        local[n] = y
        return 0

    lax.fori_loop(0, count, within, 0, unroll=8)
    zero = jnp.zeros((1, units), F32)
    finish = lax.fori_loop(0, count, lambda n, c: local[n][7:8] + eight * c, zero, unroll=8)

    def forward(n, c):
        y = local[n]
        state = y + rise * c
        old = state_dual[n]
        shift = old + SIGMA * state
        new = shift - jnp.minimum(jnp.maximum(shift, 0.0), SIGMA * cap)
        state_out[n] = new
        bar = 2.0 * new - old
        for by, factor in ((1, one), (2, two), (4, four)):
            bar = bar + jnp.where(step < 8 - by, factor * pltpu.roll(bar, 8 - by, 0), 0.0)
        bars[n] = bar
        return y[7:8] + eight * c

    lax.fori_loop(0, count, forward, finish * closing, unroll=8)

    def back(i, c):
        return bars[count - 1 - i][0:1] + eight * c

    finish = lax.fori_loop(0, count, back, zero, unroll=8)
    c = lax.fori_loop(0, count - (me + 1) * per, back, finish * closing)
    for j in reversed(range(per)):
        y = bars[me * per + j]
        fixed_p[8 * j : 8 * j + 8] = y + fall * c
        c = y[0:1] + eight * c


def shards(
    gen_start, charge_start, load, ptdf_tiles, tile_row, tile_col, gen_bus, stor_bus,
    gen_cost, gen_max, ramp_limit, stor_power, stor_loss, stor_cap, flow_limit,
):
    hours, gens = gen_start.shape
    stores = charge_start.shape[1]
    units = gens + stores
    kt = ptdf_tiles.shape[0]
    bus_tiles = load.shape[1] // LANE
    chunks = lax.axis_size("bus")
    years = lax.axis_size("tm")
    lines = flow_limit.shape[0] // chunks
    quarter_tiles = lines // LANE
    half = (quarter_tiles + 1) // 2 * LANE
    widths = (half, lines - half)
    blocks = units // LANE
    line_tiles = chunks * quarter_tiles
    mine = lax.axis_index("bus")
    balance_step = SIGMA / (gens * chunks)
    cap = blocks * kt + LARGE
    kept = min(cap, KEPT) // SMALL * SMALL
    sent_rows = -(-(hours + 2 * -(-gens // stores)) // 8) * 8
    groups = years * hours // 8

    def like(*shape, dtype=F32):
        return jax.ShapeDtypeStruct(shape, dtype)

    width = -(-(cap + SMALL) // LANE) * LANE
    place, sorted_bus, ents = pl.pallas_call(
        functools.partial(plan_kernel, chunks, quarter_tiles),
        out_shape=(
            like(units, units, dtype=BF16),
            like(blocks, LANE, LANE),
            like(8, width, dtype=jnp.int32),
        ),
        in_specs=[smem()] + [vmem()] * 4,
        out_specs=(vmem(),) * 3,
        scratch_shapes=[pltpu.VMEM((8, LANE), jnp.int32)],
        compiler_params=params(STEP_MIB),
        name="plan",
        cost_estimate=cost(3),
    )(
        mine.astype(jnp.int32).reshape(1),
        *[x[None, :] for x in (gen_bus, stor_bus, tile_row, tile_col)],
    )

    chunk_out = (like(hours, lines, dtype=BF16),) * (chunks // 2)
    staging = [pltpu.VMEM((LANE, LANE), BF16), pltpu.SemaphoreType.DMA]
    picked_shape = like(blocks + 1, hours, LANE, dtype=BF16)

    def flow_scratch(count):
        return [pltpu.VMEM((hours, (count * quarter_tiles + 1) * LANE), F32)]

    def line_scratch(count):
        return pltpu.VMEM((hours, (count * quarter_tiles + 1) * LANE), BF16)

    price_shape = (blocks + 2, hours, LANE)
    first_call = pl.pallas_call(
        functools.partial(first_kernel, cap, chunks, quarter_tiles),
        out_shape=(
            like(kept + SMALL, LANE, LANE, dtype=BF16),
            like(max(cap - kept, SPILL), LANE, LANE, dtype=BF16),
            like(hours, (line_tiles + 1) * LANE),
            like(hours, 1),
        )
        + chunk_out
        + (like(hours, LANE, dtype=BF16), like(sent_rows, stores), picked_shape),
        in_specs=[smem()] + [vmem()] * 6,
        out_specs=(vmem(), hbm()) + (vmem(),) * (chunks // 2 + 5),
        scratch_shapes=staging + flow_scratch(chunks // 2),
        compiler_params=params(STEP_MIB),
        name="first",
        cost_estimate=cost(9),
    )

    def lower_call(first, last):
        return pl.pallas_call(
            functools.partial(lower_kernel, cap, chunks, quarter_tiles, first, last),
            out_shape=(like(hours, lines, dtype=BF16),) * (last - first),
            in_specs=[smem(), vmem(), hbm()] + [vmem()] * 2,
            out_specs=(vmem(),) * (last - first),
            scratch_shapes=staging + flow_scratch(last - first),
            compiler_params=params(STEP_MIB),
            name="lower",
            cost_estimate=cost(2),
        )

    def price_call(first, last, fresh):
        return pl.pallas_call(
            functools.partial(price_kernel, cap, quarter_tiles, first, last, fresh),
            out_shape=like(*price_shape),
            in_specs=[smem(), vmem(), hbm()] + [vmem()] * (2 * (last - first) + (not fresh)),
            out_specs=vmem(),
            scratch_shapes=staging + [line_scratch(last - first)],
            compiler_params=params(STEP_MIB),
            name="price",
            cost_estimate=cost(2),
        )

    tail = chunks - chunks // 4

    def step_call(final):
        shape = (like(hours, gens), like(hours, stores))
        scratch = staging + [line_scratch(chunks - tail), pltpu.VMEM(price_shape, F32)]
        if not final:
            shape += (like(hours, 1),) + chunk_out
            shape += (like(hours, LANE, dtype=BF16), like(sent_rows, stores), picked_shape)
            scratch += flow_scratch(chunks // 2)
        return pl.pallas_call(
            functools.partial(step_kernel, cap, chunks, quarter_tiles, balance_step, final),
            out_shape=shape,
            in_specs=[smem(), vmem(), hbm()] + [vmem()] * (10 + 2 * (chunks - tail)),
            out_specs=(vmem(),) * len(shape),
            scratch_shapes=scratch,
            compiler_params=params(STEP_MIB),
            name="step",
            cost_estimate=cost(4),
        )

    spans = [1 << b for b in reversed(range(years.bit_length() - 1))]
    order = [0]
    for bit in spans:
        order += [j ^ bit for j in order]

    hourly_call = pl.pallas_call(
        functools.partial(hourly_kernel, years, hours, order),
        out_shape=(
            like(hours, gens),
            like(hours, stores),
            like(hours + 8, gens),
            like(groups, 8, stores),
        ),
        in_specs=[smem()] + [vmem()] * (4 + years),
        out_specs=(vmem(),) * 4,
        scratch_shapes=[
            pltpu.VMEM((years, sent_rows, stores), F32),
            pltpu.VMEM((hours + 16, gens), F32),
            pltpu.VMEM((groups, 8, stores), F32),
            pltpu.VMEM((groups, 8, stores), F32),
        ],
        compiler_params=params(STEP_MIB),
        name="hourly",
            cost_estimate=cost(2.4),
    )

    where = lax.axis_index("tm").astype(jnp.int32).reshape(1)
    limits = lax.dynamic_slice_in_dim(flow_limit, mine * lines, lines)[None, :] * SIGMA
    limits = (limits[:, :half], limits[:, half:])
    unit_rows = jnp.stack(
        [
            jnp.concatenate([gen_cost, stor_power]),
            jnp.concatenate([gen_max, stor_power]),
            jnp.concatenate([ramp_limit, stor_cap]),
            jnp.concatenate([ramp_limit, jnp.log1p(-stor_loss)]),
        ]
    )

    def swap(x, bit, axis="bus"):
        size = lax.axis_size(axis)
        return lax.ppermute(x, axis, [(i, i ^ bit) for i in range(size)])

    def hear(stacked, over):
        for bit in over:
            stacked = jnp.concatenate([stacked, swap(stacked, bit, "tm")])
        return stacked

    def cut(xs, h):
        return [x[:, :half] if h == 0 else x[:, half:] for x in xs]

    bits = [1 << b for b in range(chunks.bit_length() - 1)]
    line_dual = [jnp.zeros((hours, w), F32) for w in widths]
    ramp_dual = jnp.zeros((hours + 8, gens), F32)
    state_dual = jnp.zeros((groups, 8, stores), F32)
    balance_dual = jnp.zeros((hours, 1), F32)
    g, p = gen_start, charge_start
    compact, spill, base, load_sum, *upper, balance, sent, picked = first_call(
        ents, sorted_bus, load, ptdf_tiles, place, g, p
    )
    half_way = chunks // 2

    def reduce(parts):
        for bit in bits[:-1]:
            for d in sorted(parts, reverse=True):
                if d & bit and not d & (bit - 1):
                    got = swap(sum(x.astype(F32) for x in parts[d]).astype(BF16), bit)
                    parts[d ^ bit].append(got)

    for iteration in range(ITERS):
        parts = {d: [x] for d, x in zip(range(half_way, chunks), upper)}
        reduce(parts)
        ready = [sum(x.astype(F32) for x in cut(parts[half_way], h)).astype(BF16) for h in (0, 1)]
        across = [swap(x, half_way) for x in ready]
        parts = {d: [] for d in range(half_way)}
        if half_way > 1:
            made = lower_call(1, half_way)(ents, compact, spill, base, picked)
            for d, x in zip(range(1, half_way), made):
                parts[d].append(x)
        sent, picked, *_ = lax.optimization_barrier((sent, picked, *ready))
        parts[0].append(lower_call(0, 1)(ents, compact, spill, base, picked)[0])
        reduce(parts)
        sent, parts[0][0] = lax.optimization_barrier((sent, parts[0][0]))
        heard = hear(sent[None], spans[:1])
        have = {0: []}
        for h in range(2):
            flows = sum(x.astype(F32) for x in cut(parts[0], h) + [across[h]])
            shift = line_dual[h] + SIGMA * flows
            after = shift - jnp.clip(shift, -limits[h], limits[h])
            bar = (2.0 * after - line_dual[h]).astype(BF16)
            line_dual[h] = after
            have[0].append(jnp.concatenate([bar, balance], axis=1) if h == 0 else bar)
            if h == 0:
                line_dual[1], have[0][0] = lax.optimization_barrier((line_dual[1], have[0][0]))
        have[half_way] = [swap(x, half_way) for x in have[0]]
        near = [0]
        for bit in reversed(bits[:-1]):
            for d in list(near):
                have[d | bit] = [swap(x, bit) for x in have[d]]
                near.append(d | bit)
        heard, *_ = lax.optimization_barrier((heard, have[near[-1]][1]))
        heard = hear(heard, spans[1:])
        prices = price_call(0, half_way, True)(
            ents, compact, spill, *[x for d in range(half_way) for x in have[d]]
        )
        heard, prices = lax.optimization_barrier((heard, prices))
        fixed_g, fixed_p, ramp_dual, state_dual = hourly_call(
            where, g, unit_rows, ramp_dual, state_dual, *[heard[j] for j in range(years)]
        )
        have[half_way][0], prices, fixed_g, fixed_p = lax.optimization_barrier(
            (have[half_way][0], prices, fixed_g, fixed_p)
        )
        far = [half_way]
        for bit in reversed(bits[:-1]):
            for d in list(far):
                have[d | bit] = [swap(x, bit) for x in have[d]]
                far.append(d | bit)
        if tail > half_way:
            prices = price_call(half_way, tail, False)(
                ents, compact, spill, *[x for d in range(half_way, tail) for x in have[d]], prices
            )
        final = iteration == ITERS - 1
        g, p, *rest = step_call(final)(
            ents, compact, spill, place, prices, g, p, fixed_g, fixed_p, balance_dual,
            unit_rows, base, load_sum, *[x for d in range(tail, chunks) for x in have[d]],
        )
        if not final:
            balance_dual, *upper, balance, sent, picked = rest
    return g, p, jnp.concatenate(line_dual, axis=1)


STEP_MIB = 16
SPILL = 1500


def solution(mesh):
    rows = P(("scen", "tm"), "bus")
    return jax.shard_map(
        shards,
        mesh=mesh,
        in_specs=(rows, rows, rows, P("bus", None, None)) + (P("bus"),) * 10 + (P(),),
        out_specs=(rows, rows, rows),
        check_vma=False,
    )
```

profile of v0, /device:TPU:0, one launch (start us, length us, event | category | flops | bytes accessed | tf_op | source)
XLA Modules:
  0.0 122.5 jit_solution(13105003764740771890)
XLA Ops:
  5.1 2.1 %copy-done.6 = bf16[116,128,128]{2,1,0:T(8,128)(2,1)S(1)} copy-done((bf16[116,128,128]{2,1,0:T(8,128)(2,1)S(1)}, bf16[116,128,128]{2,1,0:T(8,128)(2,1)}, u32[]{:S(2)}) %copy-start.6) | copy-done | bytes 3801112
  10.0 7.3 %first.1 = (bf16[168,128,128]{2,1,0:T(8,128)(2,1)S(1)}, bf16[1500,128,128]{2,1,0:T(8,128)(2,1)}, f32[64,10368]{1,0:T(8,128)S(1)}, f32[64,1]{1,0:T(8,128)S(1)}, b...) custom-call(s32[8,896]{1,0:T(8,128)S(1)} %get-tuple-element.82.ents,, ...), custom_call_target="tpu_custom_call" | custom-call | bytes 27000000 | tf_op jit(solution)/shard_map/first/pallas_call | solution.py:619
  22.5 2.7 %collective-permute-start.2 = (bf16[64,1280]{1,0:T(8,128)(2,1)S(1)}, bf16[64,1280]{1,0:T(8,128)(2,1)S(1)}, u32[]{:S(2)}, u32[]{:S(2)}) collective-permute-start(bf16[64,1280]{1,0:T(8,128)(2,1)S(1)} %get-tuple-element.180), channel_id=1, source_target_pairs={{0,2},{1,3},{2,0},{3,1},{4,6},{5,7},{6,4},{7,5},{8,10},{9,11},{10,... | collective-permute-start | bytes 491528 | tf_op jit(solution)/shard_map/ppermute | solution.py:603
  26.2 2.6 %copy-done.1 = bf16[168,128,128]{2,1,0:T(8,128)(2,1)S(1)} copy-done((bf16[168,128,128]{2,1,0:T(8,128)(2,1)S(1)}, bf16[168,128,128]{2,1,0:T(8,128)(2,1)}, u32[]{:S(2)}) %copy-start.1) | copy-done | bytes 5505048
  28.8 2.0 %lower.6 = bf16[64,2560]{1,0:T(8,128)(2,1)S(1)} custom-call(s32[8,896]{1,0:T(8,128)S(1)} %get-tuple-element.82.ents, bf16[168,128,128]{2,1,0:T(8,128)(2,1)S(1)} %copy-done.1, bf16[1500,128,128]{2,1,0:T(8,128)(2,1)} %get-tuple-element.86.spill, f32[64,10368]{1,0:T(8,128)S(1)} %get-tuple-element.92.base, bf16[8,64,128]{2,1,0:T(8,128)(2,1)S(1)} %get-tuple-element.93.picked), custom_call_target="tpu_custom_call" | custom-call | bytes 6000000 | tf_op jit(solution)/shard_map/lower/pallas_call | solution.py:642
  30.8 3.0 %collective-permute-start.5 = (f32[1,72,256]{2,1,0:T(8,128)S(1)}, f32[1,72,256]{2,1,0:T(8,128)S(1)}, u32[]{:S(2)}, u32[]{:S(2)}) collective-permute-start(f32[1,72,256]{2,1,0:T(8,128)S(1)} %bitcast.32), channel_id=1, source_target_pairs={{0,8},{4,12},{8,0},{12,4},{1,9},{5,13},{9,1},{13,5},{2,10},{6,14},... | collective-permute-start | bytes 221192 | tf_op jit(solution)/shard_map/ppermute | solution.py:603
  42.6 2.6 %copy-done.2 = bf16[168,128,128]{2,1,0:T(8,128)(2,1)S(1)} copy-done((bf16[168,128,128]{2,1,0:T(8,128)(2,1)S(1)}, bf16[168,128,128]{2,1,0:T(8,128)(2,1)}, u32[]{:S(2)}) %copy-start.2) | copy-done | bytes 5505048
  46.1 2.8 %price.6.rest_2_ = f32[9,64,128]{2,1,0:T(8,128)S(1)} custom-call(s32[8,896]{1,0:T(8,128)S(1)} %get-tuple-element.82.ents, bf16[168,128,128]{2,1,0:T(8,128)(2,1)S(1)} %copy-done.2, bf16[1500,128,128]{2,1,0:T(8,128)(2,1)} %get-tuple-element.86.spill, bf16[64,1408]{1,0:T(8,128)(2,1)S(1)} %pad_maximum_fusion.4.rest_0_, ...), custom_call_target="tpu_custom_call" | custom-call | bytes 6000000 | tf_op jit(solution)/shard_map/price/pallas_call | solution.py:664
  52.1 2.2 %price.7.before = f32[9,64,128]{2,1,0:T(8,128)S(1)} custom-call(s32[8,896]{1,0:T(8,128)S(1)} %get-tuple-element.82.ents, bf16[168,128,128]{2,1,0:T(8,128)(2,1)S(1)} %copy-done.3, bf16[1500,128,128]{2,1,0:T(8,128)(2,1)} %get-tuple-element.86.spill, bf16[64,1408]{1,0:T(8,128)(2,1)S(1)} %collective-permute-done.4.rest_0_, ...), custom_call_target="tpu_custom_call" | custom-call | bytes 6000000 | tf_op jit(solution)/shard_map/price/pallas_call | solution.py:680
  54.3 4.4 %step.3 = (f32[64,640]{1,0:T(8,128)S(1)}, f32[64,256]{1,0:T(8,128)S(1)}, f32[64,1]{1,0:T(8,128)S(1)}, bf16[64,2560]{1,0:T(8,128)(2,1)S(1)}, bf16[64,2560]{1,0:T(...) custom-call(s32[8,896]{1,0:T(8,128)S(1)} %get-tuple-element.82.ents, ...), custom_call_target="tpu_custom_call" | custom-call | bytes 12000000 | tf_op jit(solution)/shard_map/step/pallas_call | solution.py:684
  65.2 2.7 %collective-permute-start.17 = (f32[1,72,256]{2,1,0:T(8,128)S(1)}, f32[1,72,256]{2,1,0:T(8,128)S(1)}, u32[]{:S(2)}, u32[]{:S(2)}) collective-permute-start(f32[1,72,256]{2,1,0:T(8,128)S(1)} %bitcast.36), channel_id=1, source_target_pairs={{0,8},{4,12},{8,0},{12,4},{1,9},{5,13},{9,1},{13,5},{2,10},{6,14},... | collective-permute-start | bytes 221192 | tf_op jit(solution)/shard_map/ppermute | solution.py:603
  75.6 2.7 %price.8.rest_2_ = f32[9,64,128]{2,1,0:T(8,128)S(1)} custom-call(s32[8,896]{1,0:T(8,128)S(1)} %get-tuple-element.82.ents, bf16[168,128,128]{2,1,0:T(8,128)(2,1)S(1)} %copy-done.3, bf16[1500,128,128]{2,1,0:T(8,128)(2,1)} %get-tuple-element.86.spill, bf16[64,1408]{1,0:T(8,128)(2,1)S(1)} %pad_maximum_fusion.5.rest_0_, ...), custom_call_target="tpu_custom_call" | custom-call | bytes 6000000 | tf_op jit(solution)/shard_map/price/pallas_call | solution.py:664
  80.1 3.3 %collective-permute-done.16.rest_0_ = bf16[64,1408]{1,0:T(8,128)(2,1)S(1)} collective-permute-done((bf16[64,1408]{1,0:T(8,128)(2,1)S(1)}, bf16[64,1408]{1,0:T(8,128)(2,1)S(1)}, u32[]{:S(2)}, u32[]{:S(2)}) %collective-permute-start.16) | collective-permute-done | bytes 180256 | tf_op jit(solution)/shard_map/ppermute | solution.py:603
  83.9 2.2 %price.9.before = f32[9,64,128]{2,1,0:T(8,128)S(1)} custom-call(s32[8,896]{1,0:T(8,128)S(1)} %get-tuple-element.82.ents, bf16[168,128,128]{2,1,0:T(8,128)(2,1)S(1)} %copy-done.3, bf16[1500,128,128]{2,1,0:T(8,128)(2,1)} %get-tuple-element.86.spill, bf16[64,1408]{1,0:T(8,128)(2,1)S(1)} %collective-permute-done.16.rest_0_, ...), custom_call_target="tpu_custom_call" | custom-call | bytes 6000000 | tf_op jit(solution)/shard_map/price/pallas_call | solution.py:680
  86.1 4.4 %step.4 = (f32[64,640]{1,0:T(8,128)S(1)}, f32[64,256]{1,0:T(8,128)S(1)}, f32[64,1]{1,0:T(8,128)S(1)}, bf16[64,2560]{1,0:T(8,128)(2,1)S(1)}, bf16[64,2560]{1,0:T(...) custom-call(s32[8,896]{1,0:T(8,128)S(1)} %get-tuple-element.82.ents, ...), custom_call_target="tpu_custom_call" | custom-call | bytes 12000000 | tf_op jit(solution)/shard_map/step/pallas_call | solution.py:684
  92.8 2.2 %collective-permute-start.26 = (bf16[64,1280]{1,0:T(8,128)(2,1)S(1)}, bf16[64,1280]{1,0:T(8,128)(2,1)S(1)}, u32[]{:S(2)}, u32[]{:S(2)}) collective-permute-start(bf16[64,1280]{1,0:T(8,128)(2,1)S(1)} %get-tuple-element.176), channel_id=1, source_target_pairs={{0,2},{1,3},{2,0},{3,1},{4,6},{5,7},{6,4},{7,5},{8,10},{9,11},{10,... | collective-permute-start | bytes 491528 | tf_op jit(solution)/shard_map/ppermute | solution.py:603
  95.1 1.9 %lower.10 = bf16[64,2560]{1,0:T(8,128)(2,1)S(1)} custom-call(s32[8,896]{1,0:T(8,128)S(1)} %get-tuple-element.82.ents, bf16[168,128,128]{2,1,0:T(8,128)(2,1)S(1)} %copy-done.3, bf16[1500,128,128]{2,1,0:T(8,128)(2,1)} %get-tuple-element.86.spill, f32[64,10368]{1,0:T(8,128)S(1)} %get-tuple-element.92.base, bf16[8,64,128]{2,1,0:T(8,128)(2,1)S(1)} %get-tuple-element.139.picked), custom_call_target="tpu_custom_call" | custom-call | bytes 6000000 | tf_op jit(solution)/shard_map/lower/pallas_call | solution.py:642
  97.0 2.1 %collective-permute-start.28 = (f32[1,72,256]{2,1,0:T(8,128)S(1)}, f32[1,72,256]{2,1,0:T(8,128)S(1)}, u32[]{:S(2)}, u32[]{:S(2)}) collective-permute-start(f32[1,72,256]{2,1,0:T(8,128)S(1)} %bitcast.34), channel_id=1, source_target_pairs={{0,8},{4,12},{8,0},{12,4},{1,9},{5,13},{9,1},{13,5},{2,10},{6,14},... | collective-permute-start | bytes 221192 | tf_op jit(solution)/shard_map/ppermute | solution.py:603
  100.2 2.7 %collective-permute-done.29 = bf16[64,1280]{1,0:T(8,128)(2,1)S(1)} collective-permute-done((bf16[64,1280]{1,0:T(8,128)(2,1)S(1)}, bf16[64,1280]{1,0:T(8,128)(2,1)S(1)}, u32[]{:S(2)}, u32[]{:S(2)}) %collective-permute-start.29) | collective-permute-done | bytes 163872 | tf_op jit(solution)/shard_map/ppermute | solution.py:603
  107.3 2.9 %collective-permute-done.33.rest_1_ = bf16[64,1280]{1,0:T(8,128)(2,1)S(1)} collective-permute-done((bf16[64,1280]{1,0:T(8,128)(2,1)S(1)}, bf16[64,1280]{1,0:T(8,128)(2,1)S(1)}, u32[]{:S(2)}, u32[]{:S(2)}) %collective-permute-start.33) | collective-permute-done | bytes 163872 | tf_op jit(solution)/shard_map/ppermute | solution.py:603
  110.2 2.7 %price.10.rest_2_ = f32[9,64,128]{2,1,0:T(8,128)S(1)} custom-call(s32[8,896]{1,0:T(8,128)S(1)} %get-tuple-element.82.ents, bf16[168,128,128]{2,1,0:T(8,128)(2,1)S(1)} %copy-done.3, bf16[1500,128,128]{2,1,0:T(8,128)(2,1)} %get-tuple-element.86.spill, bf16[64,1408]{1,0:T(8,128)(2,1)S(1)} %pad_maximum_fusion.6.rest_0_, ...), custom_call_target="tpu_custom_call" | custom-call | bytes 6000000 | tf_op jit(solution)/shard_map/price/pallas_call | solution.py:664
  113.0 2.2 %hourly.5 = (f32[64,640]{1,0:T(8,128)S(1)}, f32[64,256]{1,0:T(8,128)S(1)}, f32[72,640]{1,0:T(8,128)}, f32[32,8,256]{2,1,0:T(8,128)}) custom-call(s32[1]{0:T(128)} %bitcast.5.where, f32[64,640]{1,0:T(8,128)S(1)} %get-tuple-element.147.generation, f32[4,896]{1,0:T(4,128)S(1)} %pad_maximum_fusion.10.limits, f32[72,640]{1,0:T(8,128)S(1)} %get-tuple-element.148.ramp_dual, ...), custom_call_target="tpu_custom_call" | custom-call | bytes 7200000 | tf_op jit(solution)/shard_map/hourly/pallas_call | solution.py:668
  116.6 2.2 %price.11.before = f32[9,64,128]{2,1,0:T(8,128)S(1)} custom-call(s32[8,896]{1,0:T(8,128)S(1)} %get-tuple-element.82.ents, bf16[168,128,128]{2,1,0:T(8,128)(2,1)S(1)} %copy-done.3, bf16[1500,128,128]{2,1,0:T(8,128)(2,1)} %get-tuple-element.86.spill, bf16[64,1408]{1,0:T(8,128)(2,1)S(1)} %collective-permute-done.27.rest_0_, ...), custom_call_target="tpu_custom_call" | custom-call | bytes 6000000 | tf_op jit(solution)/shard_map/price/pallas_call | solution.py:680
  118.8 3.5 %step.5 = (f32[64,640]{1,0:T(8,128)}, f32[64,256]{1,0:T(8,128)}) custom-call(s32[8,896]{1,0:T(8,128)S(1)} %get-tuple-element.82.ents, bf16[168,128,128]{2,1,0:T(8,128)(2,1)S(1)} %copy-done.3, bf16[1500,128,128]{2,1,0:T(8,128)(2,1)} %get-tuple-element.86.spill, bf16[896,896]{1,0:T(8,128)(2,1)S(1)} %copy-done.5, f32[9,64,128]{2,1,0:T(8,128)S(1)} %price.11.before, ...), custom_call_target="tpu_custom_call" | custom-call | bytes 12000000 | tf_op jit(solution)/shard_map/step/pallas_call | solution.py:684
  (162 shorter events, 51.6 us)
Async XLA Ops:
  21.0 12.8 %collective-permute-start.1 = (bf16[64,2560]{1,0:T(8,128)(2,1)S(1)}, bf16[64,2560]{1,0:T(8,128)(2,1)}, u32[]{:S(2)}, u32[]{:S(2)}) collective-permute-start(bf16[64,2560]{1,0:T(8,128)(2,1)S(1)} %lower.7), channel_id=1, source_target_pairs={{0,1},{1,0},{2,3},{3,2},{4,5},{5,4},{6,7},{7,6},{8,9},{9,8},{10,11... | collective-permute-start | bytes 983048 | tf_op jit(solution)/shard_map/ppermute | solution.py:603
  22.5 11.3 %collective-permute-start.2 = (bf16[64,1280]{1,0:T(8,128)(2,1)S(1)}, bf16[64,1280]{1,0:T(8,128)(2,1)S(1)}, u32[]{:S(2)}, u32[]{:S(2)}) collective-permute-start(bf16[64,1280]{1,0:T(8,128)(2,1)S(1)} %get-tuple-element.180), channel_id=1, source_target_pairs={{0,2},{1,3},{2,0},{3,1},{4,6},{5,7},{6,4},{7,5},{8,10},{9,11},{10,... | collective-permute-start | bytes 491528 | tf_op jit(solution)/shard_map/ppermute | solution.py:603
  26.1 8.8 %collective-permute-start.3 = (bf16[64,1280]{1,0:T(8,128)(2,1)S(1)}, bf16[64,1280]{1,0:T(8,128)(2,1)S(1)}, u32[]{:S(2)}, u32[]{:S(2)}) collective-permute-start(bf16[64,1280]{1,0:T(8,128)(2,1)S(1)} %get-tuple-element.179), channel_id=1, source_target_pairs={{0,2},{1,3},{2,0},{3,1},{4,6},{5,7},{6,4},{7,5},{8,10},{9,11},{10,... | collective-permute-start | bytes 491528 | tf_op jit(solution)/shard_map/ppermute | solution.py:603
  30.8 6.8 %collective-permute-start.5 = (f32[1,72,256]{2,1,0:T(8,128)S(1)}, f32[1,72,256]{2,1,0:T(8,128)S(1)}, u32[]{:S(2)}, u32[]{:S(2)}) collective-permute-start(f32[1,72,256]{2,1,0:T(8,128)S(1)} %bitcast.32), channel_id=1, source_target_pairs={{0,8},{4,12},{8,0},{12,4},{1,9},{5,13},{9,1},{13,5},{2,10},{6,14},... | collective-permute-start | bytes 221192 | tf_op jit(solution)/shard_map/ppermute | solution.py:603
  38.2 4.3 %collective-permute-start.8 = (bf16[64,1408]{1,0:T(8,128)(2,1)S(1)}, bf16[64,1408]{1,0:T(8,128)(2,1)}, u32[]{:S(2)}, u32[]{:S(2)}) collective-permute-start(bf16[64,1408]{1,0:T(8,128)(2,1)S(1)} %pad_maximum_fusion.4.rest_0_), channel_id=1, source_target_pairs={{0,1},{1,0},{2,3},{3,2},{4,5},{5,4},{6,7},{7,6},{8,9},{9,8},{10,11... | collective-permute-start | bytes 540680 | tf_op jit(solution)/shard_map/ppermute | solution.py:603
  38.9 10.0 %collective-permute-start.7 = (f32[2,72,256]{2,1,0:T(8,128)}, f32[2,72,256]{2,1,0:T(8,128)}, u32[]{:S(2)}, u32[]{:S(2)}) collective-permute-start(f32[2,72,256]{2,1,0:T(8,128)} %pad_maximum_fusion.7), channel_id=1, source_target_pairs={{0,4},{4,0},{8,12},{12,8},{1,5},{5,1},{9,13},{13,9},{2,6},{6,2},{1... | collective-permute-start | bytes 442376 | tf_op jit(solution)/shard_map/ppermute | solution.py:603
  40.5 11.1 %collective-permute-start.9 = (bf16[64,1280]{1,0:T(8,128)(2,1)S(1)}, bf16[64,1280]{1,0:T(8,128)(2,1)S(1)}, u32[]{:S(2)}, u32[]{:S(2)}) collective-permute-start(bf16[64,1280]{1,0:T(8,128)(2,1)S(1)} %get-tuple-element.173.rest_1_), channel_id=1, source_target_pairs={{0,2},{1,3},{2,0},{3,1},{4,6},{5,7},{6,4},{7,5},{8,10},{9,11},{10,... | collective-permute-start | bytes 491528 | tf_op jit(solution)/shard_map/ppermute | solution.py:603
  42.0 9.5 %collective-permute-start.4 = (bf16[64,1408]{1,0:T(8,128)(2,1)S(1)}, bf16[64,1408]{1,0:T(8,128)(2,1)S(1)}, u32[]{:S(2)}, u32[]{:S(2)}) collective-permute-start(bf16[64,1408]{1,0:T(8,128)(2,1)S(1)} %pad_maximum_fusion.4.rest_0_), channel_id=1, source_target_pairs={{0,2},{1,3},{2,0},{3,1},{4,6},{5,7},{6,4},{7,5},{8,10},{9,11},{10,... | collective-permute-start | bytes 540680 | tf_op jit(solution)/shard_map/ppermute | solution.py:603
  60.7 7.2 %collective-permute-start.13 = (bf16[64,2560]{1,0:T(8,128)(2,1)S(1)}, bf16[64,2560]{1,0:T(8,128)(2,1)S(1)}, u32[]{:S(2)}, u32[]{:S(2)}) collective-permute-start(bf16[64,2560]{1,0:T(8,128)(2,1)S(1)} %lower.9), channel_id=1, source_target_pairs={{0,1},{1,0},{2,3},{3,2},{4,5},{5,4},{6,7},{7,6},{8,9},{9,8},{10,11... | collective-permute-start | bytes 983048 | tf_op jit(solution)/shard_map/ppermute | solution.py:603
  61.2 7.1 %collective-permute-start.14 = (bf16[64,1280]{1,0:T(8,128)(2,1)S(1)}, bf16[64,1280]{1,0:T(8,128)(2,1)S(1)}, u32[]{:S(2)}, u32[]{:S(2)}) collective-permute-start(bf16[64,1280]{1,0:T(8,128)(2,1)S(1)} %get-tuple-element.178), channel_id=1, source_target_pairs={{0,2},{1,3},{2,0},{3,1},{4,6},{5,7},{6,4},{7,5},{8,10},{9,11},{10,... | collective-permute-start | bytes 491528 | tf_op jit(solution)/shard_map/ppermute | solution.py:603
  63.1 8.0 %collective-permute-start.15 = (bf16[64,1280]{1,0:T(8,128)(2,1)S(1)}, bf16[64,1280]{1,0:T(8,128)(2,1)S(1)}, u32[]{:S(2)}, u32[]{:S(2)}) collective-permute-start(bf16[64,1280]{1,0:T(8,128)(2,1)S(1)} %get-tuple-element.177), channel_id=1, source_target_pairs={{0,2},{1,3},{2,0},{3,1},{4,6},{5,7},{6,4},{7,5},{8,10},{9,11},{10,... | collective-permute-start | bytes 491528 | tf_op jit(solution)/shard_map/ppermute | solution.py:603
  65.2 6.6 %collective-permute-start.17 = (f32[1,72,256]{2,1,0:T(8,128)S(1)}, f32[1,72,256]{2,1,0:T(8,128)S(1)}, u32[]{:S(2)}, u32[]{:S(2)}) collective-permute-start(f32[1,72,256]{2,1,0:T(8,128)S(1)} %bitcast.36), channel_id=1, source_target_pairs={{0,8},{4,12},{8,0},{12,4},{1,9},{5,13},{9,1},{13,5},{2,10},{6,14},... | collective-permute-start | bytes 221192 | tf_op jit(solution)/shard_map/ppermute | solution.py:603
  72.7 5.9 %collective-permute-start.19 = (f32[2,72,256]{2,1,0:T(8,128)S(1)}, f32[2,72,256]{2,1,0:T(8,128)S(1)}, u32[]{:S(2)}, u32[]{:S(2)}) collective-permute-start(f32[2,72,256]{2,1,0:T(8,128)S(1)} %pad_maximum_fusion.8), channel_id=1, source_target_pairs={{0,4},{4,0},{8,12},{12,8},{1,5},{5,1},{9,13},{13,9},{2,6},{6,2},{1... | collective-permute-start | bytes 442376 | tf_op jit(solution)/shard_map/ppermute | solution.py:603
  73.5 9.8 %collective-permute-start.21 = (bf16[64,1280]{1,0:T(8,128)(2,1)S(1)}, bf16[64,1280]{1,0:T(8,128)(2,1)S(1)}, u32[]{:S(2)}, u32[]{:S(2)}) collective-permute-start(bf16[64,1280]{1,0:T(8,128)(2,1)S(1)} %get-tuple-element.169.rest_1_), channel_id=1, source_target_pairs={{0,2},{1,3},{2,0},{3,1},{4,6},{5,7},{6,4},{7,5},{8,10},{9,11},{10,... | collective-permute-start | bytes 491528 | tf_op jit(solution)/shard_map/ppermute | solution.py:603
  75.3 8.1 %collective-permute-start.16 = (bf16[64,1408]{1,0:T(8,128)(2,1)S(1)}, bf16[64,1408]{1,0:T(8,128)(2,1)S(1)}, u32[]{:S(2)}, u32[]{:S(2)}) collective-permute-start(bf16[64,1408]{1,0:T(8,128)(2,1)S(1)} %pad_maximum_fusion.5.rest_0_), channel_id=1, source_target_pairs={{0,2},{1,3},{2,0},{3,1},{4,6},{5,7},{6,4},{7,5},{8,10},{9,11},{10,... | collective-permute-start | bytes 540680 | tf_op jit(solution)/shard_map/ppermute | solution.py:603
  92.3 6.8 %collective-permute-start.25 = (bf16[64,2560]{1,0:T(8,128)(2,1)S(1)}, bf16[64,2560]{1,0:T(8,128)(2,1)S(1)}, u32[]{:S(2)}, u32[]{:S(2)}) collective-permute-start(bf16[64,2560]{1,0:T(8,128)(2,1)S(1)} %lower.11), channel_id=1, source_target_pairs={{0,1},{1,0},{2,3},{3,2},{4,5},{5,4},{6,7},{7,6},{8,9},{9,8},{10,11... | collective-permute-start | bytes 983048 | tf_op jit(solution)/shard_map/ppermute | solution.py:603
  92.8 7.2 %collective-permute-start.26 = (bf16[64,1280]{1,0:T(8,128)(2,1)S(1)}, bf16[64,1280]{1,0:T(8,128)(2,1)S(1)}, u32[]{:S(2)}, u32[]{:S(2)}) collective-permute-start(bf16[64,1280]{1,0:T(8,128)(2,1)S(1)} %get-tuple-element.176), channel_id=1, source_target_pairs={{0,2},{1,3},{2,0},{3,1},{4,6},{5,7},{6,4},{7,5},{8,10},{9,11},{10,... | collective-permute-start | bytes 491528 | tf_op jit(solution)/shard_map/ppermute | solution.py:603
  95.0 7.9 %collective-permute-start.29 = (bf16[64,1280]{1,0:T(8,128)(2,1)S(1)}, bf16[64,1280]{1,0:T(8,128)(2,1)S(1)}, u32[]{:S(2)}, u32[]{:S(2)}) collective-permute-start(bf16[64,1280]{1,0:T(8,128)(2,1)S(1)} %get-tuple-element.175), channel_id=1, source_target_pairs={{0,2},{1,3},{2,0},{3,1},{4,6},{5,7},{6,4},{7,5},{8,10},{9,11},{10,... | collective-permute-start | bytes 491528 | tf_op jit(solution)/shard_map/ppermute | solution.py:603
  97.0 8.1 %collective-permute-start.28 = (f32[1,72,256]{2,1,0:T(8,128)S(1)}, f32[1,72,256]{2,1,0:T(8,128)S(1)}, u32[]{:S(2)}, u32[]{:S(2)}) collective-permute-start(f32[1,72,256]{2,1,0:T(8,128)S(1)} %bitcast.34), channel_id=1, source_target_pairs={{0,8},{4,12},{8,0},{12,4},{1,9},{5,13},{9,1},{13,5},{2,10},{6,14},... | collective-permute-start | bytes 221192 | tf_op jit(solution)/shard_map/ppermute | solution.py:603
  103.1 7.1 %collective-permute-start.33 = (bf16[64,1280]{1,0:T(8,128)(2,1)S(1)}, bf16[64,1280]{1,0:T(8,128)(2,1)S(1)}, u32[]{:S(2)}, u32[]{:S(2)}) collective-permute-start(bf16[64,1280]{1,0:T(8,128)(2,1)S(1)} %get-tuple-element.165.rest_1_), channel_id=1, source_target_pairs={{0,2},{1,3},{2,0},{3,1},{4,6},{5,7},{6,4},{7,5},{8,10},{9,11},{10,... | collective-permute-start | bytes 491528 | tf_op jit(solution)/shard_map/ppermute | solution.py:603
  104.9 5.3 %collective-permute-start.32 = (bf16[64,1408]{1,0:T(8,128)(2,1)S(1)}, bf16[64,1408]{1,0:T(8,128)(2,1)S(1)}, u32[]{:S(2)}, u32[]{:S(2)}) collective-permute-start(bf16[64,1408]{1,0:T(8,128)(2,1)S(1)} %pad_maximum_fusion.6.rest_0_), channel_id=1, source_target_pairs={{0,1},{1,0},{2,3},{3,2},{4,5},{5,4},{6,7},{7,6},{8,9},{9,8},{10,11... | collective-permute-start | bytes 540680 | tf_op jit(solution)/shard_map/ppermute | solution.py:603
  105.1 7.8 %collective-permute-start.31 = (f32[2,72,256]{2,1,0:T(8,128)S(1)}, f32[2,72,256]{2,1,0:T(8,128)S(1)}, u32[]{:S(2)}, u32[]{:S(2)}) collective-permute-start(f32[2,72,256]{2,1,0:T(8,128)S(1)} %pad_maximum_fusion.9), channel_id=1, source_target_pairs={{0,4},{4,0},{8,12},{12,8},{1,5},{5,1},{9,13},{13,9},{2,6},{6,2},{1... | collective-permute-start | bytes 442376 | tf_op jit(solution)/shard_map/ppermute | solution.py:603
  106.2 9.0 %collective-permute-start.27 = (bf16[64,1408]{1,0:T(8,128)(2,1)S(1)}, bf16[64,1408]{1,0:T(8,128)(2,1)S(1)}, u32[]{:S(2)}, u32[]{:S(2)}) collective-permute-start(bf16[64,1408]{1,0:T(8,128)(2,1)S(1)} %pad_maximum_fusion.6.rest_0_), channel_id=1, source_target_pairs={{0,2},{1,3},{2,0},{3,1},{4,6},{5,7},{6,4},{7,5},{8,10},{9,11},{10,... | collective-permute-start | bytes 540680 | tf_op jit(solution)/shard_map/ppermute | solution.py:603
  110.2 8.6 %collective-permute-start.35 = (bf16[64,1280]{1,0:T(8,128)(2,1)S(1)}, bf16[64,1280]{1,0:T(8,128)(2,1)S(1)}, u32[]{:S(2)}, u32[]{:S(2)}) collective-permute-start(bf16[64,1280]{1,0:T(8,128)(2,1)S(1)} %collective-permute-done.33.rest_1_), channel_id=1, source_target_pairs={{0,1},{1,0},{2,3},{3,2},{4,5},{5,4},{6,7},{7,6},{8,9},{9,8},{10,11... | collective-permute-start | bytes 491528 | tf_op jit(solution)/shard_map/ppermute | solution.py:603
  (40 other events, 139.1 us)
where the time goes:
time: 124 us; the launch traced here: 122 us
  Pallas kernels  52.6 us (42%)
  starting transfers between devices  29.6 us (24%)
  local copies, waits for them, and re-layouts  15.9 us (13%)
  waiting for transfers between devices  13.7 us (11%)
  other arithmetic  9.25 us (7%)
  between operations  1.39 us (1%)
    ppermute x36, starting transfers between devices, swap(): return lax.ppermute(x, axis, [(i, i ^ bit) for i in range(size)])  29.6 us
    unnamed x56, local copies, waits for them, and re-layouts  15.1 us
    ppermute x36, waiting for transfers between devices, swap(): return lax.ppermute(x, axis, [(i, i ^ bit) for i in range(size)])  13.7 us
    pallas_call x3, Pallas kernels, shards(): step_call(final)  12.3 us
    pallas_call x3, Pallas kernels, shards(): price_call(0, half_way, True)  8.31 us
    pallas_call x1, Pallas kernels, shards(): first_call(ents, sorted_bus, load, ptdf_tiles, place, g, p)  7.33 us
    pallas_call x3, Pallas kernels, shards(): price_call(half_way, tail, False)  6.55 us
    pallas_call x3, Pallas kernels, shards(): parts[0].append(lower_call(0, 1)(ents, compact, spill, base, picked)[0])  5.85 us
  transfers between devices with their start and end apart: 36, of which 9 were waited for; matrix products, arithmetic and copies ran while one was open for 8% of the time, Pallas kernels for 25%

commit v1 on v0

--- a/solution.py
+++ b/solution.py
@@ -40,8 +40,8 @@
     return pltpu.CompilerParams(vmem_limit_bytes=mib * 1024 * 1024)
 
 
-def cost(us):
-    return pl.CostEstimate(flops=0, bytes_accessed=int(us * 3.0e6), transcendentals=0)
+def cost(us, flops=0):
+    return pl.CostEstimate(flops=flops, bytes_accessed=int(us * 3.0e6), transcendentals=0)
 
 
 def lanes(at):
@@ -54,7 +54,7 @@
 def plan_kernel(
     chunks, quarter_tiles,
     mine, gen_bus, stor_bus, tile_row, tile_col,
-    place, sorted_bus, ents,
+    place, back, sorted_bus, ents,
     tiles,
 ):
     units = place.shape[0]
@@ -80,15 +80,21 @@
     ordered = jnp.zeros((1, units), F32)
     starts = jnp.zeros((1, LANE), F32)
     stops = jnp.zeros((1, LANE), F32)
+    ranks = []
     for b in range(blocks):
         here = column(bus[:, b * LANE : (b + 1) * LANE])
         rank = over_lane(key < here * units + (sub[:, :1] + float(b * LANE)), 1.0)
         mine_at = rank == unit
         place[b * LANE : (b + 1) * LANE] = jnp.where(mine_at, 1.0, 0.0).astype(BF16)
         ordered += over_sub(mine_at, here)
+        ranks.append(over_sub(eye, rank))
         starts += over_sub(here < lane * LANE, 1.0)
         stops += over_sub(here < (lane + 1.0) * LANE, 1.0)
+    ranks = jnp.concatenate(ranks, axis=1)
     for b in range(blocks):
+        back[b * LANE : (b + 1) * LANE] = jnp.where(
+            sub[:, :1] + float(b * LANE) == ranks, 1.0, 0.0
+        ).astype(BF16)
         sorted_bus[b] = jnp.broadcast_to(column(ordered[:, b * LANE : (b + 1) * LANE]), square)
 
     tiles[...] = jnp.zeros_like(tiles)
@@ -220,12 +226,9 @@
 def add_prices(
     ents, compact, spill, stage, sem, bars, lines, total, cap, quarter_tiles, first, last
 ):
-    half = (quarter_tiles + 1) // 2
-    origin = first * quarter_tiles
+    origin, width = first * quarter_tiles, quarter_tiles * LANE
     for d in range(last - first):
-        at = d * quarter_tiles
-        lines[:, at * LANE : (at + half) * LANE] = bars[2 * d][:, : half * LANE]
-        lines[:, (at + half) * LANE : (at + quarter_tiles) * LANE] = bars[2 * d + 1][...]
+        lines[:, d * width : (d + 1) * width] = bars[d][:, :width]
     spare, blocks = (last - first) * quarter_tiles, total.shape[0] - 2
 
     def entry(e, live, matrix):
@@ -236,7 +239,7 @@
     lo, hi = ents[START, first], ents[START, last]
     sweep_held(lo, hi, compact, spill, stage, sem, entry)
     for d in range(last - first):
-        total[blocks + 1] += bars[2 * d][:, half * LANE :].astype(F32)
+        total[blocks + 1] += bars[d][:, width:].astype(F32)
 
 
 def choose(g, p, place, picked):
@@ -303,7 +306,7 @@
 
 
 def price_kernel(cap, quarter_tiles, first, last, fresh, ents, compact, spill, *rest):
-    count = 2 * (last - first)
+    count = last - first
     bars, rest = rest[:count], rest[count:]
     if fresh:
         total, stage, sem, lines = rest
@@ -318,11 +321,11 @@
 
 def step_kernel(
     cap, chunks, quarter_tiles, balance_step, final,
-    ents, compact, spill, place, before, generation, charging, fixed_g, fixed_p, balance_dual,
+    ents, compact, spill, place, back, before, generation, charging, fixed_g, fixed_p, balance_dual,
     limits, base, load_sum, *rest,
 ):
     start = chunks - chunks // 4
-    count = 2 * (chunks - start)
+    count = chunks - start
     bars, rest = rest[:count], rest[count:]
     if final:
         next_g, next_p, stage, sem, lines, prices = rest
@@ -339,7 +342,7 @@
     price = jnp.concatenate([prices[m] for m in range(blocks)], axis=1)
     high = price.astype(BF16)
     low = (price - high.astype(F32)).astype(BF16)
-    price = mxu(jnp.concatenate([high, low], axis=0), place[...], NT)
+    price = mxu(jnp.concatenate([high, low], axis=0), back[...], NN)
     price = price[:hours] + price[hours:]
     old = balance_dual[...]
     new = old + balance_step * jnp.sum(prices[blocks + 1], axis=1, keepdims=True)
@@ -454,8 +457,6 @@
     years = lax.axis_size("tm")
     lines = flow_limit.shape[0] // chunks
     quarter_tiles = lines // LANE
-    half = (quarter_tiles + 1) // 2 * LANE
-    widths = (half, lines - half)
     blocks = units // LANE
     line_tiles = chunks * quarter_tiles
     mine = lax.axis_index("bus")
@@ -468,20 +469,34 @@
     def like(*shape, dtype=F32):
         return jax.ShapeDtypeStruct(shape, dtype)
 
+    limits = lax.dynamic_slice_in_dim(flow_limit, mine * lines, lines)[None, :] * SIGMA
+    unit_rows = jnp.stack(
+        [
+            jnp.concatenate([gen_cost, stor_power]),
+            jnp.concatenate([gen_max, stor_power]),
+            jnp.concatenate([ramp_limit, stor_cap]),
+            jnp.concatenate([ramp_limit, jnp.log1p(-stor_loss)]),
+        ]
+    )
+
+    gen_bus, *early = lax.optimization_barrier((gen_bus, unit_rows, limits))
+    unit_rows, limits = early
+
     width = -(-(cap + SMALL) // LANE) * LANE
-    place, sorted_bus, ents = pl.pallas_call(
+    place, back, sorted_bus, ents = pl.pallas_call(
         functools.partial(plan_kernel, chunks, quarter_tiles),
         out_shape=(
+            like(units, units, dtype=BF16),
             like(units, units, dtype=BF16),
             like(blocks, LANE, LANE),
             like(8, width, dtype=jnp.int32),
         ),
         in_specs=[smem()] + [vmem()] * 4,
-        out_specs=(vmem(),) * 3,
+        out_specs=(vmem(),) * 4,
         scratch_shapes=[pltpu.VMEM((8, LANE), jnp.int32)],
         compiler_params=params(STEP_MIB),
         name="plan",
-        cost_estimate=cost(3),
+        cost_estimate=cost(3, 3 * 10**9),
     )(
         mine.astype(jnp.int32).reshape(1),
         *[x[None, :] for x in (gen_bus, stor_bus, tile_row, tile_col)],
@@ -532,7 +547,7 @@
         return pl.pallas_call(
             functools.partial(price_kernel, cap, quarter_tiles, first, last, fresh),
             out_shape=like(*price_shape),
-            in_specs=[smem(), vmem(), hbm()] + [vmem()] * (2 * (last - first) + (not fresh)),
+            in_specs=[smem(), vmem(), hbm()] + [vmem()] * (last - first + (not fresh)),
             out_specs=vmem(),
             scratch_shapes=staging + [line_scratch(last - first)],
             compiler_params=params(STEP_MIB),
@@ -552,7 +567,7 @@
         return pl.pallas_call(
             functools.partial(step_kernel, cap, chunks, quarter_tiles, balance_step, final),
             out_shape=shape,
-            in_specs=[smem(), vmem(), hbm()] + [vmem()] * (10 + 2 * (chunks - tail)),
+            in_specs=[smem(), vmem(), hbm()] + [vmem()] * (11 + chunks - tail),
             out_specs=(vmem(),) * len(shape),
             scratch_shapes=scratch,
             compiler_params=params(STEP_MIB),
@@ -587,17 +602,6 @@
     )
 
     where = lax.axis_index("tm").astype(jnp.int32).reshape(1)
-    limits = lax.dynamic_slice_in_dim(flow_limit, mine * lines, lines)[None, :] * SIGMA
-    limits = (limits[:, :half], limits[:, half:])
-    unit_rows = jnp.stack(
-        [
-            jnp.concatenate([gen_cost, stor_power]),
-            jnp.concatenate([gen_max, stor_power]),
-            jnp.concatenate([ramp_limit, stor_cap]),
-            jnp.concatenate([ramp_limit, jnp.log1p(-stor_loss)]),
-        ]
-    )
-
     def swap(x, bit, axis="bus"):
         size = lax.axis_size(axis)
         return lax.ppermute(x, axis, [(i, i ^ bit) for i in range(size)])
@@ -607,11 +611,8 @@
             stacked = jnp.concatenate([stacked, swap(stacked, bit, "tm")])
         return stacked
 
-    def cut(xs, h):
-        return [x[:, :half] if h == 0 else x[:, half:] for x in xs]
-
     bits = [1 << b for b in range(chunks.bit_length() - 1)]
-    line_dual = [jnp.zeros((hours, w), F32) for w in widths]
+    line_dual = jnp.zeros((hours, lines), F32)
     ramp_dual = jnp.zeros((hours + 8, gens), F32)
     state_dual = jnp.zeros((groups, 8, stores), F32)
     balance_dual = jnp.zeros((hours, 1), F32)
@@ -631,63 +632,57 @@
     for iteration in range(ITERS):
         parts = {d: [x] for d, x in zip(range(half_way, chunks), upper)}
         reduce(parts)
-        ready = [sum(x.astype(F32) for x in cut(parts[half_way], h)).astype(BF16) for h in (0, 1)]
-        across = [swap(x, half_way) for x in ready]
+        ready = sum(x.astype(F32) for x in parts[half_way]).astype(BF16)
+        across = swap(ready, half_way)
         parts = {d: [] for d in range(half_way)}
         if half_way > 1:
             made = lower_call(1, half_way)(ents, compact, spill, base, picked)
             for d, x in zip(range(1, half_way), made):
                 parts[d].append(x)
-        sent, picked, *_ = lax.optimization_barrier((sent, picked, *ready))
+        sent, picked, *_ = lax.optimization_barrier((sent, picked, ready))
         parts[0].append(lower_call(0, 1)(ents, compact, spill, base, picked)[0])
         reduce(parts)
-        sent, parts[0][0] = lax.optimization_barrier((sent, parts[0][0]))
         heard = hear(sent[None], spans[:1])
-        have = {0: []}
-        for h in range(2):
-            flows = sum(x.astype(F32) for x in cut(parts[0], h) + [across[h]])
-            shift = line_dual[h] + SIGMA * flows
-            after = shift - jnp.clip(shift, -limits[h], limits[h])
-            bar = (2.0 * after - line_dual[h]).astype(BF16)
-            line_dual[h] = after
-            have[0].append(jnp.concatenate([bar, balance], axis=1) if h == 0 else bar)
-            if h == 0:
-                line_dual[1], have[0][0] = lax.optimization_barrier((line_dual[1], have[0][0]))
-        have[half_way] = [swap(x, half_way) for x in have[0]]
+        shift = line_dual + SIGMA * sum(x.astype(F32) for x in parts[0] + [across])
+        after = shift - jnp.clip(shift, -limits, limits)
+        bar = (2.0 * after - line_dual).astype(BF16)
+        line_dual = after
+        have = {0: jnp.concatenate([bar, balance], axis=1)}
+        heard, have[0] = lax.optimization_barrier((heard, have[0]))
+        have[half_way] = swap(have[0], half_way)
         near = [0]
         for bit in reversed(bits[:-1]):
             for d in list(near):
-                have[d | bit] = [swap(x, bit) for x in have[d]]
+                have[d | bit] = swap(have[d], bit)
                 near.append(d | bit)
-        heard, *_ = lax.optimization_barrier((heard, have[near[-1]][1]))
+        prices = price_call(0, half_way, True)(
+            ents, compact, spill, *[have[d] for d in range(half_way)]
+        )
         heard = hear(heard, spans[1:])
-        prices = price_call(0, half_way, True)(
-            ents, compact, spill, *[x for d in range(half_way) for x in have[d]]
-        )
         heard, prices = lax.optimization_barrier((heard, prices))
         fixed_g, fixed_p, ramp_dual, state_dual = hourly_call(
             where, g, unit_rows, ramp_dual, state_dual, *[heard[j] for j in range(years)]
         )
-        have[half_way][0], prices, fixed_g, fixed_p = lax.optimization_barrier(
-            (have[half_way][0], prices, fixed_g, fixed_p)
+        have[half_way], prices, fixed_g, fixed_p = lax.optimization_barrier(
+            (have[half_way], prices, fixed_g, fixed_p)
         )
         far = [half_way]
         for bit in reversed(bits[:-1]):
             for d in list(far):
-                have[d | bit] = [swap(x, bit) for x in have[d]]
+                have[d | bit] = swap(have[d], bit)
                 far.append(d | bit)
         if tail > half_way:
             prices = price_call(half_way, tail, False)(
-                ents, compact, spill, *[x for d in range(half_way, tail) for x in have[d]], prices
+                ents, compact, spill, *[have[d] for d in range(half_way, tail)], prices
             )
         final = iteration == ITERS - 1
         g, p, *rest = step_call(final)(
-            ents, compact, spill, place, prices, g, p, fixed_g, fixed_p, balance_dual,
-            unit_rows, base, load_sum, *[x for d in range(tail, chunks) for x in have[d]],
+            ents, compact, spill, place, back, prices, g, p, fixed_g, fixed_p, balance_dual,
+            unit_rows, base, load_sum, *[have[d] for d in range(tail, chunks)],
         )
         if not final:
             balance_dual, *upper, balance, sent, picked = rest
-    return g, p, jnp.concatenate(line_dual, axis=1)
+    return g, p, line_dual
 
 
 STEP_MIB = 16

time: 124 us -> 116 us (0.935); the launches traced: 122 us -> 116 us
  waiting for transfers between devices: 13.7 us -> 23.7 us
  local copies, waits for them, and re-layouts: 15.9 us -> 8.1 us
  starting transfers between devices: 29.6 us -> 22 us
  other arithmetic: 9.25 us -> 6.86 us
  Pallas kernels: 52.6 us -> 54.3 us
    ppermute x36 -> x24, waiting for transfers between devices: 13.7 us -> 23.7 us  [swap(): return lax.ppermute(x, axis, [(i, i ^ bit) for i in range(size)])]
    unnamed x56 -> x46, local copies, waits for them, and re-layouts: 15.1 us -> 7.28 us
    ppermute x36 -> x24, starting transfers between devices: 29.6 us -> 22 us  [swap(): return lax.ppermute(x, axis, [(i, i ^ bit) for i in range(size)])]
    convert_element_type x9 -> x6, other arithmetic: 5.7 us -> 2.04 us  [the longest x3 1.81 us: shards(): bar = (2.0 * after - line_dual).astype(BF16)]
  transfers between devices with their start and end apart: 36 -> 24, of which waited for: 9 -> 10; matrix products, arithmetic and copies ran while one was open for 8% -> 2% of each run, Pallas kernels for 25% -> 29%
where the time goes in v1:
time: 116 us
  Pallas kernels  54.3 us (47%)
  waiting for transfers between devices  23.7 us (20%)
  starting transfers between devices  22 us (19%)
  local copies, waits for them, and re-layouts  8.1 us (7%)
  other arithmetic  6.86 us (6%)
  between operations  1.32 us (1%)
    ppermute x24, waiting for transfers between devices, swap(): return lax.ppermute(x, axis, [(i, i ^ bit) for i in range(size)])  23.7 us
    ppermute x24, starting transfers between devices, swap(): return lax.ppermute(x, axis, [(i, i ^ bit) for i in range(size)])  22 us
    pallas_call x3, Pallas kernels, shards(): step_call(final)  11.9 us
    pallas_call x3, Pallas kernels, shards(): price_call(0, half_way, True)  9.32 us
    pallas_call x3, Pallas kernels, shards(): price_call(half_way, tail, False)  7.41 us
    unnamed x46, local copies, waits for them, and re-layouts  7.28 us
    pallas_call x1, Pallas kernels, shards(): first_call(ents, sorted_bus, load, ptdf_tiles, place, g, p)  7.13 us
    pallas_call x3, Pallas kernels, shards(): parts[0].append(lower_call(0, 1)(ents, compact, spill, base, picked)[0])  5.86 us
  transfers between devices with their start and end apart: 24, of which 10 were waited for; matrix products, arithmetic and copies ran while one was open for 2% of the time, Pallas kernels for 29%

profile of v1, /device:TPU:0, one launch (start us, length us, event | category | flops | bytes accessed | tf_op | source)
XLA Modules:
  0.0 116.2 jit_solution(9801471786637730162)
XLA Ops:
  9.6 7.1 %first.1 = (bf16[168,128,128]{2,1,0:T(8,128)(2,1)S(1)}, bf16[1500,128,128]{2,1,0:T(8,128)(2,1)}, f32[64,10368]{1,0:T(8,128)S(1)}, f32[64,1]{1,0:T(8,128)S(1)}, b...) custom-call(s32[8,896]{1,0:T(8,128)S(1)} %get-tuple-element.78.ents,, ...), custom_call_target="tpu_custom_call" | custom-call | bytes 27000000 | tf_op jit(solution)/shard_map/first/pallas_call | solution.py:620
  20.3 2.4 %collective-permute-start.3 = (bf16[64,2560]{1,0:T(8,128)(2,1)S(1)}, bf16[64,2560]{1,0:T(8,128)(2,1)S(1)}, u32[]{:S(2)}, u32[]{:S(2)}) collective-permute-start(bf16[64,2560]{1,0:T(8,128)(2,1)S(1)} %add_convert_fusion.2), channel_id=1, source_target_pairs={{0,2},{1,3},{2,0},{3,1},{4,6},{5,7},{6,4},{7,5},{8,10},{9,11},{10,... | collective-permute-start | bytes 983048 | tf_op jit(solution)/shard_map/ppermute | solution.py:607
  22.7 2.6 %collective-permute-start.1 = (f32[1,72,256]{2,1,0:T(8,128)S(1)}, f32[1,72,256]{2,1,0:T(8,128)S(1)}, u32[]{:S(2)}, u32[]{:S(2)}) collective-permute-start(f32[1,72,256]{2,1,0:T(8,128)S(1)} %bitcast.34), channel_id=1, source_target_pairs={{0,8},{4,12},{8,0},{12,4},{1,9},{5,13},{9,1},{13,5},{2,10},{6,14},... | collective-permute-start | bytes 221192 | tf_op jit(solution)/shard_map/ppermute | solution.py:607
  27.3 2.2 %collective-permute-done.1 = f32[1,72,256]{2,1,0:T(8,128)S(1)} collective-permute-done((f32[1,72,256]{2,1,0:T(8,128)S(1)}, f32[1,72,256]{2,1,0:T(8,128)S(1)}, u32[]{:S(2)}, u32[]{:S(2)}) %collective-permute-start.1) | collective-permute-done | bytes 73760 | tf_op jit(solution)/shard_map/ppermute | solution.py:607
  31.5 2.2 %collective-permute-start.5 = (f32[2,72,256]{2,1,0:T(8,128)}, f32[2,72,256]{2,1,0:T(8,128)}, u32[]{:S(2)}, u32[]{:S(2)}) collective-permute-start(f32[2,72,256]{2,1,0:T(8,128)} %pad_maximum_fusion.6), channel_id=1, source_target_pairs={{0,4},{4,0},{8,12},{12,8},{1,5},{5,1},{9,13},{13,9},{2,6},{6,2},{1... | collective-permute-start | bytes 442376 | tf_op jit(solution)/shard_map/ppermute | solution.py:607
  34.8 3.4 %collective-permute-done.5 = f32[2,72,256]{2,1,0:T(8,128)} collective-permute-done((f32[2,72,256]{2,1,0:T(8,128)}, f32[2,72,256]{2,1,0:T(8,128)}, u32[]{:S(2)}, u32[]{:S(2)}) %collective-permute-start.5) | collective-permute-done | bytes 147488 | tf_op jit(solution)/shard_map/ppermute | solution.py:607
  39.3 2.6 %copy-done.1 = bf16[168,128,128]{2,1,0:T(8,128)(2,1)S(1)} copy-done((bf16[168,128,128]{2,1,0:T(8,128)(2,1)S(1)}, bf16[168,128,128]{2,1,0:T(8,128)(2,1)}, u32[]{:S(2)}) %copy-start.1) | copy-done | bytes 5505048
  41.8 3.2 %price.6.rest_1_ = f32[9,64,128]{2,1,0:T(8,128)S(1)} custom-call(s32[8,896]{1,0:T(8,128)S(1)} %get-tuple-element.78.ents, bf16[168,128,128]{2,1,0:T(8,128)(2,1)S(1)} %copy-done.1, bf16[1500,128,128]{2,1,0:T(8,128)(2,1)} %get-tuple-element.82.spill, bf16[64,2688]{1,0:T(8,128)(2,1)S(1)} %pad_maximum_fusion.rest_0_, bf16[64,2688]{1,0:T(8,128)(2,1)} %collective-permute-done.6.rest_1_), custom_call_target="tpu_custom_call" | custom-call | bytes 6000000 | tf_op jit(solution)/shard_map/price/pallas_call | solution.py:658
  46.7 2.5 %price.7.before = f32[9,64,128]{2,1,0:T(8,128)S(1)} custom-call(s32[8,896]{1,0:T(8,128)S(1)} %get-tuple-element.78.ents, bf16[168,128,128]{2,1,0:T(8,128)(2,1)S(1)} %copy-done.2, bf16[1500,128,128]{2,1,0:T(8,128)(2,1)} %get-tuple-element.82.spill, bf16[64,2688]{1,0:T(8,128)(2,1)S(1)} %collective-permute-done.4.rest_0_, f32[9,64,128]{2,1,0:T(8,128)S(1)} %price.6.rest_1_), custom_call_target="tpu_custom_call" | custom-call | bytes 6000000 | tf_op jit(solution)/shard_map/price/pallas_call | solution.py:675
  49.2 4.3 %step.3 = (f32[64,640]{1,0:T(8,128)S(1)}, f32[64,256]{1,0:T(8,128)S(1)}, f32[64,1]{1,0:T(8,128)S(1)}, bf16[64,2560]{1,0:T(8,128)(2,1)S(1)}, bf16[64,2560]{1,0:T(...) custom-call(s32[8,896]{1,0:T(8,128)S(1)} %get-tuple-element.78.ents, ...), custom_call_target="tpu_custom_call" | custom-call | bytes 12000000 | tf_op jit(solution)/shard_map/step/pallas_call | solution.py:679
  57.3 2.5 %collective-permute-start.9 = (f32[1,72,256]{2,1,0:T(8,128)S(1)}, f32[1,72,256]{2,1,0:T(8,128)S(1)}, u32[]{:S(2)}, u32[]{:S(2)}) collective-permute-start(f32[1,72,256]{2,1,0:T(8,128)S(1)} %bitcast.36), channel_id=1, source_target_pairs={{0,8},{4,12},{8,0},{12,4},{1,9},{5,13},{9,1},{13,5},{2,10},{6,14},... | collective-permute-start | bytes 221192 | tf_op jit(solution)/shard_map/ppermute | solution.py:607
  61.7 2.4 %collective-permute-done.9 = f32[1,72,256]{2,1,0:T(8,128)S(1)} collective-permute-done((f32[1,72,256]{2,1,0:T(8,128)S(1)}, f32[1,72,256]{2,1,0:T(8,128)S(1)}, u32[]{:S(2)}, u32[]{:S(2)}) %collective-permute-start.9) | collective-permute-done | bytes 73760 | tf_op jit(solution)/shard_map/ppermute | solution.py:607
  69.3 3.4 %collective-permute-done.13 = f32[2,72,256]{2,1,0:T(8,128)S(1)} collective-permute-done((f32[2,72,256]{2,1,0:T(8,128)S(1)}, f32[2,72,256]{2,1,0:T(8,128)S(1)}, u32[]{:S(2)}, u32[]{:S(2)}) %collective-permute-start.13) | collective-permute-done | bytes 147488 | tf_op jit(solution)/shard_map/ppermute | solution.py:607
  72.8 3.1 %price.8.rest_1_ = f32[9,64,128]{2,1,0:T(8,128)S(1)} custom-call(s32[8,896]{1,0:T(8,128)S(1)} %get-tuple-element.78.ents, bf16[168,128,128]{2,1,0:T(8,128)(2,1)S(1)} %copy-done.2, bf16[1500,128,128]{2,1,0:T(8,128)(2,1)} %get-tuple-element.82.spill, bf16[64,2688]{1,0:T(8,128)(2,1)S(1)} %pad_maximum_fusion.1.rest_0_, ...), custom_call_target="tpu_custom_call" | custom-call | bytes 6000000 | tf_op jit(solution)/shard_map/price/pallas_call | solution.py:658
  78.4 2.5 %price.9.before = f32[9,64,128]{2,1,0:T(8,128)S(1)} custom-call(s32[8,896]{1,0:T(8,128)S(1)} %get-tuple-element.78.ents, bf16[168,128,128]{2,1,0:T(8,128)(2,1)S(1)} %copy-done.2, bf16[1500,128,128]{2,1,0:T(8,128)(2,1)} %get-tuple-element.82.spill, bf16[64,2688]{1,0:T(8,128)(2,1)S(1)} %collective-permute-done.12.rest_0_, f32[9,64,128]{2,1,0:T(8,128)S(1)} %price.8.rest_1_), custom_call_target="tpu_custom_call" | custom-call | bytes 6000000 | tf_op jit(solution)/shard_map/price/pallas_call | solution.py:675
  80.9 4.3 %step.4 = (f32[64,640]{1,0:T(8,128)S(1)}, f32[64,256]{1,0:T(8,128)S(1)}, f32[64,1]{1,0:T(8,128)S(1)}, bf16[64,2560]{1,0:T(8,128)(2,1)S(1)}, bf16[64,2560]{1,0:T(...) custom-call(s32[8,896]{1,0:T(8,128)S(1)} %get-tuple-element.78.ents, ...), custom_call_target="tpu_custom_call" | custom-call | bytes 12000000 | tf_op jit(solution)/shard_map/step/pallas_call | solution.py:679
  88.5 2.5 %collective-permute-start.17 = (f32[1,72,256]{2,1,0:T(8,128)S(1)}, f32[1,72,256]{2,1,0:T(8,128)S(1)}, u32[]{:S(2)}, u32[]{:S(2)}) collective-permute-start(f32[1,72,256]{2,1,0:T(8,128)S(1)} %bitcast.32), channel_id=1, source_target_pairs={{0,8},{4,12},{8,0},{12,4},{1,9},{5,13},{9,1},{13,5},{2,10},{6,14},... | collective-permute-start | bytes 221192 | tf_op jit(solution)/shard_map/ppermute | solution.py:607
  93.0 2.2 %collective-permute-done.17 = f32[1,72,256]{2,1,0:T(8,128)S(1)} collective-permute-done((f32[1,72,256]{2,1,0:T(8,128)S(1)}, f32[1,72,256]{2,1,0:T(8,128)S(1)}, u32[]{:S(2)}, u32[]{:S(2)}) %collective-permute-start.17) | collective-permute-done | bytes 73760 | tf_op jit(solution)/shard_map/ppermute | solution.py:607
  95.2 2.2 %collective-permute-done.19 = bf16[64,2560]{1,0:T(8,128)(2,1)S(1)} collective-permute-done((bf16[64,2560]{1,0:T(8,128)(2,1)S(1)}, bf16[64,2560]{1,0:T(8,128)(2,1)S(1)}, u32[]{:S(2)}, u32[]{:S(2)}) %collective-permute-start.19) | collective-permute-done | bytes 327712 | tf_op jit(solution)/shard_map/ppermute | solution.py:607
  100.4 4.4 %collective-permute-done.21 = f32[2,72,256]{2,1,0:T(8,128)S(1)} collective-permute-done((f32[2,72,256]{2,1,0:T(8,128)S(1)}, f32[2,72,256]{2,1,0:T(8,128)S(1)}, u32[]{:S(2)}, u32[]{:S(2)}) %collective-permute-start.21) | collective-permute-done | bytes 147488 | tf_op jit(solution)/shard_map/ppermute | solution.py:607
  104.9 3.1 %price.10.rest_1_ = f32[9,64,128]{2,1,0:T(8,128)S(1)} custom-call(s32[8,896]{1,0:T(8,128)S(1)} %get-tuple-element.78.ents, bf16[168,128,128]{2,1,0:T(8,128)(2,1)S(1)} %copy-done.2, bf16[1500,128,128]{2,1,0:T(8,128)(2,1)} %get-tuple-element.82.spill, bf16[64,2688]{1,0:T(8,128)(2,1)S(1)} %pad_maximum_fusion.2.rest_0_, ...), custom_call_target="tpu_custom_call" | custom-call | bytes 6000000 | tf_op jit(solution)/shard_map/price/pallas_call | solution.py:658
  108.0 2.2 %hourly.5 = (f32[64,640]{1,0:T(8,128)S(1)}, f32[64,256]{1,0:T(8,128)S(1)}, f32[72,640]{1,0:T(8,128)}, f32[32,8,256]{2,1,0:T(8,128)}) custom-call(s32[1]{0:T(128)} %bitcast.5.where, f32[64,640]{1,0:T(8,128)S(1)} %get-tuple-element.137.generation, f32[4,896]{1,0:T(4,128)S(1)} %pad_maximum_fusion.9.limits, f32[72,640]{1,0:T(8,128)S(1)} %get-tuple-element.138.ramp_dual, ...), custom_call_target="tpu_custom_call" | custom-call | bytes 7200000 | tf_op jit(solution)/shard_map/hourly/pallas_call | solution.py:663
  110.2 2.5 %price.11.before = f32[9,64,128]{2,1,0:T(8,128)S(1)} custom-call(s32[8,896]{1,0:T(8,128)S(1)} %get-tuple-element.78.ents, bf16[168,128,128]{2,1,0:T(8,128)(2,1)S(1)} %copy-done.2, bf16[1500,128,128]{2,1,0:T(8,128)(2,1)} %get-tuple-element.82.spill, bf16[64,2688]{1,0:T(8,128)(2,1)S(1)} %collective-permute-done.20.rest_0_, f32[9,64,128]{2,1,0:T(8,128)S(1)} %price.10.rest_1_), custom_call_target="tpu_custom_call" | custom-call | bytes 6000000 | tf_op jit(solution)/shard_map/price/pallas_call | solution.py:675
  112.7 3.3 %step.5 = (f32[64,640]{1,0:T(8,128)}, f32[64,256]{1,0:T(8,128)}) custom-call(s32[8,896]{1,0:T(8,128)S(1)} %get-tuple-element.78.ents, bf16[168,128,128]{2,1,0:T(8,128)(2,1)S(1)} %copy-done.2, bf16[1500,128,128]{2,1,0:T(8,128)(2,1)} %get-tuple-element.82.spill, bf16[896,896]{1,0:T(8,128)(2,1)S(1)} %copy-done.4, bf16[896,896]{1,0:T(8,128)(2,1)S(1)} %copy-done.6, ...), custom_call_target="tpu_custom_call" | custom-call | bytes 12000000 | tf_op jit(solution)/shard_map/step/pallas_call | solution.py:679
  (123 shorter events, 42.0 us)
Async XLA Ops:
  17.9 2.3 %collective-permute-start = (bf16[64,2560]{1,0:T(8,128)(2,1)S(1)}, bf16[64,2560]{1,0:T(8,128)(2,1)S(1)}, u32[]{:S(2)}, u32[]{:S(2)}) collective-permute-start(bf16[64,2560]{1,0:T(8,128)(2,1)S(1)} %get-tuple-element.87), channel_id=1, source_target_pairs={{0,1},{1,0},{2,3},{3,2},{4,5},{5,4},{6,7},{7,6},{8,9},{9,8},{10,11... | collective-permute-start | bytes 983048 | tf_op jit(solution)/shard_map/ppermute | solution.py:607
  19.9 10.3 %collective-permute-start.2 = (bf16[64,2560]{1,0:T(8,128)(2,1)S(1)}, bf16[64,2560]{1,0:T(8,128)(2,1)S(1)}, u32[]{:S(2)}, u32[]{:S(2)}) collective-permute-start(bf16[64,2560]{1,0:T(8,128)(2,1)S(1)} %lower.7), channel_id=1, source_target_pairs={{0,1},{1,0},{2,3},{3,2},{4,5},{5,4},{6,7},{7,6},{8,9},{9,8},{10,11... | collective-permute-start | bytes 983048 | tf_op jit(solution)/shard_map/ppermute | solution.py:607
  20.3 10.5 %collective-permute-start.3 = (bf16[64,2560]{1,0:T(8,128)(2,1)S(1)}, bf16[64,2560]{1,0:T(8,128)(2,1)S(1)}, u32[]{:S(2)}, u32[]{:S(2)}) collective-permute-start(bf16[64,2560]{1,0:T(8,128)(2,1)S(1)} %add_convert_fusion.2), channel_id=1, source_target_pairs={{0,2},{1,3},{2,0},{3,1},{4,6},{5,7},{6,4},{7,5},{8,10},{9,11},{10,... | collective-permute-start | bytes 983048 | tf_op jit(solution)/shard_map/ppermute | solution.py:607
  22.7 6.8 %collective-permute-start.1 = (f32[1,72,256]{2,1,0:T(8,128)S(1)}, f32[1,72,256]{2,1,0:T(8,128)S(1)}, u32[]{:S(2)}, u32[]{:S(2)}) collective-permute-start(f32[1,72,256]{2,1,0:T(8,128)S(1)} %bitcast.34), channel_id=1, source_target_pairs={{0,8},{4,12},{8,0},{12,4},{1,9},{5,13},{9,1},{13,5},{2,10},{6,14},... | collective-permute-start | bytes 221192 | tf_op jit(solution)/shard_map/ppermute | solution.py:607
  31.1 8.2 %collective-permute-start.6 = (bf16[64,2688]{1,0:T(8,128)(2,1)S(1)}, bf16[64,2688]{1,0:T(8,128)(2,1)}, u32[]{:S(2)}, u32[]{:S(2)}) collective-permute-start(bf16[64,2688]{1,0:T(8,128)(2,1)S(1)} %pad_maximum_fusion.rest_0_), channel_id=1, source_target_pairs={{0,1},{1,0},{2,3},{3,2},{4,5},{5,4},{6,7},{7,6},{8,9},{9,8},{10,11... | collective-permute-start | bytes 1032200 | tf_op jit(solution)/shard_map/ppermute | solution.py:607
  31.5 6.7 %collective-permute-start.5 = (f32[2,72,256]{2,1,0:T(8,128)}, f32[2,72,256]{2,1,0:T(8,128)}, u32[]{:S(2)}, u32[]{:S(2)}) collective-permute-start(f32[2,72,256]{2,1,0:T(8,128)} %pad_maximum_fusion.6), channel_id=1, source_target_pairs={{0,4},{4,0},{8,12},{12,8},{1,5},{5,1},{9,13},{13,9},{2,6},{6,2},{1... | collective-permute-start | bytes 442376 | tf_op jit(solution)/shard_map/ppermute | solution.py:607
  33.8 12.8 %collective-permute-start.4 = (bf16[64,2688]{1,0:T(8,128)(2,1)S(1)}, bf16[64,2688]{1,0:T(8,128)(2,1)S(1)}, u32[]{:S(2)}, u32[]{:S(2)}) collective-permute-start(bf16[64,2688]{1,0:T(8,128)(2,1)S(1)} %pad_maximum_fusion.rest_0_), channel_id=1, source_target_pairs={{0,2},{1,3},{2,0},{3,1},{4,6},{5,7},{6,4},{7,5},{8,10},{9,11},{10,... | collective-permute-start | bytes 1032200 | tf_op jit(solution)/shard_map/ppermute | solution.py:607
  46.6 2.6 %collective-permute-start.7 = (bf16[64,2688]{1,0:T(8,128)(2,1)S(1)}, bf16[64,2688]{1,0:T(8,128)(2,1)S(1)}, u32[]{:S(2)}, u32[]{:S(2)}) collective-permute-start(bf16[64,2688]{1,0:T(8,128)(2,1)S(1)} %collective-permute-done.4.rest_0_), channel_id=1, source_target_pairs={{0,1},{1,0},{2,3},{3,2},{4,5},{5,4},{6,7},{7,6},{8,9},{9,8},{10,11... | collective-permute-start | bytes 1032200 | tf_op jit(solution)/shard_map/ppermute | solution.py:607
  53.5 2.6 %collective-permute-start.8 = (bf16[64,2560]{1,0:T(8,128)(2,1)S(1)}, bf16[64,2560]{1,0:T(8,128)(2,1)S(1)}, u32[]{:S(2)}, u32[]{:S(2)}) collective-permute-start(bf16[64,2560]{1,0:T(8,128)(2,1)S(1)} %get-tuple-element.108), channel_id=1, source_target_pairs={{0,1},{1,0},{2,3},{3,2},{4,5},{5,4},{6,7},{7,6},{8,9},{9,8},{10,11... | collective-permute-start | bytes 983048 | tf_op jit(solution)/shard_map/ppermute | solution.py:607
  55.5 8.5 %collective-permute-start.10 = (bf16[64,2560]{1,0:T(8,128)(2,1)S(1)}, bf16[64,2560]{1,0:T(8,128)(2,1)S(1)}, u32[]{:S(2)}, u32[]{:S(2)}) collective-permute-start(bf16[64,2560]{1,0:T(8,128)(2,1)S(1)} %lower.9), channel_id=1, source_target_pairs={{0,1},{1,0},{2,3},{3,2},{4,5},{5,4},{6,7},{7,6},{8,9},{9,8},{10,11... | collective-permute-start | bytes 983048 | tf_op jit(solution)/shard_map/ppermute | solution.py:607
  56.2 9.7 %collective-permute-start.11 = (bf16[64,2560]{1,0:T(8,128)(2,1)S(1)}, bf16[64,2560]{1,0:T(8,128)(2,1)S(1)}, u32[]{:S(2)}, u32[]{:S(2)}) collective-permute-start(bf16[64,2560]{1,0:T(8,128)(2,1)S(1)} %add_convert_fusion.1), channel_id=1, source_target_pairs={{0,2},{1,3},{2,0},{3,1},{4,6},{5,7},{6,4},{7,5},{8,10},{9,11},{10,... | collective-permute-start | bytes 983048 | tf_op jit(solution)/shard_map/ppermute | solution.py:607
  57.3 6.8 %collective-permute-start.9 = (f32[1,72,256]{2,1,0:T(8,128)S(1)}, f32[1,72,256]{2,1,0:T(8,128)S(1)}, u32[]{:S(2)}, u32[]{:S(2)}) collective-permute-start(f32[1,72,256]{2,1,0:T(8,128)S(1)} %bitcast.36), channel_id=1, source_target_pairs={{0,8},{4,12},{8,0},{12,4},{1,9},{5,13},{9,1},{13,5},{2,10},{6,14},... | collective-permute-start | bytes 221192 | tf_op jit(solution)/shard_map/ppermute | solution.py:607
  66.4 6.4 %collective-permute-start.14 = (bf16[64,2688]{1,0:T(8,128)(2,1)S(1)}, bf16[64,2688]{1,0:T(8,128)(2,1)S(1)}, u32[]{:S(2)}, u32[]{:S(2)}) collective-permute-start(bf16[64,2688]{1,0:T(8,128)(2,1)S(1)} %pad_maximum_fusion.1.rest_0_), channel_id=1, source_target_pairs={{0,1},{1,0},{2,3},{3,2},{4,5},{5,4},{6,7},{7,6},{8,9},{9,8},{10,11... | collective-permute-start | bytes 1032200 | tf_op jit(solution)/shard_map/ppermute | solution.py:607
  66.5 6.3 %collective-permute-start.13 = (f32[2,72,256]{2,1,0:T(8,128)S(1)}, f32[2,72,256]{2,1,0:T(8,128)S(1)}, u32[]{:S(2)}, u32[]{:S(2)}) collective-permute-start(f32[2,72,256]{2,1,0:T(8,128)S(1)} %pad_maximum_fusion.7), channel_id=1, source_target_pairs={{0,4},{4,0},{8,12},{12,8},{1,5},{5,1},{9,13},{13,9},{2,6},{6,2},{1... | collective-permute-start | bytes 442376 | tf_op jit(solution)/shard_map/ppermute | solution.py:607
  68.2 10.1 %collective-permute-start.12 = (bf16[64,2688]{1,0:T(8,128)(2,1)S(1)}, bf16[64,2688]{1,0:T(8,128)(2,1)S(1)}, u32[]{:S(2)}, u32[]{:S(2)}) collective-permute-start(bf16[64,2688]{1,0:T(8,128)(2,1)S(1)} %pad_maximum_fusion.1.rest_0_), channel_id=1, source_target_pairs={{0,2},{1,3},{2,0},{3,1},{4,6},{5,7},{6,4},{7,5},{8,10},{9,11},{10,... | collective-permute-start | bytes 1032200 | tf_op jit(solution)/shard_map/ppermute | solution.py:607
  78.4 2.5 %collective-permute-start.15 = (bf16[64,2688]{1,0:T(8,128)(2,1)S(1)}, bf16[64,2688]{1,0:T(8,128)(2,1)S(1)}, u32[]{:S(2)}, u32[]{:S(2)}) collective-permute-start(bf16[64,2688]{1,0:T(8,128)(2,1)S(1)} %collective-permute-done.12.rest_0_), channel_id=1, source_target_pairs={{0,1},{1,0},{2,3},{3,2},{4,5},{5,4},{6,7},{7,6},{8,9},{9,8},{10,11... | collective-permute-start | bytes 1032200 | tf_op jit(solution)/shard_map/ppermute | solution.py:607
  85.2 2.4 %collective-permute-start.16 = (bf16[64,2560]{1,0:T(8,128)(2,1)S(1)}, bf16[64,2560]{1,0:T(8,128)(2,1)S(1)}, u32[]{:S(2)}, u32[]{:S(2)}) collective-permute-start(bf16[64,2560]{1,0:T(8,128)(2,1)S(1)} %get-tuple-element.130), channel_id=1, source_target_pairs={{0,1},{1,0},{2,3},{3,2},{4,5},{5,4},{6,7},{7,6},{8,9},{9,8},{10,11... | collective-permute-start | bytes 983048 | tf_op jit(solution)/shard_map/ppermute | solution.py:607
  87.0 8.2 %collective-permute-start.18 = (bf16[64,2560]{1,0:T(8,128)(2,1)S(1)}, bf16[64,2560]{1,0:T(8,128)(2,1)S(1)}, u32[]{:S(2)}, u32[]{:S(2)}) collective-permute-start(bf16[64,2560]{1,0:T(8,128)(2,1)S(1)} %lower.11), channel_id=1, source_target_pairs={{0,1},{1,0},{2,3},{3,2},{4,5},{5,4},{6,7},{7,6},{8,9},{9,8},{10,11... | collective-permute-start | bytes 983048 | tf_op jit(solution)/shard_map/ppermute | solution.py:607
  87.6 9.7 %collective-permute-start.19 = (bf16[64,2560]{1,0:T(8,128)(2,1)S(1)}, bf16[64,2560]{1,0:T(8,128)(2,1)S(1)}, u32[]{:S(2)}, u32[]{:S(2)}) collective-permute-start(bf16[64,2560]{1,0:T(8,128)(2,1)S(1)} %add_convert_fusion), channel_id=1, source_target_pairs={{0,2},{1,3},{2,0},{3,1},{4,6},{5,7},{6,4},{7,5},{8,10},{9,11},{10,... | collective-permute-start | bytes 983048 | tf_op jit(solution)/shard_map/ppermute | solution.py:607
  88.5 6.7 %collective-permute-start.17 = (f32[1,72,256]{2,1,0:T(8,128)S(1)}, f32[1,72,256]{2,1,0:T(8,128)S(1)}, u32[]{:S(2)}, u32[]{:S(2)}) collective-permute-start(f32[1,72,256]{2,1,0:T(8,128)S(1)} %bitcast.32), channel_id=1, source_target_pairs={{0,8},{4,12},{8,0},{12,4},{1,9},{5,13},{9,1},{13,5},{2,10},{6,14},... | collective-permute-start | bytes 221192 | tf_op jit(solution)/shard_map/ppermute | solution.py:607
  98.5 6.4 %collective-permute-start.22 = (bf16[64,2688]{1,0:T(8,128)(2,1)S(1)}, bf16[64,2688]{1,0:T(8,128)(2,1)S(1)}, u32[]{:S(2)}, u32[]{:S(2)}) collective-permute-start(bf16[64,2688]{1,0:T(8,128)(2,1)S(1)} %pad_maximum_fusion.2.rest_0_), channel_id=1, source_target_pairs={{0,1},{1,0},{2,3},{3,2},{4,5},{5,4},{6,7},{7,6},{8,9},{9,8},{10,11... | collective-permute-start | bytes 1032200 | tf_op jit(solution)/shard_map/ppermute | solution.py:607
  98.6 6.3 %collective-permute-start.21 = (f32[2,72,256]{2,1,0:T(8,128)S(1)}, f32[2,72,256]{2,1,0:T(8,128)S(1)}, u32[]{:S(2)}, u32[]{:S(2)}) collective-permute-start(f32[2,72,256]{2,1,0:T(8,128)S(1)} %pad_maximum_fusion.8), channel_id=1, source_target_pairs={{0,4},{4,0},{8,12},{12,8},{1,5},{5,1},{9,13},{13,9},{2,6},{6,2},{1... | collective-permute-start | bytes 442376 | tf_op jit(solution)/shard_map/ppermute | solution.py:607
  99.3 10.9 %collective-permute-start.20 = (bf16[64,2688]{1,0:T(8,128)(2,1)S(1)}, bf16[64,2688]{1,0:T(8,128)(2,1)S(1)}, u32[]{:S(2)}, u32[]{:S(2)}) collective-permute-start(bf16[64,2688]{1,0:T(8,128)(2,1)S(1)} %pad_maximum_fusion.2.rest_0_), channel_id=1, source_target_pairs={{0,2},{1,3},{2,0},{3,1},{4,6},{5,7},{6,4},{7,5},{8,10},{9,11},{10,... | collective-permute-start | bytes 1032200 | tf_op jit(solution)/shard_map/ppermute | solution.py:607
  110.2 2.5 %collective-permute-start.23 = (bf16[64,2688]{1,0:T(8,128)(2,1)S(1)}, bf16[64,2688]{1,0:T(8,128)(2,1)S(1)}, u32[]{:S(2)}, u32[]{:S(2)}) collective-permute-start(bf16[64,2688]{1,0:T(8,128)(2,1)S(1)} %collective-permute-done.20.rest_0_), channel_id=1, source_target_pairs={{0,1},{1,0},{2,3},{3,2},{4,5},{5,4},{6,7},{7,6},{8,9},{9,8},{10,11... | collective-permute-start | bytes 1032200 | tf_op jit(solution)/shard_map/ppermute | solution.py:607
  (23 other events, 77.8 us)

commit v2 on v1

v2 whole, which is shorter than its diff:
```python
import functools

import jax
import jax.numpy as jnp
from jax import lax
from jax.experimental import pallas as pl
from jax.experimental.pallas import tpu as pltpu
from jax.sharding import PartitionSpec as P

ITERS = 3
TAU = 0.5
SIGMA = 0.5
LANE = 128
LARGE, SMALL = 32, 8
KEPT = 160
F32 = jnp.float32
BF16 = jnp.bfloat16

NN = (((1,), (0,)), ((), ()))
NT = (((1,), (1,)), ((), ()))


def mxu(a, b, dims):
    return lax.dot_general(a, b, dims, preferred_element_type=F32)


def smem():
    return pl.BlockSpec(memory_space=pltpu.SMEM)


def vmem():
    return pl.BlockSpec(memory_space=pltpu.VMEM)


def hbm():
    return pl.BlockSpec(memory_space=pl.ANY)


def params(mib):
    return pltpu.CompilerParams(vmem_limit_bytes=mib * 1024 * 1024)


def cost(us, flops=0):
    return pl.CostEstimate(flops=flops, bytes_accessed=int(us * 3.0e6), transcendentals=0)


def lanes(at):
    return pl.ds(pl.multiple_of(at * LANE, LANE), LANE)


ROW, BLOCK, START, TILE, COLUMN, FIRST = range(6)
FEW = 256
LOW = 7

COST, HIGH, RAMP, CAP, LOSS = range(5)
BUS, TILES = range(2)


def plan_kernel(
    chunks, quarter_tiles, kt,
    mine, whole,
    place, back, sorted_bus, ents, few,
):
    units = place.shape[0]
    blocks = units // LANE
    square = (LANE, LANE)
    sub = lax.broadcasted_iota(jnp.int32, square, 0).astype(F32)
    lane = lax.broadcasted_iota(jnp.int32, square, 1).astype(F32)
    eye = sub == lane

    def column(row):
        return jnp.sum(jnp.where(eye, jnp.broadcast_to(row, square), 0.0), axis=1, keepdims=True)

    def over_sub(mask, values):
        return jnp.sum(jnp.where(mask, values, 0.0), axis=0, keepdims=True)

    def over_lane(mask, values):
        return jnp.sum(jnp.where(mask, values, 0.0), axis=1, keepdims=True)

    bus = whole[BUS : BUS + 1].astype(F32)
    unit = lax.broadcasted_iota(jnp.int32, (1, units), 1).astype(F32)
    key = bus * units + unit
    ordered = jnp.zeros((1, units), F32)
    starts = jnp.zeros((1, LANE), F32)
    stops = jnp.zeros((1, LANE), F32)
    ranks = []
    for b in range(blocks):
        here = column(bus[:, b * LANE : (b + 1) * LANE])
        rank = over_lane(key < here * units + (sub[:, :1] + float(b * LANE)), 1.0)
        mine_at = rank == unit
        place[b * LANE : (b + 1) * LANE] = jnp.where(mine_at, 1.0, 0.0).astype(BF16)
        ordered += over_sub(mine_at, here)
        ranks.append(over_sub(eye, rank))
        starts += over_sub(here < lane * LANE, 1.0)
        stops += over_sub(here < (lane + 1.0) * LANE, 1.0)
    ranks = jnp.concatenate(ranks, axis=1)
    for b in range(blocks):
        back[b * LANE : (b + 1) * LANE] = jnp.where(
            sub[:, :1] + float(b * LANE) == ranks, 1.0, 0.0
        ).astype(BF16)
        sorted_bus[b] = jnp.broadcast_to(column(ordered[:, b * LANE : (b + 1) * LANE]), square)

    row = whole[TILES : TILES + 1, :LANE]
    col = whole[TILES : TILES + 1, LANE : 2 * LANE].astype(F32)
    chunk = jnp.zeros_like(row)
    for d in range(1, chunks):
        chunk = chunk + (row >= d * quarter_tiles).astype(jnp.int32)
    relative = (((chunk ^ mine[...]) - chunk) * quarter_tiles + row).astype(F32)
    number = lane[:1]
    tile_key = jnp.where(number < kt, relative, float(chunks * quarter_tiles)) * LANE + number
    rank = over_sub(column(tile_key) < tile_key, 1.0)
    sorting = rank == sub
    relative, col, tile = (over_lane(sorting, x) for x in (relative, col, number))
    first, last = over_lane(lane == col, starts), over_lane(lane == col, stops)
    block = jnp.minimum(jnp.floor(first * (1.0 / LANE)), float(blocks - 1))
    until = jnp.floor((last - 1.0) * (1.0 / LANE))
    count = jnp.where(last > first, until - block + 1.0, 1.0)
    count = jnp.where(sub[:, :1] < kt, count, 0.0)
    at = over_lane(lane < sub, over_sub(eye, count))
    entry = lax.broadcasted_iota(jnp.int32, (1, ents.shape[1]), 1).astype(F32)
    inside = (at <= entry) & (entry < at + count)
    ents[...] = jnp.zeros_like(ents)
    for name, values in (
        (ROW, relative),
        (BLOCK, block - at + entry),
        (TILE, tile),
        (COLUMN, col),
        (FIRST, (entry == at).astype(F32)),
    ):
        ents[name : name + 1] = over_sub(inside, values).astype(jnp.int32)
    ents[START : START + 1, :LANE] = over_sub(relative < lane * quarter_tiles, count).astype(
        jnp.int32
    )
    few[...] = ents[: few.shape[0], :FEW]


def sweep(lo, hi, body):
    hi = jnp.maximum(lo, hi)
    long = (hi - lo) // LARGE

    def group(n, _):
        for u in range(LARGE):
            body(lo + n * LARGE + u, None)
        return 0

    lax.fori_loop(0, long, group, 0)
    rest = lo + long * LARGE

    def short(n, _):
        for u in range(SMALL):
            e = rest + n * SMALL + u
            body(e, e < hi)
        return 0

    lax.fori_loop(0, (hi - rest + SMALL - 1) // SMALL, short, 0)


class Lists:
    def __init__(self, few, ents, compact, spill, few_held, ents_held, stage, sems):
        self.ents, self.compact, self.spill = ents, compact, spill
        self.few_held, self.ents_held, self.stage, self.sems = few_held, ents_held, stage, sems
        self.copy = pltpu.make_async_copy(few, few_held, sems.at[0])
        self.copy.start()
        self.kept = compact.shape[0] - SMALL

    def ready(self, chunks):
        self.copy.wait()

        @pl.when(self.few_held[START, chunks] > self.kept)
        def _():
            copy = pltpu.make_async_copy(self.ents, self.ents_held, self.sems.at[1])
            copy.start()
            copy.wait()

    def sweep(self, first, last, body):
        lo, hi = self.few_held[START, first], self.few_held[START, last]
        held, more = self.few_held, self.ents_held
        sweep(
            lo,
            jnp.minimum(hi, self.kept),
            lambda e, live: body(held[ROW, e], held[BLOCK, e], live, self.compact.at[e]),
        )

        def fetched(e, _):
            copy = pltpu.make_async_copy(self.spill.at[e - self.kept], self.stage, self.sems.at[1])
            copy.start()
            copy.wait()
            body(more[ROW, e], more[BLOCK, e], None, self.stage)
            return 0

        lax.fori_loop(jnp.maximum(lo, self.kept), hi, fetched, 0)


def split(x):
    high = x.astype(BF16)
    rest = x - high.astype(F32)
    middle = rest.astype(BF16)
    low = (rest - middle.astype(F32)).astype(BF16)
    return jnp.concatenate([high, middle, low], axis=0)


def joined(x):
    rows = x.shape[0] // 3
    return x[:rows] + x[rows : 2 * rows] + x[2 * rows :]


def pick(live, value, other):
    return value if live is None else jnp.where(live, value, other)


def build(ents, sorted_bus, load, tiles, compact, spill, base, load_sum, stage, sem, found):
    kept = compact.shape[0] - SMALL
    hours = load.shape[0]
    spare = base.shape[1] // LANE - 1
    base[...] = jnp.zeros_like(base)
    lane = lax.broadcasted_iota(jnp.int32, (LANE, LANE), 1)

    def restricted(e, live):
        col = pick(live, ents[COLUMN, e], 0)
        row = jnp.where(pick(live, ents[FIRST, e], 0) == 1, ents[ROW, e], spare)
        bus = sorted_bus[pick(live, ents[BLOCK, e], 0)]
        hot = jnp.where(bus == (lane + col * LANE).astype(F32), 1.0, 0.0).astype(BF16)
        left = jnp.concatenate([load[:, lanes(col)], hot], axis=0)
        both = mxu(left, tiles[pick(live, ents[TILE, e], 0)], NT)
        base[:, lanes(row)] -= both[:hours]
        return both[hours:].astype(BF16)

    def keep(e, live):
        compact[e] = restricted(e, live)

    def put_out(e, _):
        stage[...] = restricted(e, None)
        copy = pltpu.make_async_copy(stage, spill.at[e - kept], sem)
        copy.start()
        copy.wait()
        return 0

    sweep(jnp.int32(0), jnp.minimum(found, kept), keep)
    lax.fori_loop(jnp.int32(kept), found, put_out, 0)
    total = load[:, :LANE].astype(F32)
    for c in range(1, load.shape[1] // LANE):
        total += load[:, c * LANE : (c + 1) * LANE].astype(F32)
    load_sum[...] = jnp.sum(total, axis=1, keepdims=True)


def start_flows(base, total, quarter_tiles, first, last):
    origin, width = first * quarter_tiles, (last - first) * quarter_tiles
    total[:, : width * LANE] = base[:, origin * LANE : (origin + width) * LANE]


def add_flows(lists, picked, total, quarter_tiles, first, last, outs):
    origin, spare, blocks = first * quarter_tiles, (last - first) * quarter_tiles, picked.shape[0] - 1

    def entry(row, m, live, matrix):
        row, m = pick(live, row - origin, spare), pick(live, m, blocks)
        total[:, lanes(row)] += mxu(picked[m], matrix[...], NN)

    lists.sweep(first, last, entry)
    for d in range(last - first):
        at = d * quarter_tiles
        outs[d][...] = total[:, at * LANE : (at + quarter_tiles) * LANE].astype(BF16)


def start_prices(bars, lines, quarter_tiles):
    width = quarter_tiles * LANE
    for d, bar in enumerate(bars):
        lines[:, d * width : (d + 1) * width] = bar[:, :width]


def add_prices(lists, bars, lines, total, quarter_tiles, first, last):
    origin, width = first * quarter_tiles, quarter_tiles * LANE
    spare, blocks = (last - first) * quarter_tiles, total.shape[0] - 2

    def entry(row, m, live, matrix):
        row, m = pick(live, row - origin, spare), pick(live, m, blocks)
        total[m] += mxu(lines[:, lanes(row)], matrix[...], NT)

    lists.sweep(first, last, entry)
    for bar in bars:
        total[blocks + 1] += bar[:, width:].astype(F32)


def put_picked(z, picked):
    for m in range(picked.shape[0] - 1):
        picked[m] = z[:, m * LANE : (m + 1) * LANE].astype(BF16)


def send_hours(z, own, sent):
    hours, units = z.shape
    stores = own.shape[1]
    sent[:hours] = own
    sent[hours:] = jnp.zeros_like(sent[hours:])
    each = -(-units // stores)
    for i, row in enumerate((z[:1], z[hours - 1 :])):
        for j in range(each):
            piece = row[:, j * stores : min((j + 1) * stores, units)]
            sent[hours + i * each + j : hours + i * each + j + 1, : piece.shape[1]] = piece


def own_balance(z, load_sum, balance):
    value = jnp.sum(z, axis=1, keepdims=True) - load_sum[...]
    lane = lax.broadcasted_iota(jnp.int32, balance.shape, 1)
    high = value.astype(BF16).astype(F32)
    middle = (value - high).astype(BF16).astype(F32)
    low = value - high - middle
    balance[...] = jnp.where(
        lane == 0, high, jnp.where(lane == 1, middle, jnp.where(lane == 2, low, 0.0))
    ).astype(BF16)


def first_kernel(
    chunks, quarter_tiles,
    few, ents, pars, sorted_bus, load, tiles, place, generation, charging,
    compact, spill, base, load_sum, state, rows, *rest,
):
    upper = chunks - chunks // 2
    outs = rest[:upper]
    balance, picked, few_held, ents_held, stage, sems, total = rest[upper:]
    copy = pltpu.make_async_copy(ents, ents_held, sems.at[2])
    copy.start()
    lists = Lists(few, ents, compact, spill, few_held, ents_held, stage, sems)
    hours, gens = generation.shape
    x = jnp.concatenate([generation[...], -charging[...]], axis=1)
    unit = lax.broadcasted_iota(jnp.int32, pars.shape, 1)
    name = lax.broadcasted_iota(jnp.int32, pars.shape, 0)
    own = pars[...]
    low = jnp.broadcast_to(jnp.where(unit[:1] < gens, 0.0, -own[HIGH : HIGH + 1]), own.shape)
    own = jnp.where(name == LOW, low, own)
    own = jnp.where((name == RAMP) & (unit >= gens), 1e30, own)
    left = jnp.concatenate([split(x), split(own)], axis=0)
    ordered = mxu(left, place[...], NN)
    z = joined(ordered[: 3 * hours])
    state[...] = z
    rows[...] = joined(ordered[3 * hours :])
    put_picked(z, picked)
    copy.wait()
    found = ents_held[START, chunks]
    build(ents_held, sorted_bus, load, tiles, compact, spill, base, load_sum, stage, sems.at[1], found)
    own_balance(z, load_sum, balance)
    lists.ready(chunks)
    start_flows(base, total, quarter_tiles, chunks // 2, chunks)
    add_flows(lists, picked, total, quarter_tiles, chunks // 2, chunks, outs)


def lower_kernel(
    chunks, quarter_tiles, first, last,
    few, ents, compact, spill, base, picked, state, back,
    *rest,
):
    outs, rest = rest[: last - first], rest[last - first :]
    if first:
        sent, rest = rest[0], rest[1:]
    few_held, ents_held, stage, sems, total = rest
    lists = Lists(few, ents, compact, spill, few_held, ents_held, stage, sems)
    start_flows(base, total, quarter_tiles, first, last)
    if first:
        z = state[...]
        stores = sent.shape[1]
        own = -joined(mxu(split(z), back[:, z.shape[1] - stores :], NN))
        send_hours(z, own, sent)
    lists.ready(chunks)
    add_flows(lists, picked, total, quarter_tiles, first, last, outs)


def price_kernel(
    chunks, quarter_tiles, first, last, fresh,
    few, ents, compact, spill, *rest,
):
    bars, rest = rest[: last - first], rest[last - first :]
    if not fresh:
        before, rest = rest[0], rest[1:]
    total, few_held, ents_held, stage, sems, lines = rest
    lists = Lists(few, ents, compact, spill, few_held, ents_held, stage, sems)
    total[...] = jnp.zeros_like(total) if fresh else before[...]
    start_prices(bars, lines, quarter_tiles)
    lists.ready(chunks)
    add_prices(lists, bars, lines, total, quarter_tiles, first, last)


def step_kernel(
    chunks, quarter_tiles, balance_step, final,
    few, ents, compact, spill, before, state, fixed, balance_dual, rows, base, load_sum, back,
    *rest,
):
    start, upper = chunks - chunks // 4, chunks // 2
    bars, rest = rest[: chunks - start], rest[chunks - start :]
    if final:
        next_g, next_p, few_held, ents_held, stage, sems, lines, prices = rest
    else:
        next_state, next_balance, *rest = rest
        outs, rest = rest[: chunks - upper], rest[chunks - upper :]
        balance, picked, few_held, ents_held, stage, sems, lines, prices, total = rest
    lists = Lists(few, ents, compact, spill, few_held, ents_held, stage, sems)
    prices[...] = before[...]
    start_prices(bars, lines, quarter_tiles)
    if not final:
        start_flows(base, total, quarter_tiles, upper, chunks)
    lists.ready(chunks)
    add_prices(lists, bars, lines, prices, quarter_tiles, start, chunks)
    blocks = prices.shape[0] - 2
    price = jnp.concatenate([prices[m] for m in range(blocks)], axis=1)
    old = balance_dual[...]
    new = old + balance_step * jnp.sum(prices[blocks + 1], axis=1, keepdims=True)
    bb = 2.0 * new - old
    high = rows[HIGH : HIGH + 1]
    z = state[...] - TAU * (bb + price + fixed[...])
    z = jnp.minimum(jnp.maximum(z, rows[LOW : LOW + 1]), high)
    if final:
        gens = next_g.shape[1]
        x = joined(mxu(split(z), back[...], NN))
        next_g[...] = x[:, :gens]
        next_p[...] = -x[:, gens:]
    else:
        next_state[...] = z
        next_balance[...] = new
        own_balance(z, load_sum, balance)
        put_picked(z, picked)
        add_flows(lists, picked, total, quarter_tiles, upper, chunks, outs)


def hourly_kernel(
    years, hours, order, final,
    where, state, rows, pars, place, ramp_dual, state_dual,
    *rest,
):
    heard, rest = rest[:years], rest[years:]
    if final:
        fixed, everyone, wide, local, bars, adjoint = rest
    else:
        fixed, ramp_out, state_out, everyone, wide, local, bars, adjoint = rest
    gens = state.shape[1]
    units = adjoint.shape[1]
    cost, ramp_limit = rows[COST : COST + 1], rows[RAMP : RAMP + 1]
    cap = pars[CAP : CAP + 1, gens - units :]
    keep = jnp.log1p(-pars[LOSS : LOSS + 1, gens - units :])
    each = -(-gens // units)
    me = where[0]
    before = lax.rem(me + years - 1, years)
    after = lax.rem(me + 1, years)
    for j in range(years):
        everyone[me ^ order[j]] = heard[j][...]
    wide[8 : 8 + hours] = state[...]
    for j in range(each):
        span = min(units, gens - j * units)
        to = slice(j * units, j * units + span)
        at = hours + each + j
        wide[7:8, to] = everyone[before, at : at + 1, :span]
        at = hours + j
        wide[8 + hours : 9 + hours, to] = everyone[after, at : at + 1, :span]
    ramps = wide[8 : 16 + hours] - wide[7 : 15 + hours]
    old = ramp_dual[...]
    shift = old + SIGMA * ramps
    limit = SIGMA * ramp_limit
    new = shift - jnp.minimum(jnp.maximum(shift, -limit), limit)
    if not final:
        ramp_out[...] = new
    wide[0 : 8 + hours] = 2.0 * new - old
    fixed[...] = cost + wide[0:hours] - wide[1 : 1 + hours]

    step = lax.broadcasted_iota(jnp.int32, (8, units), 0)
    rise = jnp.exp((step + 1).astype(F32) * keep)
    fall = jnp.exp((8 - step).astype(F32) * keep)
    one, two, four, eight = (jnp.exp(k * keep) for k in (1.0, 2.0, 4.0, 8.0))
    closing = 1.0 / (1.0 - jnp.exp(float(years * hours) * keep))
    count = years * hours // 8
    per = hours // 8

    def within(n, _):
        y = everyone[n // per, pl.ds(pl.multiple_of((n % per) * 8, 8), 8), :]
        for by, factor in ((1, one), (2, two), (4, four)):
            y = y + jnp.where(step >= by, factor * pltpu.roll(y, by, 0), 0.0)
        local[n] = y
        return 0

    lax.fori_loop(0, count, within, 0, unroll=8)
    zero = jnp.zeros((1, units), F32)
    finish = lax.fori_loop(0, count, lambda n, c: local[n][7:8] + eight * c, zero, unroll=8)

    def forward(n, c):
        y = local[n]
        state = y + rise * c
        old = state_dual[n]
        shift = old + SIGMA * state
        new = shift - jnp.minimum(jnp.maximum(shift, 0.0), SIGMA * cap)
        if not final:
            state_out[n] = new
        bar = 2.0 * new - old
        for by, factor in ((1, one), (2, two), (4, four)):
            bar = bar + jnp.where(step < 8 - by, factor * pltpu.roll(bar, 8 - by, 0), 0.0)
        bars[n] = bar
        return y[7:8] + eight * c

    lax.fori_loop(0, count, forward, finish * closing, unroll=8)

    def back(i, c):
        return bars[count - 1 - i][0:1] + eight * c

    finish = lax.fori_loop(0, count, back, zero, unroll=8)
    c = lax.fori_loop(0, count - (me + 1) * per, back, finish * closing)
    for j in reversed(range(per)):
        y = bars[me * per + j]
        adjoint[8 * j : 8 * j + 8] = y + fall * c
        c = y[0:1] + eight * c
    fixed[...] -= joined(mxu(split(adjoint[...]), place[gens - units :], NN))


def shards(
    gen_start, charge_start, load, ptdf_tiles, tile_row, tile_col, gen_bus, stor_bus,
    gen_cost, gen_max, ramp_limit, stor_power, stor_loss, stor_cap, flow_limit,
):
    hours, gens = gen_start.shape
    stores = charge_start.shape[1]
    units = gens + stores
    kt = ptdf_tiles.shape[0]
    bus_tiles = load.shape[1] // LANE
    chunks = lax.axis_size("bus")
    years = lax.axis_size("tm")
    lines = flow_limit.shape[0] // chunks
    quarter_tiles = lines // LANE
    blocks = units // LANE
    line_tiles = chunks * quarter_tiles
    mine = lax.axis_index("bus")
    balance_step = SIGMA / (gens * chunks)
    cap = blocks * kt + LARGE
    kept = min(cap, KEPT) // SMALL * SMALL
    sent_rows = -(-(hours + 2 * -(-units // stores)) // 8) * 8
    groups = years * hours // 8

    def like(*shape, dtype=F32):
        return jax.ShapeDtypeStruct(shape, dtype)


    def placed(count, *parts):
        total = 0
        for row, at, x in parts:
            before = row * units + at
            total += jnp.pad(x, (before, count * units - before - x.shape[0]))
        return total.reshape(count, units)

    pars = placed(
        8,
        (COST, 0, gen_cost),
        (HIGH, 0, gen_max),
        (HIGH, gens, stor_power),
        (RAMP, 0, ramp_limit),
        (CAP, gens, stor_cap),
        (LOSS, gens, stor_loss),
    )
    whole = placed(
        2, (BUS, 0, gen_bus), (BUS, gens, stor_bus), (TILES, 0, tile_row), (TILES, LANE, tile_col)
    )

    width = -(-(cap + SMALL) // LANE) * LANE
    where = lax.axis_index("tm").astype(jnp.int32).reshape(1)
    from_line = mine.astype(jnp.uint32) * lines
    whole, where, from_line = lax.optimization_barrier((whole, where, from_line))
    place, back, sorted_bus, ents, few = pl.pallas_call(
        functools.partial(plan_kernel, chunks, quarter_tiles, kt),
        out_shape=(
            like(units, units, dtype=BF16),
            like(units, units, dtype=BF16),
            like(blocks, LANE, LANE),
            like(8, width, dtype=jnp.int32),
            like(4, FEW, dtype=jnp.int32),
        ),
        in_specs=[vmem()] * 2,
        out_specs=(vmem(),) * 5,
        compiler_params=params(STEP_MIB),
        name="plan",
        cost_estimate=cost(3, 3 * 10**9),
    )(jnp.broadcast_to(mine.astype(jnp.int32), (1, LANE)), whole)

    chunk_out = (like(hours, lines, dtype=BF16),) * (chunks // 2)
    staging = [
        pltpu.SMEM((4, FEW), jnp.int32),
        pltpu.SMEM((8, width), jnp.int32),
        pltpu.VMEM((LANE, LANE), BF16),
        pltpu.SemaphoreType.DMA((3,)),
    ]
    lists = [vmem(), vmem(), vmem(), hbm()]
    picked_shape = like(blocks + 1, hours, LANE, dtype=BF16)

    def flow_scratch(count):
        return [pltpu.VMEM((hours, (count * quarter_tiles + 1) * LANE), F32)]

    def line_scratch(count):
        return pltpu.VMEM((hours, (count * quarter_tiles + 1) * LANE), BF16)

    price_shape = (blocks + 2, hours, LANE)
    first_call = pl.pallas_call(
        functools.partial(first_kernel, chunks, quarter_tiles),
        out_shape=(
            like(kept + SMALL, LANE, LANE, dtype=BF16),
            like(max(cap - kept, SPILL), LANE, LANE, dtype=BF16),
            like(hours, (line_tiles + 1) * LANE),
            like(hours, 1),
            like(hours, units),
            like(8, units),
        )
        + chunk_out
        + (like(hours, LANE, dtype=BF16), picked_shape),
        in_specs=[vmem()] * 9,
        out_specs=(vmem(), hbm()) + (vmem(),) * (chunks // 2 + 6),
        scratch_shapes=staging + flow_scratch(chunks // 2),
        compiler_params=params(STEP_MIB),
        name="first",
        cost_estimate=cost(9),
    )

    def lower_call(first, last):
        return pl.pallas_call(
            functools.partial(lower_kernel, chunks, quarter_tiles, first, last),
            out_shape=(like(hours, lines, dtype=BF16),) * (last - first)
            + ((like(sent_rows, stores),) if first else ()),
            in_specs=lists + [vmem()] * 4,
            out_specs=(vmem(),) * (last - first + (first > 0)),
            scratch_shapes=staging + flow_scratch(last - first),
            compiler_params=params(STEP_MIB),
            name="lower",
            cost_estimate=cost(2),
        )

    def line_scratch(count):
        return pltpu.VMEM((hours, (count * quarter_tiles + 1) * LANE), BF16)

    price_shape = (blocks + 2, hours, LANE)

    def price_call(first, last, fresh):
        return pl.pallas_call(
            functools.partial(price_kernel, chunks, quarter_tiles, first, last, fresh),
            out_shape=like(*price_shape),
            in_specs=lists + [vmem()] * (last - first + (not fresh)),
            out_specs=vmem(),
            scratch_shapes=staging + [line_scratch(last - first)],
            compiler_params=params(STEP_MIB),
            name="price",
            cost_estimate=cost(2),
        )

    tail = chunks - chunks // 4

    def step_call(final):
        scratch = staging + [line_scratch(chunks - tail), pltpu.VMEM(price_shape, F32)]
        if final:
            shape = (like(hours, gens), like(hours, stores))
        else:
            shape = (like(hours, units), like(hours, 1)) + chunk_out
            shape += (like(hours, LANE, dtype=BF16), picked_shape)
            scratch += flow_scratch(chunks // 2)
        return pl.pallas_call(
            functools.partial(step_kernel, chunks, quarter_tiles, balance_step, final),
            out_shape=shape,
            in_specs=lists + [vmem()] * (8 + chunks - tail),
            out_specs=(vmem(),) * len(shape),
            scratch_shapes=scratch,
            compiler_params=params(STEP_MIB),
            name="step",
            cost_estimate=cost(4),
        )

    spans = [1 << b for b in reversed(range(years.bit_length() - 1))]
    order = [0]
    for bit in spans:
        order += [j ^ bit for j in order]

    def hourly_call(final):
        shape = (like(hours, units),)
        if not final:
            shape += (like(hours + 8, units), like(groups, 8, stores))
        return pl.pallas_call(
            functools.partial(hourly_kernel, years, hours, order, final),
            out_shape=shape,
            in_specs=[smem()] + [vmem()] * (6 + years),
            out_specs=(vmem(),) * len(shape),
            scratch_shapes=[
                pltpu.VMEM((years, sent_rows, stores), F32),
                pltpu.VMEM((hours + 16, units), F32),
                pltpu.VMEM((groups, 8, stores), F32),
                pltpu.VMEM((groups, 8, stores), F32),
                pltpu.VMEM((hours, stores), F32),
            ],
            compiler_params=params(STEP_MIB),
            name="hourly",
            cost_estimate=cost(2.4),
        )

    def swap(x, bit, axis="bus"):
        size = lax.axis_size(axis)
        return lax.ppermute(x, axis, [(i, i ^ bit) for i in range(size)])

    def hear(stacked, over):
        for bit in over:
            stacked = jnp.concatenate([stacked, swap(stacked, bit, "tm")])
        return stacked

    bits = [1 << b for b in range(chunks.bit_length() - 1)]
    line_dual = jnp.zeros((hours, lines), F32)
    ramp_dual = jnp.zeros((hours + 8, units), F32)
    state_dual = jnp.zeros((groups, 8, stores), F32)
    balance_dual = jnp.zeros((hours, 1), F32)
    compact, spill, base, load_sum, state, unit_rows, *upper, balance, picked = first_call(
        few, ents, pars, sorted_bus, load, ptdf_tiles, place, gen_start, charge_start
    )
    held = (few, ents, compact, spill)
    half_way = chunks // 2

    def reduce(parts):
        for bit in bits[:-1]:
            for d in sorted(parts, reverse=True):
                if d & bit and not d & (bit - 1):
                    got = swap(sum(x.astype(F32) for x in parts[d]).astype(BF16), bit)
                    parts[d ^ bit].append(got)

    for iteration in range(ITERS):
        parts = {d: [x] for d, x in zip(range(half_way, chunks), upper)}
        reduce(parts)
        ready = sum(x.astype(F32) for x in parts[half_way]).astype(BF16)
        across = swap(ready, half_way)
        parts = {d: [] for d in range(half_way)}
        *made, sent = lower_call(1, half_way)(*held, base, picked, state, back)
        for d, x in zip(range(1, half_way), made):
            parts[d].append(x)
        sent, picked, *_ = lax.optimization_barrier((sent, picked, ready))
        parts[0].append(lower_call(0, 1)(*held, base, picked, state, back)[0])
        reduce(parts)
        heard = hear(sent[None], spans[:1])
        limits = SIGMA * lax.dynamic_slice(flow_limit, (from_line,), (lines,))
        shift = line_dual + SIGMA * sum(x.astype(F32) for x in parts[0] + [across])
        after = shift - jnp.clip(shift, -limits, limits)
        bar = (2.0 * after - line_dual).astype(BF16)
        line_dual = after
        have = {0: jnp.concatenate([bar, balance], axis=1)}
        heard, have[0] = lax.optimization_barrier((heard, have[0]))
        have[half_way] = swap(have[0], half_way)
        near = [0]
        for bit in reversed(bits[:-1]):
            for d in list(near):
                have[d | bit] = swap(have[d], bit)
                near.append(d | bit)
        final = iteration == ITERS - 1
        heard = hear(heard, spans[1:])
        fixed, *duals = hourly_call(final)(
            where, state, unit_rows, pars, place, ramp_dual, state_dual,
            *[heard[j] for j in range(years)],
        )
        have[0], fixed = lax.optimization_barrier((have[0], fixed))
        prices = price_call(0, half_way, True)(*held, *[have[d] for d in range(half_way)])
        have[half_way], prices, fixed = lax.optimization_barrier((have[half_way], prices, fixed))
        far = [half_way]
        for bit in reversed(bits[:-1]):
            for d in list(far):
                have[d | bit] = swap(have[d], bit)
                far.append(d | bit)
        if tail > half_way:
            prices = price_call(half_way, tail, False)(
                *held, *[have[d] for d in range(half_way, tail)], prices
            )
        made = step_call(final)(
            *held, prices, state, fixed, balance_dual, unit_rows, base, load_sum, back,
            *[have[d] for d in range(tail, chunks)],
        )
        if not final:
            ramp_dual, state_dual = duals
            state, balance_dual, *upper, balance, picked = made
    return *made, line_dual


STEP_MIB = 16
SPILL = 1500


def solution(mesh):
    rows = P(("scen", "tm"), "bus")
    return jax.shard_map(
        shards,
        mesh=mesh,
        in_specs=(rows, rows, rows, P("bus", None, None)) + (P("bus"),) * 10 + (P(),),
        out_specs=(rows, rows, rows),
        check_vma=False,
    )
```

time: 116 us -> 103 us (0.89)
  Pallas kernels: 54.3 us -> 46.3 us
  local copies, waits for them, and re-layouts: 8.1 us -> 0.25 us
  waiting for transfers between devices: 23.7 us -> 27.8 us
  other arithmetic: 6.86 us -> 4.47 us
    unnamed x46 -> x8, local copies, waits for them, and re-layouts: 7.28 us -> 0.12 us
    ppermute x24, waiting for transfers between devices: 23.7 us -> 27.8 us  [swap(): return lax.ppermute(x, axis, [(i, i ^ bit) for i in range(size)])]
    pallas_call x14, Pallas kernels: 34.9 us -> 31 us  [the longest x3 7.81 us: shards(): price_call(0, half_way, True)(*held, *[have[d] for d in range(half_way)])]
    pallas_call x3, Pallas kernels: 11.9 us -> 9.85 us  [shards(): step_call(final)]
    pallas_call x3, Pallas kernels: 7.41 us -> 5.46 us  [shards(): price_call(half_way, tail, False)]
    concatenate x6 -> x3, other arithmetic: 1.73 us -> 0.04 us  [hear(): stacked = jnp.concatenate([stacked, swap(stacked, bit, 'tm')])]
    add x0 -> x2, other arithmetic: none -> 1.52 us  [placed(): total += jnp.pad(x, (before, count * units - before - x.shape[0]))]
    concatenate x2 -> x0, other arithmetic: 1.44 us -> none  [the longest x1 0.73 us: shards(): jnp.concatenate([gen_cost, stor_power])]
  transfers between devices with their start and end apart: 24 -> 24, of which waited for: 10 -> 9; matrix products, arithmetic and copies ran while one was open for 2% -> 1% of each run, Pallas kernels for 29% -> 27%
where the time goes in v2:
time: 103 us
  Pallas kernels  46.3 us (45%)
  waiting for transfers between devices  27.8 us (27%)
  starting transfers between devices  22.5 us (22%)
  other arithmetic  4.47 us (4%)
  between operations  1.3 us (1%)
    ppermute x24, waiting for transfers between devices, swap(): return lax.ppermute(x, axis, [(i, i ^ bit) for i in range(size)])  27.8 us
    ppermute x24, starting transfers between devices, swap(): return lax.ppermute(x, axis, [(i, i ^ bit) for i in range(size)])  22.5 us
    pallas_call x3, Pallas kernels, shards(): step_call(final)  9.85 us
    pallas_call x3, Pallas kernels, shards(): price_call(0, half_way, True)(*held, *[have[d] for d in range(half_way)])  7.81 us
    pallas_call x1, Pallas kernels, shards(): first_call(few, ents, pars, sorted_bus, load, ptdf_tiles, place, gen_star...  6.87 us
    pallas_call x3, Pallas kernels, shards(): price_call(half_way, tail, False)  5.46 us
    pallas_call x3, Pallas kernels, shards(): hourly_call(final)  5.39 us
    pallas_call x3, Pallas kernels, shards(): *made, sent = lower_call(1, half_way)(*held, base, picked, state, back)  4.85 us
  transfers between devices with their start and end apart: 24, of which 9 were waited for; matrix products, arithmetic and copies ran while one was open for 1% of the time, Pallas kernels for 27%

profile of v2, /device:TPU:0, one launch (start us, length us, event | category | flops | bytes accessed | tf_op | source)
XLA Modules:
  0.0 102.7 jit_solution(16705446536149568304)
XLA Ops:
  2.2 2.1 %plan.1 = (bf16[896,896]{1,0:T(8,128)(2,1)S(1)}, bf16[896,896]{1,0:T(8,128)(2,1)S(1)}, f32[7,128,128]{2,1,0:T(8,128)S(1)}, s32[8,896]{1,0:T(8,128)S(1)}, s32[4,256]{1,0:T(4,128)S(1)}) custom-call(s32[1,128]{1,0:T(1,128)S(1)} %broadcast_in_dim.29.mine, s32[2,896]{1,0:T(2,128)S(1)} %reshape.17.whole), custom_call_target="tpu_custom_call" | custom-call | flops 3000000000 | bytes 9000000 | tf_op jit(solution)/shard_map/plan/pallas_call | solution.py:557
  4.4 6.9 %first.1 = (bf16[168,128,128]{2,1,0:T(8,128)(2,1)S(1)}, bf16[1500,128,128]{2,1,0:T(8,128)(2,1)}, f32[64,10368]{1,0:T(8,128)S(1)}, f32[64,1]{1,0:T(8,128)S(1)}, f...) custom-call(s32[4,256]{1,0:T(4,128)S(1)} %get-tuple-element.75.few, ...), custom_call_target="tpu_custom_call" | custom-call | bytes 27000000 | tf_op jit(solution)/shard_map/first/pallas_call | solution.py:701
  13.7 2.4 %collective-permute-start.3 = (bf16[64,2560]{1,0:T(8,128)(2,1)S(1)}, bf16[64,2560]{1,0:T(8,128)(2,1)S(1)}, u32[]{:S(2)}, u32[]{:S(2)}) collective-permute-start(bf16[64,2560]{1,0:T(8,128)(2,1)S(1)} %add_convert_fusion.2), channel_id=1, source_target_pairs={{0,2},{1,3},{2,0},{3,1},{4,6},{5,7},{6,4},{7,5},{8,10},{9,11},{10,... | collective-permute-start | bytes 983048 | tf_op jit(solution)/shard_map/ppermute | solution.py:689
  16.1 2.6 %collective-permute-start.1 = (f32[1,72,256]{2,1,0:T(8,128)S(1)}, f32[1,72,256]{2,1,0:T(8,128)S(1)}, u32[]{:S(2)}, u32[]{:S(2)}) collective-permute-start(f32[1,72,256]{2,1,0:T(8,128)S(1)} %bitcast.28), channel_id=1, source_target_pairs={{0,8},{4,12},{8,0},{12,4},{1,9},{5,13},{9,1},{13,5},{2,10},{6,14},... | collective-permute-start | bytes 221192 | tf_op jit(solution)/shard_map/ppermute | solution.py:689
  20.8 1.9 %collective-permute-done.1 = f32[1,72,256]{2,1,0:T(8,128)S(1)} collective-permute-done((f32[1,72,256]{2,1,0:T(8,128)S(1)}, f32[1,72,256]{2,1,0:T(8,128)S(1)}, u32[]{:S(2)}, u32[]{:S(2)}) %collective-permute-start.1) | collective-permute-done | bytes 73760 | tf_op jit(solution)/shard_map/ppermute | solution.py:689
  24.3 1.8 %collective-permute-start.4 = (bf16[64,2688]{1,0:T(8,128)(2,1)S(1)}, bf16[64,2688]{1,0:T(8,128)(2,1)S(1)}, u32[]{:S(2)}, u32[]{:S(2)}) collective-permute-start(bf16[64,2688]{1,0:T(8,128)(2,1)S(1)} %pad_maximum_fusion.rest_0_), channel_id=1, source_target_pairs={{0,2},{1,3},{2,0},{3,1},{4,6},{5,7},{6,4},{7,5},{8,10},{9,11},{10,... | collective-permute-start | bytes 1032200 | tf_op jit(solution)/shard_map/ppermute | solution.py:689
  27.7 4.3 %collective-permute-done.5 = f32[2,72,256]{2,1,0:T(8,128)S(1)} collective-permute-done((f32[2,72,256]{2,1,0:T(8,128)S(1)}, f32[2,72,256]{2,1,0:T(8,128)S(1)}, u32[]{:S(2)}, u32[]{:S(2)}) %collective-permute-start.5) | collective-permute-done | bytes 147488 | tf_op jit(solution)/shard_map/ppermute | solution.py:689
  33.9 2.6 %price.6.rest_1_ = f32[9,64,128]{2,1,0:T(8,128)S(1)} custom-call(s32[4,256]{1,0:T(4,128)S(1)} %get-tuple-element.75.few, s32[8,896]{1,0:T(8,128)S(1)} %get-tuple-element.76.ents, bf16[168,128,128]{2,1,0:T(8,128)(2,1)S(1)} %get-tuple-element.79.compact, bf16[1500,128,128]{2,1,0:T(8,128)(2,1)} %get-tuple-element.80.spill, ...), custom_call_target="tpu_custom_call" | custom-call | bytes 6000000 | tf_op jit(solution)/shard_map/price/pallas_call | solution.py:747
  36.6 1.8 %price.7.before = f32[9,64,128]{2,1,0:T(8,128)S(1)} custom-call(s32[4,256]{1,0:T(4,128)S(1)} %get-tuple-element.75.few, s32[8,896]{1,0:T(8,128)S(1)} %get-tuple-element.76.ents, bf16[168,128,128]{2,1,0:T(8,128)(2,1)S(1)} %get-tuple-element.79.compact, bf16[1500,128,128]{2,1,0:T(8,128)(2,1)} %get-tuple-element.80.spill, ...), custom_call_target="tpu_custom_call" | custom-call | bytes 6000000 | tf_op jit(solution)/shard_map/price/pallas_call | solution.py:755
  38.5 3.3 %step.3 = (f32[64,896]{1,0:T(8,128)S(1)}, f32[64,1]{1,0:T(8,128)S(1)}, bf16[64,2560]{1,0:T(8,128)(2,1)S(1)}, bf16[64,2560]{1,0:T(8,128)(2,1)S(1)}, bf16[64,128]{...) custom-call(s32[4,256]{1,0:T(4,128)S(1)} %get-tuple-element.75.few, s32[8,896]{1,0:T(8,128)S(1)} %get-tuple-element.76.ents, ...), custom_call_target="tpu_custom_call" | custom-call | bytes 12000000 | tf_op jit(solution)/shard_map/step/pallas_call | solution.py:758
  45.1 2.6 %collective-permute-start.9 = (f32[1,72,256]{2,1,0:T(8,128)S(1)}, f32[1,72,256]{2,1,0:T(8,128)S(1)}, u32[]{:S(2)}, u32[]{:S(2)}) collective-permute-start(f32[1,72,256]{2,1,0:T(8,128)S(1)} %bitcast.30), channel_id=1, source_target_pairs={{0,8},{4,12},{8,0},{12,4},{1,9},{5,13},{9,1},{13,5},{2,10},{6,14},... | collective-permute-start | bytes 221192 | tf_op jit(solution)/shard_map/ppermute | solution.py:689
  49.1 3.2 %collective-permute-done.9 = f32[1,72,256]{2,1,0:T(8,128)S(1)} collective-permute-done((f32[1,72,256]{2,1,0:T(8,128)S(1)}, f32[1,72,256]{2,1,0:T(8,128)S(1)}, u32[]{:S(2)}, u32[]{:S(2)}) %collective-permute-start.9) | collective-permute-done | bytes 73760 | tf_op jit(solution)/shard_map/ppermute | solution.py:689
  52.3 2.9 %collective-permute-done.11 = bf16[64,2560]{1,0:T(8,128)(2,1)S(1)} collective-permute-done((bf16[64,2560]{1,0:T(8,128)(2,1)S(1)}, bf16[64,2560]{1,0:T(8,128)(2,1)S(1)}, u32[]{:S(2)}, u32[]{:S(2)}) %collective-permute-start.11) | collective-permute-done | bytes 327712 | tf_op jit(solution)/shard_map/ppermute | solution.py:689
  57.6 4.4 %collective-permute-done.13 = f32[2,72,256]{2,1,0:T(8,128)S(1)} collective-permute-done((f32[2,72,256]{2,1,0:T(8,128)S(1)}, f32[2,72,256]{2,1,0:T(8,128)S(1)}, u32[]{:S(2)}, u32[]{:S(2)}) %collective-permute-start.13) | collective-permute-done | bytes 147488 | tf_op jit(solution)/shard_map/ppermute | solution.py:689
  63.8 2.6 %price.8.rest_1_ = f32[9,64,128]{2,1,0:T(8,128)S(1)} custom-call(s32[4,256]{1,0:T(4,128)S(1)} %get-tuple-element.75.few, s32[8,896]{1,0:T(8,128)S(1)} %get-tuple-element.76.ents, bf16[168,128,128]{2,1,0:T(8,128)(2,1)S(1)} %get-tuple-element.79.compact, bf16[1500,128,128]{2,1,0:T(8,128)(2,1)} %get-tuple-element.80.spill, ...), custom_call_target="tpu_custom_call" | custom-call | bytes 6000000 | tf_op jit(solution)/shard_map/price/pallas_call | solution.py:747
  66.5 1.8 %price.9.before = f32[9,64,128]{2,1,0:T(8,128)S(1)} custom-call(s32[4,256]{1,0:T(4,128)S(1)} %get-tuple-element.75.few, s32[8,896]{1,0:T(8,128)S(1)} %get-tuple-element.76.ents, bf16[168,128,128]{2,1,0:T(8,128)(2,1)S(1)} %get-tuple-element.79.compact, bf16[1500,128,128]{2,1,0:T(8,128)(2,1)} %get-tuple-element.80.spill, ...), custom_call_target="tpu_custom_call" | custom-call | bytes 6000000 | tf_op jit(solution)/shard_map/price/pallas_call | solution.py:755
  68.3 3.3 %step.4 = (f32[64,896]{1,0:T(8,128)S(1)}, f32[64,1]{1,0:T(8,128)S(1)}, bf16[64,2560]{1,0:T(8,128)(2,1)S(1)}, bf16[64,2560]{1,0:T(8,128)(2,1)S(1)}, bf16[64,128]{...) custom-call(s32[4,256]{1,0:T(4,128)S(1)} %get-tuple-element.75.few, s32[8,896]{1,0:T(8,128)S(1)} %get-tuple-element.76.ents, ...), custom_call_target="tpu_custom_call" | custom-call | bytes 12000000 | tf_op jit(solution)/shard_map/step/pallas_call | solution.py:758
  75.6 2.4 %collective-permute-start.17 = (f32[1,72,256]{2,1,0:T(8,128)S(1)}, f32[1,72,256]{2,1,0:T(8,128)S(1)}, u32[]{:S(2)}, u32[]{:S(2)}) collective-permute-start(f32[1,72,256]{2,1,0:T(8,128)S(1)} %bitcast.32), channel_id=1, source_target_pairs={{0,8},{4,12},{8,0},{12,4},{1,9},{5,13},{9,1},{13,5},{2,10},{6,14},... | collective-permute-start | bytes 221192 | tf_op jit(solution)/shard_map/ppermute | solution.py:689
  79.4 3.1 %collective-permute-done.17 = f32[1,72,256]{2,1,0:T(8,128)S(1)} collective-permute-done((f32[1,72,256]{2,1,0:T(8,128)S(1)}, f32[1,72,256]{2,1,0:T(8,128)S(1)}, u32[]{:S(2)}, u32[]{:S(2)}) %collective-permute-start.17) | collective-permute-done | bytes 73760 | tf_op jit(solution)/shard_map/ppermute | solution.py:689
  82.5 2.3 %collective-permute-done.19 = bf16[64,2560]{1,0:T(8,128)(2,1)S(1)} collective-permute-done((bf16[64,2560]{1,0:T(8,128)(2,1)S(1)}, bf16[64,2560]{1,0:T(8,128)(2,1)S(1)}, u32[]{:S(2)}, u32[]{:S(2)}) %collective-permute-start.19) | collective-permute-done | bytes 327712 | tf_op jit(solution)/shard_map/ppermute | solution.py:689
  88.5 4.4 %collective-permute-done.21 = f32[2,72,256]{2,1,0:T(8,128)S(1)} collective-permute-done((f32[2,72,256]{2,1,0:T(8,128)S(1)}, f32[2,72,256]{2,1,0:T(8,128)S(1)}, u32[]{:S(2)}, u32[]{:S(2)}) %collective-permute-start.21) | collective-permute-done | bytes 147488 | tf_op jit(solution)/shard_map/ppermute | solution.py:689
  94.8 2.6 %price.10.rest_1_ = f32[9,64,128]{2,1,0:T(8,128)S(1)} custom-call(s32[4,256]{1,0:T(4,128)S(1)} %get-tuple-element.75.few, s32[8,896]{1,0:T(8,128)S(1)} %get-tuple-element.76.ents, bf16[168,128,128]{2,1,0:T(8,128)(2,1)S(1)} %get-tuple-element.79.compact, bf16[1500,128,128]{2,1,0:T(8,128)(2,1)} %get-tuple-element.80.spill, ...), custom_call_target="tpu_custom_call" | custom-call | bytes 6000000 | tf_op jit(solution)/shard_map/price/pallas_call | solution.py:747
  97.5 1.8 %price.11.before = f32[9,64,128]{2,1,0:T(8,128)S(1)} custom-call(s32[4,256]{1,0:T(4,128)S(1)} %get-tuple-element.75.few, s32[8,896]{1,0:T(8,128)S(1)} %get-tuple-element.76.ents, bf16[168,128,128]{2,1,0:T(8,128)(2,1)S(1)} %get-tuple-element.79.compact, bf16[1500,128,128]{2,1,0:T(8,128)(2,1)} %get-tuple-element.80.spill, ...), custom_call_target="tpu_custom_call" | custom-call | bytes 6000000 | tf_op jit(solution)/shard_map/price/pallas_call | solution.py:755
  99.3 3.2 %step.5 = (f32[64,640]{1,0:T(8,128)}, f32[64,256]{1,0:T(8,128)}) custom-call(s32[4,256]{1,0:T(4,128)S(1)} %get-tuple-element.75.few, s32[8,896]{1,0:T(8,128)S(1)} %get-tuple-element.76.ents, bf16[168,128,128]{2,1,0:T(8,128)(2,1)S(1)} %get-tuple-element.79.compact, bf16[1500,128,128]{2,1,0:T(8,128)(2,1)} %get-tuple-element.80.spill, ...), custom_call_target="tpu_custom_call" | custom-call | bytes 12000000 | tf_op jit(solution)/shard_map/step/pallas_call | solution.py:758
  (79 shorter events, 30.9 us)
Async XLA Ops:
  11.3 2.3 %collective-permute-start = (bf16[64,2560]{1,0:T(8,128)(2,1)S(1)}, bf16[64,2560]{1,0:T(8,128)(2,1)S(1)}, u32[]{:S(2)}, u32[]{:S(2)}) collective-permute-start(bf16[64,2560]{1,0:T(8,128)(2,1)S(1)} %get-tuple-element.87), channel_id=1, source_target_pairs={{0,1},{1,0},{2,3},{3,2},{4,5},{5,4},{6,7},{7,6},{8,9},{9,8},{10,11... | collective-permute-start | bytes 983048 | tf_op jit(solution)/shard_map/ppermute | solution.py:689
  13.5 9.2 %collective-permute-start.2 = (bf16[64,2560]{1,0:T(8,128)(2,1)S(1)}, bf16[64,2560]{1,0:T(8,128)(2,1)S(1)}, u32[]{:S(2)}, u32[]{:S(2)}) collective-permute-start(bf16[64,2560]{1,0:T(8,128)(2,1)S(1)} %get-tuple-element.90), channel_id=1, source_target_pairs={{0,1},{1,0},{2,3},{3,2},{4,5},{5,4},{6,7},{7,6},{8,9},{9,8},{10,11... | collective-permute-start | bytes 983048 | tf_op jit(solution)/shard_map/ppermute | solution.py:689
  13.7 10.3 %collective-permute-start.3 = (bf16[64,2560]{1,0:T(8,128)(2,1)S(1)}, bf16[64,2560]{1,0:T(8,128)(2,1)S(1)}, u32[]{:S(2)}, u32[]{:S(2)}) collective-permute-start(bf16[64,2560]{1,0:T(8,128)(2,1)S(1)} %add_convert_fusion.2), channel_id=1, source_target_pairs={{0,2},{1,3},{2,0},{3,1},{4,6},{5,7},{6,4},{7,5},{8,10},{9,11},{10,... | collective-permute-start | bytes 983048 | tf_op jit(solution)/shard_map/ppermute | solution.py:689
  16.1 6.6 %collective-permute-start.1 = (f32[1,72,256]{2,1,0:T(8,128)S(1)}, f32[1,72,256]{2,1,0:T(8,128)S(1)}, u32[]{:S(2)}, u32[]{:S(2)}) collective-permute-start(f32[1,72,256]{2,1,0:T(8,128)S(1)} %bitcast.28), channel_id=1, source_target_pairs={{0,8},{4,12},{8,0},{12,4},{1,9},{5,13},{9,1},{13,5},{2,10},{6,14},... | collective-permute-start | bytes 221192 | tf_op jit(solution)/shard_map/ppermute | solution.py:689
  24.2 9.7 %collective-permute-start.6 = (bf16[64,2688]{1,0:T(8,128)(2,1)S(1)}, bf16[64,2688]{1,0:T(8,128)(2,1)S(1)}, u32[]{:S(2)}, u32[]{:S(2)}) collective-permute-start(bf16[64,2688]{1,0:T(8,128)(2,1)S(1)} %pad_maximum_fusion.rest_0_), channel_id=1, source_target_pairs={{0,1},{1,0},{2,3},{3,2},{4,5},{5,4},{6,7},{7,6},{8,9},{9,8},{10,11... | collective-permute-start | bytes 1032200 | tf_op jit(solution)/shard_map/ppermute | solution.py:689
  24.3 12.2 %collective-permute-start.4 = (bf16[64,2688]{1,0:T(8,128)(2,1)S(1)}, bf16[64,2688]{1,0:T(8,128)(2,1)S(1)}, u32[]{:S(2)}, u32[]{:S(2)}) collective-permute-start(bf16[64,2688]{1,0:T(8,128)(2,1)S(1)} %pad_maximum_fusion.rest_0_), channel_id=1, source_target_pairs={{0,2},{1,3},{2,0},{3,1},{4,6},{5,7},{6,4},{7,5},{8,10},{9,11},{10,... | collective-permute-start | bytes 1032200 | tf_op jit(solution)/shard_map/ppermute | solution.py:689
  26.1 5.9 %collective-permute-start.5 = (f32[2,72,256]{2,1,0:T(8,128)S(1)}, f32[2,72,256]{2,1,0:T(8,128)S(1)}, u32[]{:S(2)}, u32[]{:S(2)}) collective-permute-start(f32[2,72,256]{2,1,0:T(8,128)S(1)} %pad_maximum_fusion.3), channel_id=1, source_target_pairs={{0,4},{4,0},{8,12},{12,8},{1,5},{5,1},{9,13},{13,9},{2,6},{6,2},{1... | collective-permute-start | bytes 442376 | tf_op jit(solution)/shard_map/ppermute | solution.py:689
  36.5 1.9 %collective-permute-start.7 = (bf16[64,2688]{1,0:T(8,128)(2,1)S(1)}, bf16[64,2688]{1,0:T(8,128)(2,1)S(1)}, u32[]{:S(2)}, u32[]{:S(2)}) collective-permute-start(bf16[64,2688]{1,0:T(8,128)(2,1)S(1)} %collective-permute-done.4.rest_0_), channel_id=1, source_target_pairs={{0,1},{1,0},{2,3},{3,2},{4,5},{5,4},{6,7},{7,6},{8,9},{9,8},{10,11... | collective-permute-start | bytes 1032200 | tf_op jit(solution)/shard_map/ppermute | solution.py:689
  41.8 3.1 %collective-permute-start.8 = (bf16[64,2560]{1,0:T(8,128)(2,1)S(1)}, bf16[64,2560]{1,0:T(8,128)(2,1)S(1)}, u32[]{:S(2)}, u32[]{:S(2)}) collective-permute-start(bf16[64,2560]{1,0:T(8,128)(2,1)S(1)} %get-tuple-element.108), channel_id=1, source_target_pairs={{0,1},{1,0},{2,3},{3,2},{4,5},{5,4},{6,7},{7,6},{8,9},{9,8},{10,11... | collective-permute-start | bytes 983048 | tf_op jit(solution)/shard_map/ppermute | solution.py:689
  44.8 7.5 %collective-permute-start.10 = (bf16[64,2560]{1,0:T(8,128)(2,1)S(1)}, bf16[64,2560]{1,0:T(8,128)(2,1)S(1)}, u32[]{:S(2)}, u32[]{:S(2)}) collective-permute-start(bf16[64,2560]{1,0:T(8,128)(2,1)S(1)} %get-tuple-element.111), channel_id=1, source_target_pairs={{0,1},{1,0},{2,3},{3,2},{4,5},{5,4},{6,7},{7,6},{8,9},{9,8},{10,11... | collective-permute-start | bytes 983048 | tf_op jit(solution)/shard_map/ppermute | solution.py:689
  45.0 10.2 %collective-permute-start.11 = (bf16[64,2560]{1,0:T(8,128)(2,1)S(1)}, bf16[64,2560]{1,0:T(8,128)(2,1)S(1)}, u32[]{:S(2)}, u32[]{:S(2)}) collective-permute-start(bf16[64,2560]{1,0:T(8,128)(2,1)S(1)} %add_convert_fusion.1), channel_id=1, source_target_pairs={{0,2},{1,3},{2,0},{3,1},{4,6},{5,7},{6,4},{7,5},{8,10},{9,11},{10,... | collective-permute-start | bytes 983048 | tf_op jit(solution)/shard_map/ppermute | solution.py:689
  45.1 7.2 %collective-permute-start.9 = (f32[1,72,256]{2,1,0:T(8,128)S(1)}, f32[1,72,256]{2,1,0:T(8,128)S(1)}, u32[]{:S(2)}, u32[]{:S(2)}) collective-permute-start(f32[1,72,256]{2,1,0:T(8,128)S(1)} %bitcast.30), channel_id=1, source_target_pairs={{0,8},{4,12},{8,0},{12,4},{1,9},{5,13},{9,1},{13,5},{2,10},{6,14},... | collective-permute-start | bytes 221192 | tf_op jit(solution)/shard_map/ppermute | solution.py:689
  55.6 8.2 %collective-permute-start.14 = (bf16[64,2688]{1,0:T(8,128)(2,1)S(1)}, bf16[64,2688]{1,0:T(8,128)(2,1)S(1)}, u32[]{:S(2)}, u32[]{:S(2)}) collective-permute-start(bf16[64,2688]{1,0:T(8,128)(2,1)S(1)} %pad_maximum_fusion.1.rest_0_), channel_id=1, source_target_pairs={{0,1},{1,0},{2,3},{3,2},{4,5},{5,4},{6,7},{7,6},{8,9},{9,8},{10,11... | collective-permute-start | bytes 1032200 | tf_op jit(solution)/shard_map/ppermute | solution.py:689
  55.7 10.7 %collective-permute-start.12 = (bf16[64,2688]{1,0:T(8,128)(2,1)S(1)}, bf16[64,2688]{1,0:T(8,128)(2,1)S(1)}, u32[]{:S(2)}, u32[]{:S(2)}) collective-permute-start(bf16[64,2688]{1,0:T(8,128)(2,1)S(1)} %pad_maximum_fusion.1.rest_0_), channel_id=1, source_target_pairs={{0,2},{1,3},{2,0},{3,1},{4,6},{5,7},{6,4},{7,5},{8,10},{9,11},{10,... | collective-permute-start | bytes 1032200 | tf_op jit(solution)/shard_map/ppermute | solution.py:689
  56.1 5.9 %collective-permute-start.13 = (f32[2,72,256]{2,1,0:T(8,128)S(1)}, f32[2,72,256]{2,1,0:T(8,128)S(1)}, u32[]{:S(2)}, u32[]{:S(2)}) collective-permute-start(f32[2,72,256]{2,1,0:T(8,128)S(1)} %pad_maximum_fusion.4), channel_id=1, source_target_pairs={{0,4},{4,0},{8,12},{12,8},{1,5},{5,1},{9,13},{13,9},{2,6},{6,2},{1... | collective-permute-start | bytes 442376 | tf_op jit(solution)/shard_map/ppermute | solution.py:689
  66.4 1.9 %collective-permute-start.15 = (bf16[64,2688]{1,0:T(8,128)(2,1)S(1)}, bf16[64,2688]{1,0:T(8,128)(2,1)S(1)}, u32[]{:S(2)}, u32[]{:S(2)}) collective-permute-start(bf16[64,2688]{1,0:T(8,128)(2,1)S(1)} %collective-permute-done.12.rest_0_), channel_id=1, source_target_pairs={{0,1},{1,0},{2,3},{3,2},{4,5},{5,4},{6,7},{7,6},{8,9},{9,8},{10,11... | collective-permute-start | bytes 1032200 | tf_op jit(solution)/shard_map/ppermute | solution.py:689
  71.7 2.9 %collective-permute-start.16 = (bf16[64,2560]{1,0:T(8,128)(2,1)S(1)}, bf16[64,2560]{1,0:T(8,128)(2,1)S(1)}, u32[]{:S(2)}, u32[]{:S(2)}) collective-permute-start(bf16[64,2560]{1,0:T(8,128)(2,1)S(1)} %get-tuple-element.128), channel_id=1, source_target_pairs={{0,1},{1,0},{2,3},{3,2},{4,5},{5,4},{6,7},{7,6},{8,9},{9,8},{10,11... | collective-permute-start | bytes 983048 | tf_op jit(solution)/shard_map/ppermute | solution.py:689
  74.5 8.0 %collective-permute-start.18 = (bf16[64,2560]{1,0:T(8,128)(2,1)S(1)}, bf16[64,2560]{1,0:T(8,128)(2,1)S(1)}, u32[]{:S(2)}, u32[]{:S(2)}) collective-permute-start(bf16[64,2560]{1,0:T(8,128)(2,1)S(1)} %get-tuple-element.131), channel_id=1, source_target_pairs={{0,1},{1,0},{2,3},{3,2},{4,5},{5,4},{6,7},{7,6},{8,9},{9,8},{10,11... | collective-permute-start | bytes 983048 | tf_op jit(solution)/shard_map/ppermute | solution.py:689
  74.7 10.2 %collective-permute-start.19 = (bf16[64,2560]{1,0:T(8,128)(2,1)S(1)}, bf16[64,2560]{1,0:T(8,128)(2,1)S(1)}, u32[]{:S(2)}, u32[]{:S(2)}) collective-permute-start(bf16[64,2560]{1,0:T(8,128)(2,1)S(1)} %add_convert_fusion), channel_id=1, source_target_pairs={{0,2},{1,3},{2,0},{3,1},{4,6},{5,7},{6,4},{7,5},{8,10},{9,11},{10,... | collective-permute-start | bytes 983048 | tf_op jit(solution)/shard_map/ppermute | solution.py:689
  75.6 6.9 %collective-permute-start.17 = (f32[1,72,256]{2,1,0:T(8,128)S(1)}, f32[1,72,256]{2,1,0:T(8,128)S(1)}, u32[]{:S(2)}, u32[]{:S(2)}) collective-permute-start(f32[1,72,256]{2,1,0:T(8,128)S(1)} %bitcast.32), channel_id=1, source_target_pairs={{0,8},{4,12},{8,0},{12,4},{1,9},{5,13},{9,1},{13,5},{2,10},{6,14},... | collective-permute-start | bytes 221192 | tf_op jit(solution)/shard_map/ppermute | solution.py:689
  86.0 8.8 %collective-permute-start.22 = (bf16[64,2688]{1,0:T(8,128)(2,1)S(1)}, bf16[64,2688]{1,0:T(8,128)(2,1)S(1)}, u32[]{:S(2)}, u32[]{:S(2)}) collective-permute-start(bf16[64,2688]{1,0:T(8,128)(2,1)S(1)} %pad_maximum_fusion.2.rest_0_), channel_id=1, source_target_pairs={{0,1},{1,0},{2,3},{3,2},{4,5},{5,4},{6,7},{7,6},{8,9},{9,8},{10,11... | collective-permute-start | bytes 1032200 | tf_op jit(solution)/shard_map/ppermute | solution.py:689
  86.0 11.3 %collective-permute-start.20 = (bf16[64,2688]{1,0:T(8,128)(2,1)S(1)}, bf16[64,2688]{1,0:T(8,128)(2,1)S(1)}, u32[]{:S(2)}, u32[]{:S(2)}) collective-permute-start(bf16[64,2688]{1,0:T(8,128)(2,1)S(1)} %pad_maximum_fusion.2.rest_0_), channel_id=1, source_target_pairs={{0,2},{1,3},{2,0},{3,1},{4,6},{5,7},{6,4},{7,5},{8,10},{9,11},{10,... | collective-permute-start | bytes 1032200 | tf_op jit(solution)/shard_map/ppermute | solution.py:689
  87.0 5.9 %collective-permute-start.21 = (f32[2,72,256]{2,1,0:T(8,128)S(1)}, f32[2,72,256]{2,1,0:T(8,128)S(1)}, u32[]{:S(2)}, u32[]{:S(2)}) collective-permute-start(f32[2,72,256]{2,1,0:T(8,128)S(1)} %pad_maximum_fusion.5), channel_id=1, source_target_pairs={{0,4},{4,0},{8,12},{12,8},{1,5},{5,1},{9,13},{13,9},{2,6},{6,2},{1... | collective-permute-start | bytes 442376 | tf_op jit(solution)/shard_map/ppermute | solution.py:689
  97.4 1.9 %collective-permute-start.23 = (bf16[64,2688]{1,0:T(8,128)(2,1)S(1)}, bf16[64,2688]{1,0:T(8,128)(2,1)S(1)}, u32[]{:S(2)}, u32[]{:S(2)}) collective-permute-start(bf16[64,2688]{1,0:T(8,128)(2,1)S(1)} %collective-permute-done.20.rest_0_), channel_id=1, source_target_pairs={{0,1},{1,0},{2,3},{3,2},{4,5},{5,4},{6,7},{7,6},{8,9},{9,8},{10,11... | collective-permute-start | bytes 1032200 | tf_op jit(solution)/shard_map/ppermute | solution.py:689
  (4 other events, 8.7 us)

commit v3 on v2

--- a/solution.py
+++ b/solution.py
@@ -11,7 +11,8 @@
 TAU = 0.5
 SIGMA = 0.5
 LANE = 128
-LARGE, SMALL = 32, 8
+GROUPS = (64, 32, 8)
+LARGE, SMALL = GROUPS[0], GROUPS[-1]
 KEPT = 160
 F32 = jnp.float32
 BF16 = jnp.bfloat16
@@ -105,7 +106,10 @@
     chunk = jnp.zeros_like(row)
     for d in range(1, chunks):
         chunk = chunk + (row >= d * quarter_tiles).astype(jnp.int32)
-    relative = (((chunk ^ mine[...]) - chunk) * quarter_tiles + row).astype(F32)
+    relative = chunk ^ mine[...]
+    half = chunks // 2
+    slot = 2 * (relative & (half - 1)) + (relative >= half).astype(jnp.int32)
+    relative = ((slot - chunk) * quarter_tiles + row).astype(F32)
     number = lane[:1]
     tile_key = jnp.where(number < kt, relative, float(chunks * quarter_tiles)) * LANE + number
     rank = over_sub(column(tile_key) < tile_key, 1.0)
@@ -136,23 +140,24 @@
 
 def sweep(lo, hi, body):
     hi = jnp.maximum(lo, hi)
-    long = (hi - lo) // LARGE
-
-    def group(n, _):
-        for u in range(LARGE):
-            body(lo + n * LARGE + u, None)
-        return 0
-
-    lax.fori_loop(0, long, group, 0)
-    rest = lo + long * LARGE
+    for size in GROUPS[:-1]:
+
+        def group(n, _, size=size, lo=lo):
+            for u in range(size):
+                body(lo + n * size + u, None)
+            return 0
+
+        count = (hi - lo) // size
+        lax.fori_loop(0, count, group, 0)
+        lo = lo + count * size
 
     def short(n, _):
         for u in range(SMALL):
-            e = rest + n * SMALL + u
+            e = lo + n * SMALL + u
             body(e, e < hi)
         return 0
 
-    lax.fori_loop(0, (hi - rest + SMALL - 1) // SMALL, short, 0)
+    lax.fori_loop(0, (hi - lo + SMALL - 1) // SMALL, short, 0)
 
 
 class Lists:
@@ -244,40 +249,42 @@
 
 
 def start_flows(base, total, quarter_tiles, first, last):
-    origin, width = first * quarter_tiles, (last - first) * quarter_tiles
-    total[:, : width * LANE] = base[:, origin * LANE : (origin + width) * LANE]
-
-
-def add_flows(lists, picked, total, quarter_tiles, first, last, outs):
-    origin, spare, blocks = first * quarter_tiles, (last - first) * quarter_tiles, picked.shape[0] - 1
+    width = 2 * quarter_tiles * LANE
+    total[:, : (last - first) * width] = base[:, first * width : last * width]
+
+
+def add_flows(lists, picked, total, balance, quarter_tiles, first, last, outs):
+    width = quarter_tiles * LANE
+    origin, spare = 2 * first * quarter_tiles, 2 * (last - first) * quarter_tiles
+    blocks = picked.shape[0] - 1
 
     def entry(row, m, live, matrix):
         row, m = pick(live, row - origin, spare), pick(live, m, blocks)
         total[:, lanes(row)] += mxu(picked[m], matrix[...], NN)
 
-    lists.sweep(first, last, entry)
-    for d in range(last - first):
-        at = d * quarter_tiles
-        outs[d][...] = total[:, at * LANE : (at + quarter_tiles) * LANE].astype(BF16)
+    lists.sweep(2 * first, 2 * last, entry)
+    for d, out in enumerate(outs):
+        at = 2 * d * width
+        out[:, :width] = total[:, at : at + width].astype(BF16)
+        out[:, width : width + LANE] = balance
+        out[:, width + LANE :] = total[:, at + width : at + 2 * width].astype(BF16)
 
 
 def start_prices(bars, lines, quarter_tiles):
     width = quarter_tiles * LANE
     for d, bar in enumerate(bars):
-        lines[:, d * width : (d + 1) * width] = bar[:, :width]
-
-
-def add_prices(lists, bars, lines, total, quarter_tiles, first, last):
-    origin, width = first * quarter_tiles, quarter_tiles * LANE
-    spare, blocks = (last - first) * quarter_tiles, total.shape[0] - 2
+        lines[:, d * width : (d + 1) * width] = bar[...]
+
+
+def add_prices(lists, lines, total, quarter_tiles, first, last):
+    origin = first * quarter_tiles
+    spare, blocks = (last - first) * quarter_tiles, total.shape[0] - 1
 
     def entry(row, m, live, matrix):
         row, m = pick(live, row - origin, spare), pick(live, m, blocks)
         total[m] += mxu(lines[:, lanes(row)], matrix[...], NT)
 
     lists.sweep(first, last, entry)
-    for bar in bars:
-        total[blocks + 1] += bar[:, width:].astype(F32)
 
 
 def put_picked(z, picked):
@@ -297,25 +304,24 @@
             sent[hours + i * each + j : hours + i * each + j + 1, : piece.shape[1]] = piece
 
 
-def own_balance(z, load_sum, balance):
+def own_balance(z, load_sum, mine):
     value = jnp.sum(z, axis=1, keepdims=True) - load_sum[...]
-    lane = lax.broadcasted_iota(jnp.int32, balance.shape, 1)
+    lane = lax.broadcasted_iota(jnp.int32, (z.shape[0], LANE), 1) - 3 * mine[...]
     high = value.astype(BF16).astype(F32)
     middle = (value - high).astype(BF16).astype(F32)
     low = value - high - middle
-    balance[...] = jnp.where(
+    return jnp.where(
         lane == 0, high, jnp.where(lane == 1, middle, jnp.where(lane == 2, low, 0.0))
     ).astype(BF16)
 
 
 def first_kernel(
     chunks, quarter_tiles,
-    few, ents, pars, sorted_bus, load, tiles, place, generation, charging,
+    few, ents, pars, sorted_bus, load, tiles, place, generation, charging, mine,
     compact, spill, base, load_sum, state, rows, *rest,
 ):
-    upper = chunks - chunks // 2
-    outs = rest[:upper]
-    balance, picked, few_held, ents_held, stage, sems, total = rest[upper:]
+    outs, rest = rest[: chunks // 2 - 1], rest[chunks // 2 - 1 :]
+    balance, picked, few_held, ents_held, stage, sems, total = rest
     copy = pltpu.make_async_copy(ents, ents_held, sems.at[2])
     copy.start()
     lists = Lists(few, ents, compact, spill, few_held, ents_held, stage, sems)
@@ -336,30 +342,28 @@
     copy.wait()
     found = ents_held[START, chunks]
     build(ents_held, sorted_bus, load, tiles, compact, spill, base, load_sum, stage, sems.at[1], found)
-    own_balance(z, load_sum, balance)
     lists.ready(chunks)
-    start_flows(base, total, quarter_tiles, chunks // 2, chunks)
-    add_flows(lists, picked, total, quarter_tiles, chunks // 2, chunks, outs)
+    start_flows(base, total, quarter_tiles, 1, chunks // 2)
+    balance[...] = own_balance(z, load_sum, mine)
+    add_flows(lists, picked, total, balance[...], quarter_tiles, 1, chunks // 2, outs)
 
 
 def lower_kernel(
-    chunks, quarter_tiles, first, last,
-    few, ents, compact, spill, base, picked, state, back,
-    *rest,
+    chunks, quarter_tiles,
+    few, ents, compact, spill, base, picked, balance,
+    out, few_held, ents_held, stage, sems, total,
 ):
-    outs, rest = rest[: last - first], rest[last - first :]
-    if first:
-        sent, rest = rest[0], rest[1:]
-    few_held, ents_held, stage, sems, total = rest
     lists = Lists(few, ents, compact, spill, few_held, ents_held, stage, sems)
-    start_flows(base, total, quarter_tiles, first, last)
-    if first:
-        z = state[...]
-        stores = sent.shape[1]
-        own = -joined(mxu(split(z), back[:, z.shape[1] - stores :], NN))
-        send_hours(z, own, sent)
+    start_flows(base, total, quarter_tiles, 0, 1)
     lists.ready(chunks)
-    add_flows(lists, picked, total, quarter_tiles, first, last, outs)
+    add_flows(lists, picked, total, balance[...], quarter_tiles, 0, 1, [out])
+
+
+def hours_kernel(state, back, sent):
+    z = state[...]
+    stores = sent.shape[1]
+    own = -joined(mxu(split(z), back[:, z.shape[1] - stores :], NN))
+    send_hours(z, own, sent)
 
 
 def price_kernel(
@@ -374,33 +378,33 @@
     total[...] = jnp.zeros_like(total) if fresh else before[...]
     start_prices(bars, lines, quarter_tiles)
     lists.ready(chunks)
-    add_prices(lists, bars, lines, total, quarter_tiles, first, last)
+    add_prices(lists, lines, total, quarter_tiles, first, last)
 
 
 def step_kernel(
     chunks, quarter_tiles, balance_step, final,
-    few, ents, compact, spill, before, state, fixed, balance_dual, rows, base, load_sum, back,
-    *rest,
+    few, ents, compact, spill, before, state, fixed, balance_dual, balances, rows, base, load_sum,
+    back, mine, *rest,
 ):
-    start, upper = chunks - chunks // 4, chunks // 2
+    start = 2
     bars, rest = rest[: chunks - start], rest[chunks - start :]
     if final:
         next_g, next_p, few_held, ents_held, stage, sems, lines, prices = rest
     else:
         next_state, next_balance, *rest = rest
-        outs, rest = rest[: chunks - upper], rest[chunks - upper :]
+        outs, rest = rest[: chunks // 2 - 1], rest[chunks // 2 - 1 :]
         balance, picked, few_held, ents_held, stage, sems, lines, prices, total = rest
     lists = Lists(few, ents, compact, spill, few_held, ents_held, stage, sems)
     prices[...] = before[...]
     start_prices(bars, lines, quarter_tiles)
     if not final:
-        start_flows(base, total, quarter_tiles, upper, chunks)
+        start_flows(base, total, quarter_tiles, 1, chunks // 2)
     lists.ready(chunks)
-    add_prices(lists, bars, lines, prices, quarter_tiles, start, chunks)
-    blocks = prices.shape[0] - 2
+    add_prices(lists, lines, prices, quarter_tiles, start, chunks)
+    blocks = prices.shape[0] - 1
     price = jnp.concatenate([prices[m] for m in range(blocks)], axis=1)
     old = balance_dual[...]
-    new = old + balance_step * jnp.sum(prices[blocks + 1], axis=1, keepdims=True)
+    new = old + balance_step * jnp.sum(balances[...], axis=1, keepdims=True)
     bb = 2.0 * new - old
     high = rows[HIGH : HIGH + 1]
     z = state[...] - TAU * (bb + price + fixed[...])
@@ -413,9 +417,9 @@
     else:
         next_state[...] = z
         next_balance[...] = new
-        own_balance(z, load_sum, balance)
         put_picked(z, picked)
-        add_flows(lists, picked, total, quarter_tiles, upper, chunks, outs)
+        balance[...] = own_balance(z, load_sum, mine)
+        add_flows(lists, picked, total, balance[...], quarter_tiles, 1, chunks // 2, outs)
 
 
 def hourly_kernel(
@@ -529,7 +533,6 @@
     def like(*shape, dtype=F32):
         return jax.ShapeDtypeStruct(shape, dtype)
 
-
     def placed(count, *parts):
         total = 0
         for row, at, x in parts:
@@ -552,8 +555,12 @@
 
     width = -(-(cap + SMALL) // LANE) * LANE
     where = lax.axis_index("tm").astype(jnp.int32).reshape(1)
-    from_line = mine.astype(jnp.uint32) * lines
-    whole, where, from_line = lax.optimization_barrier((whole, where, from_line))
+    near_line = mine.astype(jnp.uint32) * lines
+    far_line = (mine ^ (chunks // 2)).astype(jnp.uint32) * lines
+    whole, where, near_line, far_line = lax.optimization_barrier(
+        (whole, where, near_line, far_line)
+    )
+    mine_row = jnp.broadcast_to(mine.astype(jnp.int32), (1, LANE))
     place, back, sorted_bus, ents, few = pl.pallas_call(
         functools.partial(plan_kernel, chunks, quarter_tiles, kt),
         out_shape=(
@@ -568,9 +575,11 @@
         compiler_params=params(STEP_MIB),
         name="plan",
         cost_estimate=cost(3, 3 * 10**9),
-    )(jnp.broadcast_to(mine.astype(jnp.int32), (1, LANE)), whole)
-
-    chunk_out = (like(hours, lines, dtype=BF16),) * (chunks // 2)
+    )(mine_row, whole)
+
+    pair_out = (like(hours, 2 * lines + LANE, dtype=BF16),)
+    step_out = pair_out * (chunks // 2 - 1)
+    step_out += (like(hours, LANE, dtype=BF16), like(blocks + 1, hours, LANE, dtype=BF16))
     staging = [
         pltpu.SMEM((4, FEW), jnp.int32),
         pltpu.SMEM((8, width), jnp.int32),
@@ -578,15 +587,14 @@
         pltpu.SemaphoreType.DMA((3,)),
     ]
     lists = [vmem(), vmem(), vmem(), hbm()]
-    picked_shape = like(blocks + 1, hours, LANE, dtype=BF16)
-
-    def flow_scratch(count):
-        return [pltpu.VMEM((hours, (count * quarter_tiles + 1) * LANE), F32)]
+
+    def flow_scratch(pairs):
+        return [pltpu.VMEM((hours, (2 * pairs * quarter_tiles + 1) * LANE), F32)]
 
     def line_scratch(count):
         return pltpu.VMEM((hours, (count * quarter_tiles + 1) * LANE), BF16)
 
-    price_shape = (blocks + 2, hours, LANE)
+    price_shape = (blocks + 1, hours, LANE)
     first_call = pl.pallas_call(
         functools.partial(first_kernel, chunks, quarter_tiles),
         out_shape=(
@@ -597,33 +605,34 @@
             like(hours, units),
             like(8, units),
         )
-        + chunk_out
-        + (like(hours, LANE, dtype=BF16), picked_shape),
-        in_specs=[vmem()] * 9,
-        out_specs=(vmem(), hbm()) + (vmem(),) * (chunks // 2 + 6),
-        scratch_shapes=staging + flow_scratch(chunks // 2),
+        + step_out,
+        in_specs=[vmem()] * 10,
+        out_specs=(vmem(), hbm()) + (vmem(),) * (len(step_out) + 4),
+        scratch_shapes=staging + flow_scratch(chunks // 2 - 1),
         compiler_params=params(STEP_MIB),
         name="first",
         cost_estimate=cost(9),
     )
 
-    def lower_call(first, last):
-        return pl.pallas_call(
-            functools.partial(lower_kernel, chunks, quarter_tiles, first, last),
-            out_shape=(like(hours, lines, dtype=BF16),) * (last - first)
-            + ((like(sent_rows, stores),) if first else ()),
-            in_specs=lists + [vmem()] * 4,
-            out_specs=(vmem(),) * (last - first + (first > 0)),
-            scratch_shapes=staging + flow_scratch(last - first),
-            compiler_params=params(STEP_MIB),
-            name="lower",
-            cost_estimate=cost(2),
-        )
-
-    def line_scratch(count):
-        return pltpu.VMEM((hours, (count * quarter_tiles + 1) * LANE), BF16)
-
-    price_shape = (blocks + 2, hours, LANE)
+    lower_call = pl.pallas_call(
+        functools.partial(lower_kernel, chunks, quarter_tiles),
+        out_shape=pair_out[0],
+        in_specs=lists + [vmem()] * 3,
+        out_specs=vmem(),
+        scratch_shapes=staging + flow_scratch(1),
+        compiler_params=params(STEP_MIB),
+        name="lower",
+        cost_estimate=cost(2),
+    )
+    hours_call = pl.pallas_call(
+        hours_kernel,
+        out_shape=like(sent_rows, stores),
+        in_specs=[vmem()] * 2,
+        out_specs=vmem(),
+        compiler_params=params(STEP_MIB),
+        name="hours",
+        cost_estimate=cost(1),
+    )
 
     def price_call(first, last, fresh):
         return pl.pallas_call(
@@ -637,20 +646,19 @@
             cost_estimate=cost(2),
         )
 
-    tail = chunks - chunks // 4
+    tail = 2
 
     def step_call(final):
         scratch = staging + [line_scratch(chunks - tail), pltpu.VMEM(price_shape, F32)]
         if final:
             shape = (like(hours, gens), like(hours, stores))
         else:
-            shape = (like(hours, units), like(hours, 1)) + chunk_out
-            shape += (like(hours, LANE, dtype=BF16), picked_shape)
-            scratch += flow_scratch(chunks // 2)
+            shape = (like(hours, units), like(hours, 1)) + step_out
+            scratch += flow_scratch(chunks // 2 - 1)
         return pl.pallas_call(
             functools.partial(step_kernel, chunks, quarter_tiles, balance_step, final),
             out_shape=shape,
-            in_specs=lists + [vmem()] * (8 + chunks - tail),
+            in_specs=lists + [vmem()] * (10 + chunks - tail),
             out_specs=(vmem(),) * len(shape),
             scratch_shapes=scratch,
             compiler_params=params(STEP_MIB),
@@ -694,75 +702,61 @@
         return stacked
 
     bits = [1 << b for b in range(chunks.bit_length() - 1)]
-    line_dual = jnp.zeros((hours, lines), F32)
+    near_dual = jnp.zeros((hours, lines), F32)
+    far_dual = jnp.zeros((hours, lines), F32)
     ramp_dual = jnp.zeros((hours + 8, units), F32)
     state_dual = jnp.zeros((groups, 8, stores), F32)
     balance_dual = jnp.zeros((hours, 1), F32)
-    compact, spill, base, load_sum, state, unit_rows, *upper, balance, picked = first_call(
-        few, ents, pars, sorted_bus, load, ptdf_tiles, place, gen_start, charge_start
+    compact, spill, base, load_sum, state, unit_rows, *made = first_call(
+        few, ents, pars, sorted_bus, load, ptdf_tiles, place, gen_start, charge_start, mine_row
     )
     held = (few, ents, compact, spill)
     half_way = chunks // 2
 
-    def reduce(parts):
+    def renew(dual, flows, from_line):
+        limits = SIGMA * lax.dynamic_slice(flow_limit, (from_line,), (lines,))
+        shift = dual + SIGMA * flows
+        after = shift - jnp.clip(shift, -limits, limits)
+        return after, (2.0 * after - dual).astype(BF16)
+
+    for iteration in range(ITERS):
+        final = iteration == ITERS - 1
+        *made, balance, picked = made
+        made = [lower_call(*held, base, picked, balance), *made]
+        sums = [x.astype(F32) for x in made]
         for bit in bits[:-1]:
-            for d in sorted(parts, reverse=True):
+            for d in range(half_way):
                 if d & bit and not d & (bit - 1):
-                    got = swap(sum(x.astype(F32) for x in parts[d]).astype(BF16), bit)
-                    parts[d ^ bit].append(got)
-
-    for iteration in range(ITERS):
-        parts = {d: [x] for d, x in zip(range(half_way, chunks), upper)}
-        reduce(parts)
-        ready = sum(x.astype(F32) for x in parts[half_way]).astype(BF16)
-        across = swap(ready, half_way)
-        parts = {d: [] for d in range(half_way)}
-        *made, sent = lower_call(1, half_way)(*held, base, picked, state, back)
-        for d, x in zip(range(1, half_way), made):
-            parts[d].append(x)
-        sent, picked, *_ = lax.optimization_barrier((sent, picked, ready))
-        parts[0].append(lower_call(0, 1)(*held, base, picked, state, back)[0])
-        reduce(parts)
-        heard = hear(sent[None], spans[:1])
-        limits = SIGMA * lax.dynamic_slice(flow_limit, (from_line,), (lines,))
-        shift = line_dual + SIGMA * sum(x.astype(F32) for x in parts[0] + [across])
-        after = shift - jnp.clip(shift, -limits, limits)
-        bar = (2.0 * after - line_dual).astype(BF16)
-        line_dual = after
-        have = {0: jnp.concatenate([bar, balance], axis=1)}
-        heard, have[0] = lax.optimization_barrier((heard, have[0]))
-        have[half_way] = swap(have[0], half_way)
-        near = [0]
-        for bit in reversed(bits[:-1]):
-            for d in list(near):
-                have[d | bit] = swap(have[d], bit)
-                near.append(d | bit)
-        final = iteration == ITERS - 1
-        heard = hear(heard, spans[1:])
+                    sums[d ^ bit] = sums[d ^ bit] + swap(sums[d].astype(BF16), bit).astype(F32)
+        ready = sums[0].astype(BF16)
+        got = swap(ready, half_way)
+        state, ready = lax.optimization_barrier((state, ready))
+        heard = hear(hours_call(state, back)[None], spans)
         fixed, *duals = hourly_call(final)(
             where, state, unit_rows, pars, place, ramp_dual, state_dual,
             *[heard[j] for j in range(years)],
         )
-        have[0], fixed = lax.optimization_barrier((have[0], fixed))
-        prices = price_call(0, half_way, True)(*held, *[have[d] for d in range(half_way)])
-        have[half_way], prices, fixed = lax.optimization_barrier((have[half_way], prices, fixed))
-        far = [half_way]
+        got, fixed = lax.optimization_barrier((got, fixed))
+        ours, theirs = ready.astype(F32), got.astype(F32)
+        balances = ours[:, lines : lines + LANE] + theirs[:, lines : lines + LANE]
+        near_dual, near = renew(
+            near_dual, ours[:, :lines] + theirs[:, lines + LANE :], near_line
+        )
+        far_dual, far = renew(far_dual, ours[:, lines + LANE :] + theirs[:, :lines], far_line)
+        have = {0: (near, far)}
         for bit in reversed(bits[:-1]):
-            for d in list(far):
-                have[d | bit] = swap(have[d], bit)
-                far.append(d | bit)
-        if tail > half_way:
-            prices = price_call(half_way, tail, False)(
-                *held, *[have[d] for d in range(half_way, tail)], prices
-            )
+            for d in list(have):
+                have[d | bit] = tuple(swap(x, bit) for x in have[d])
+        bars = [x for d in range(half_way) for x in have[d]]
+        prices = price_call(0, tail, True)(*held, *bars[:tail])
         made = step_call(final)(
-            *held, prices, state, fixed, balance_dual, unit_rows, base, load_sum, back,
-            *[have[d] for d in range(tail, chunks)],
+            *held, prices, state, fixed, balance_dual, balances, unit_rows, base, load_sum, back,
+            mine_row, *bars[tail:],
         )
         if not final:
             ramp_dual, state_dual = duals
-            state, balance_dual, *upper, balance, picked = made
-    return *made, line_dual
+            state, balance_dual, *made = made
+    return *made, near_dual
 
 
 STEP_MIB = 16

time: 103 us -> 96.8 us (0.940)
  starting transfers between devices: 22.5 us -> 16 us
  waiting for transfers between devices: 27.8 us -> 32.2 us
  Pallas kernels: 46.3 us -> 42.5 us
    pallas_call x12 -> x9, Pallas kernels: 22.1 us -> 15 us  [the longest x3 8.55 us: shards(): prices = price_call(0, tail, True)(*held, *bars[:tail])]
    ppermute x24 -> x18, starting transfers between devices: 22.5 us -> 16 us  [swap(): return lax.ppermute(x, axis, [(i, i ^ bit) for i in range(size)])]
    ppermute x24 -> x18, waiting for transfers between devices: 27.8 us -> 32.2 us  [swap(): return lax.ppermute(x, axis, [(i, i ^ bit) for i in range(size)])]
    pallas_call x3, Pallas kernels: 9.85 us -> 13.1 us  [shards(): step_call(final)]
    convert_element_type x6 -> x12, other arithmetic: 2.04 us -> 3.35 us  [the longest x3 2.32 us: renew(): return (after, (2.0 * after - dual).astype(BF16))]
  transfers between devices with their start and end apart: 24 -> 18, of which waited for: 9 -> 12; matrix products, arithmetic and copies ran while one was open for 1% -> 0% of each run, Pallas kernels for 27% -> 21%
where the time goes in v3:
time: 96.8 us; the launch traced here: 97.1 us
  Pallas kernels  42.5 us (44%)
  waiting for transfers between devices  32.2 us (33%)
  starting transfers between devices  16 us (17%)
  other arithmetic  5.01 us (5%)
  between operations  1.21 us (1%)
    ppermute x18, waiting for transfers between devices, swap(): return lax.ppermute(x, axis, [(i, i ^ bit) for i in range(size)])  32.2 us
    ppermute x18, starting transfers between devices, swap(): return lax.ppermute(x, axis, [(i, i ^ bit) for i in range(size)])  16 us
    pallas_call x3, Pallas kernels, shards(): step_call(final)  13.1 us
    pallas_call x3, Pallas kernels, shards(): prices = price_call(0, tail, True)(*held, *bars[:tail])  8.55 us
    pallas_call x1, Pallas kernels, shards(): first_call(few, ents, pars, sorted_bus, load, ptdf_tiles, place, gen_star...  6.84 us
    pallas_call x3, Pallas kernels, shards(): made = [lower_call(*held, base, picked, balance), *made]  5.66 us
    pallas_call x3, Pallas kernels, shards(): hourly_call(final)  5.39 us
    convert_element_type x3, other arithmetic, renew(): return (after, (2.0 * after - dual).astype(BF16))  2.32 us
  transfers between devices with their start and end apart: 18, of which 12 were waited for; matrix products, arithmetic and copies ran while one was open for 0% of the time, Pallas kernels for 21%

profile of v3, /device:TPU:0, one launch (start us, length us, event | category | flops | bytes accessed | tf_op | source)
XLA Modules:
  0.0 97.1 jit_solution(13727976581545516413)
XLA Ops:
  2.3 2.1 %plan.1 = (bf16[896,896]{1,0:T(8,128)(2,1)S(1)}, bf16[896,896]{1,0:T(8,128)(2,1)S(1)}, f32[7,128,128]{2,1,0:T(8,128)S(1)}, s32[8,896]{1,0:T(8,128)S(1)}, s32[4,256]{1,0:T(4,128)S(1)}) custom-call(s32[1,128]{1,0:T(1,128)S(1)} %broadcast_in_dim.35.mine, s32[2,896]{1,0:T(2,128)S(1)} %reshape.19.whole), custom_call_target="tpu_custom_call" | custom-call | flops 3000000000 | bytes 9000000 | tf_op jit(solution)/shard_map/plan/pallas_call | solution.py:564
  4.4 6.8 %first.1 = (bf16[168,128,128]{2,1,0:T(8,128)(2,1)S(1)}, bf16[1500,128,128]{2,1,0:T(8,128)(2,1)}, f32[64,10368]{1,0:T(8,128)S(1)}, f32[64,1]{1,0:T(8,128)S(1)}, f...) custom-call(s32[4,256]{1,0:T(4,128)S(1)} %get-tuple-element.52.few, ...), custom_call_target="tpu_custom_call" | custom-call | bytes 27000000 | tf_op jit(solution)/shard_map/first/pallas_call | solution.py:710
  11.4 1.9 %lower.3 = bf16[64,5248]{1,0:T(8,128)(2,1)S(1)} custom-call(s32[4,256]{1,0:T(4,128)S(1)} %get-tuple-element.52.few, s32[8,896]{1,0:T(8,128)S(1)} %get-tuple-element.53.ents, bf16[168,128,128]{2,1,0:T(8,128)(2,1)S(1)} %get-tuple-element.56.compact, bf16[1500,128,128]{2,1,0:T(8,128)(2,1)} %get-tuple-element.57.spill, f32[64,10368]{1,0:T(8,128)S(1)} %get-tuple-element.59.base, ...), custom_call_target="tpu_custom_call" | custom-call | bytes 6000000 | tf_op jit(solution)/shard_map/lower/pallas_call | solution.py:725
  13.7 2.7 %collective-permute-start.1 = (bf16[64,5248]{1,0:T(8,128)(2,1)S(1)}, bf16[64,5248]{1,0:T(8,128)(2,1)S(1)}, u32[]{:S(2)}, u32[]{:S(2)}) collective-permute-start(bf16[64,5248]{1,0:T(8,128)(2,1)S(1)} %add_convert_fusion.2), channel_id=1, source_target_pairs={{0,2},{1,3},{2,0},{3,1},{4,6},{5,7},{6,4},{7,5},{8,10},{9,11},{10,... | collective-permute-start | bytes 2015240 | tf_op jit(solution)/shard_map/ppermute | solution.py:697
  16.6 2.7 %collective-permute-start.2 = (f32[1,72,256]{2,1,0:T(8,128)S(1)}, f32[1,72,256]{2,1,0:T(8,128)S(1)}, u32[]{:S(2)}, u32[]{:S(2)}) collective-permute-start(f32[1,72,256]{2,1,0:T(8,128)S(1)} %bitcast.19), channel_id=1, source_target_pairs={{0,8},{4,12},{8,0},{12,4},{1,9},{5,13},{9,1},{13,5},{2,10},{6,14},... | collective-permute-start | bytes 221192 | tf_op jit(solution)/shard_map/ppermute | solution.py:697
  19.3 4.1 %collective-permute-done.2 = f32[1,72,256]{2,1,0:T(8,128)S(1)} collective-permute-done((f32[1,72,256]{2,1,0:T(8,128)S(1)}, f32[1,72,256]{2,1,0:T(8,128)S(1)}, u32[]{:S(2)}, u32[]{:S(2)}) %collective-permute-start.2) | collective-permute-done | bytes 73760 | tf_op jit(solution)/shard_map/ppermute | solution.py:697
  24.1 4.5 %collective-permute-done.3 = f32[2,72,256]{2,1,0:T(8,128)S(1)} collective-permute-done((f32[2,72,256]{2,1,0:T(8,128)S(1)}, f32[2,72,256]{2,1,0:T(8,128)S(1)}, u32[]{:S(2)}, u32[]{:S(2)}) %collective-permute-start.3) | collective-permute-done | bytes 147488 | tf_op jit(solution)/shard_map/ppermute | solution.py:697
  28.7 1.8 %hourly.3 = (f32[64,896]{1,0:T(8,128)S(1)}, f32[72,896]{1,0:T(8,128)S(1)}, f32[32,8,256]{2,1,0:T(8,128)S(1)}) custom-call(s32[1]{0:T(128)} %bitcast.where, f32[64,896]{1,0:T(8,128)S(1)} %get-tuple-element.65.state, f32[8,896]{1,0:T(8,128)S(1)} %get-tuple-element.66.rows, f32[8,896]{1,0:T(8,128)S(1)} %reshape.21.pars, ...), custom_call_target="tpu_custom_call" | custom-call | bytes 7200000 | tf_op jit(solution)/shard_map/hourly/pallas_call | solution.py:735
  32.7 3.0 %price.3.before = f32[8,64,128]{2,1,0:T(8,128)S(1)} custom-call(s32[4,256]{1,0:T(4,128)S(1)} %get-tuple-element.52.few, s32[8,896]{1,0:T(8,128)S(1)} %get-tuple-element.53.ents, bf16[168,128,128]{2,1,0:T(8,128)(2,1)S(1)} %get-tuple-element.56.compact, bf16[1500,128,128]{2,1,0:T(8,128)(2,1)} %get-tuple-element.57.spill, ...), custom_call_target="tpu_custom_call" | custom-call | bytes 6000000 | tf_op jit(solution)/shard_map/price/pallas_call | solution.py:751
  35.7 4.4 %step.3 = (f32[64,896]{1,0:T(8,128)S(1)}, f32[64,1]{1,0:T(8,128)S(1)}, bf16[64,5248]{1,0:T(8,128)(2,1)S(1)}, bf16[64,128]{1,0:T(8,128)(2,1)S(1)}, bf16[8,64,128]{2,1,0:T(8,128)(2,1)S(1)}) custom-call(s32[4,256]{1,0:T(4,128)S(1)} %get-tuple-element.52.few, s32[8,896]{1,0:T(8,128)S(1)} %get-tuple-element.53.ents, ...), custom_call_target="tpu_custom_call" | custom-call | bytes 12000000 | tf_op jit(solution)/shard_map/step/pallas_call | solution.py:752
  40.2 1.9 %lower.4 = bf16[64,5248]{1,0:T(8,128)(2,1)S(1)} custom-call(s32[4,256]{1,0:T(4,128)S(1)} %get-tuple-element.52.few, s32[8,896]{1,0:T(8,128)S(1)} %get-tuple-element.53.ents, bf16[168,128,128]{2,1,0:T(8,128)(2,1)S(1)} %get-tuple-element.56.compact, bf16[1500,128,128]{2,1,0:T(8,128)(2,1)} %get-tuple-element.57.spill, f32[64,10368]{1,0:T(8,128)S(1)} %get-tuple-element.59.base, ...), custom_call_target="tpu_custom_call" | custom-call | bytes 6000000 | tf_op jit(solution)/shard_map/lower/pallas_call | solution.py:725
  43.8 2.7 %collective-permute-start.8 = (f32[1,72,256]{2,1,0:T(8,128)S(1)}, f32[1,72,256]{2,1,0:T(8,128)S(1)}, u32[]{:S(2)}, u32[]{:S(2)}) collective-permute-start(f32[1,72,256]{2,1,0:T(8,128)S(1)} %bitcast.21), channel_id=1, source_target_pairs={{0,8},{4,12},{8,0},{12,4},{1,9},{5,13},{9,1},{13,5},{2,10},{6,14},... | collective-permute-start | bytes 221192 | tf_op jit(solution)/shard_map/ppermute | solution.py:697
  46.5 4.1 %collective-permute-done.8 = f32[1,72,256]{2,1,0:T(8,128)S(1)} collective-permute-done((f32[1,72,256]{2,1,0:T(8,128)S(1)}, f32[1,72,256]{2,1,0:T(8,128)S(1)}, u32[]{:S(2)}, u32[]{:S(2)}) %collective-permute-start.8) | collective-permute-done | bytes 73760 | tf_op jit(solution)/shard_map/ppermute | solution.py:697
  51.3 4.6 %collective-permute-done.9 = f32[2,72,256]{2,1,0:T(8,128)S(1)} collective-permute-done((f32[2,72,256]{2,1,0:T(8,128)S(1)}, f32[2,72,256]{2,1,0:T(8,128)S(1)}, u32[]{:S(2)}, u32[]{:S(2)}) %collective-permute-start.9) | collective-permute-done | bytes 147488 | tf_op jit(solution)/shard_map/ppermute | solution.py:697
  57.7 2.0 %collective-permute-done.7 = bf16[64,5248]{1,0:T(8,128)(2,1)S(1)} collective-permute-done((bf16[64,5248]{1,0:T(8,128)(2,1)S(1)}, bf16[64,5248]{1,0:T(8,128)(2,1)S(1)}, u32[]{:S(2)}, u32[]{:S(2)}) %collective-permute-start.7) | collective-permute-done | bytes 671776 | tf_op jit(solution)/shard_map/ppermute | solution.py:697
  60.9 2.8 %price.4.before = f32[8,64,128]{2,1,0:T(8,128)S(1)} custom-call(s32[4,256]{1,0:T(4,128)S(1)} %get-tuple-element.52.few, s32[8,896]{1,0:T(8,128)S(1)} %get-tuple-element.53.ents, bf16[168,128,128]{2,1,0:T(8,128)(2,1)S(1)} %get-tuple-element.56.compact, bf16[1500,128,128]{2,1,0:T(8,128)(2,1)} %get-tuple-element.57.spill, ...), custom_call_target="tpu_custom_call" | custom-call | bytes 6000000 | tf_op jit(solution)/shard_map/price/pallas_call | solution.py:751
  63.7 4.6 %step.4 = (f32[64,896]{1,0:T(8,128)S(1)}, f32[64,1]{1,0:T(8,128)S(1)}, bf16[64,5248]{1,0:T(8,128)(2,1)S(1)}, bf16[64,128]{1,0:T(8,128)(2,1)S(1)}, bf16[8,64,128]{2,1,0:T(8,128)(2,1)S(1)}) custom-call(s32[4,256]{1,0:T(4,128)S(1)} %get-tuple-element.52.few, s32[8,896]{1,0:T(8,128)S(1)} %get-tuple-element.53.ents, ...), custom_call_target="tpu_custom_call" | custom-call | bytes 12000000 | tf_op jit(solution)/shard_map/step/pallas_call | solution.py:752
  68.4 1.9 %lower.5 = bf16[64,5248]{1,0:T(8,128)(2,1)S(1)} custom-call(s32[4,256]{1,0:T(4,128)S(1)} %get-tuple-element.52.few, s32[8,896]{1,0:T(8,128)S(1)} %get-tuple-element.53.ents, bf16[168,128,128]{2,1,0:T(8,128)(2,1)S(1)} %get-tuple-element.56.compact, bf16[1500,128,128]{2,1,0:T(8,128)(2,1)} %get-tuple-element.57.spill, f32[64,10368]{1,0:T(8,128)S(1)} %get-tuple-element.59.base, ...), custom_call_target="tpu_custom_call" | custom-call | bytes 6000000 | tf_op jit(solution)/shard_map/lower/pallas_call | solution.py:725
  71.3 3.1 %collective-permute-start.14 = (f32[1,72,256]{2,1,0:T(8,128)S(1)}, f32[1,72,256]{2,1,0:T(8,128)S(1)}, u32[]{:S(2)}, u32[]{:S(2)}) collective-permute-start(f32[1,72,256]{2,1,0:T(8,128)S(1)} %bitcast.23), channel_id=1, source_target_pairs={{0,8},{4,12},{8,0},{12,4},{1,9},{5,13},{9,1},{13,5},{2,10},{6,14},... | collective-permute-start | bytes 221192 | tf_op jit(solution)/shard_map/ppermute | solution.py:697
  74.3 4.2 %collective-permute-done.14 = f32[1,72,256]{2,1,0:T(8,128)S(1)} collective-permute-done((f32[1,72,256]{2,1,0:T(8,128)S(1)}, f32[1,72,256]{2,1,0:T(8,128)S(1)}, u32[]{:S(2)}, u32[]{:S(2)}) %collective-permute-start.14) | collective-permute-done | bytes 73760 | tf_op jit(solution)/shard_map/ppermute | solution.py:697
  79.4 4.3 %collective-permute-done.15 = f32[2,72,256]{2,1,0:T(8,128)S(1)} collective-permute-done((f32[2,72,256]{2,1,0:T(8,128)S(1)}, f32[2,72,256]{2,1,0:T(8,128)S(1)}, u32[]{:S(2)}, u32[]{:S(2)}) %collective-permute-start.15) | collective-permute-done | bytes 147488 | tf_op jit(solution)/shard_map/ppermute | solution.py:697
  85.5 2.4 %collective-permute-done.13 = bf16[64,5248]{1,0:T(8,128)(2,1)S(1)} collective-permute-done((bf16[64,5248]{1,0:T(8,128)(2,1)S(1)}, bf16[64,5248]{1,0:T(8,128)(2,1)S(1)}, u32[]{:S(2)}, u32[]{:S(2)}) %collective-permute-start.13) | collective-permute-done | bytes 671776 | tf_op jit(solution)/shard_map/ppermute | solution.py:697
  90.0 2.8 %price.5.before = f32[8,64,128]{2,1,0:T(8,128)S(1)} custom-call(s32[4,256]{1,0:T(4,128)S(1)} %get-tuple-element.52.few, s32[8,896]{1,0:T(8,128)S(1)} %get-tuple-element.53.ents, bf16[168,128,128]{2,1,0:T(8,128)(2,1)S(1)} %get-tuple-element.56.compact, bf16[1500,128,128]{2,1,0:T(8,128)(2,1)} %get-tuple-element.57.spill, ...), custom_call_target="tpu_custom_call" | custom-call | bytes 6000000 | tf_op jit(solution)/shard_map/price/pallas_call | solution.py:751
  92.8 4.1 %step.5 = (f32[64,640]{1,0:T(8,128)}, f32[64,256]{1,0:T(8,128)}) custom-call(s32[4,256]{1,0:T(4,128)S(1)} %get-tuple-element.52.few, s32[8,896]{1,0:T(8,128)S(1)} %get-tuple-element.53.ents, bf16[168,128,128]{2,1,0:T(8,128)(2,1)S(1)} %get-tuple-element.56.compact, bf16[1500,128,128]{2,1,0:T(8,128)(2,1)} %get-tuple-element.57.spill, ...), custom_call_target="tpu_custom_call" | custom-call | bytes 12000000 | tf_op jit(solution)/shard_map/step/pallas_call | solution.py:752
  (69 shorter events, 16.5 us)
Async XLA Ops:
  2.2 2.1 %copy-start = (bf16[116,128,128]{2,1,0:T(8,128)(2,1)S(1)}, bf16[116,128,128]{2,1,0:T(8,128)(2,1)}, u32[]{:S(2)}) copy-start(bf16[116,128,128]{2,1,0:T(8,128)(2,1)} %tiles.1) | copy-start | bytes 11403268
  2.2 2.2 %copy-start.1 = (bf16[64,4480]{1,0:T(8,128)(2,1)S(1)}, bf16[64,4480]{1,0:T(8,128)(2,1)}, u32[]{:S(2)}) copy-start(bf16[64,4480]{1,0:T(8,128)(2,1)} %load.1) | copy-start | bytes 1720324
  2.2 2.2 %copy-start.2 = (f32[64,640]{1,0:T(8,128)S(1)}, f32[64,640]{1,0:T(8,128)}, u32[]{:S(2)}) copy-start(f32[64,640]{1,0:T(8,128)} %generation.1) | copy-start | bytes 491524
  2.2 2.2 %copy-start.3 = (f32[64,256]{1,0:T(8,128)S(1)}, f32[64,256]{1,0:T(8,128)}, u32[]{:S(2)}) copy-start(f32[64,256]{1,0:T(8,128)} %charging.1) | copy-start | bytes 196612
  11.3 2.2 %collective-permute-start = (bf16[64,5248]{1,0:T(8,128)(2,1)S(1)}, bf16[64,5248]{1,0:T(8,128)(2,1)S(1)}, u32[]{:S(2)}, u32[]{:S(2)}) collective-permute-start(bf16[64,5248]{1,0:T(8,128)(2,1)S(1)} %get-tuple-element.62), channel_id=1, source_target_pairs={{0,1},{1,0},{2,3},{3,2},{4,5},{5,4},{6,7},{7,6},{8,9},{9,8},{10,11... | collective-permute-start | bytes 2015240 | tf_op jit(solution)/shard_map/ppermute | solution.py:697
  13.6 10.3 %copy-start.4 = (f32[10240]{0:T(1024)S(1)}, f32[10240]{0:T(1024)}, u32[]{:S(2)}) copy-start(f32[10240]{0:T(1024)} %param.29) | copy-start | bytes 122884
  13.7 18.0 %collective-permute-start.1 = (bf16[64,5248]{1,0:T(8,128)(2,1)S(1)}, bf16[64,5248]{1,0:T(8,128)(2,1)S(1)}, u32[]{:S(2)}, u32[]{:S(2)}) collective-permute-start(bf16[64,5248]{1,0:T(8,128)(2,1)S(1)} %add_convert_fusion.2), channel_id=1, source_target_pairs={{0,2},{1,3},{2,0},{3,1},{4,6},{5,7},{6,4},{7,5},{8,10},{9,11},{10,... | collective-permute-start | bytes 2015240 | tf_op jit(solution)/shard_map/ppermute | solution.py:697
  16.6 6.8 %collective-permute-start.2 = (f32[1,72,256]{2,1,0:T(8,128)S(1)}, f32[1,72,256]{2,1,0:T(8,128)S(1)}, u32[]{:S(2)}, u32[]{:S(2)}) collective-permute-start(f32[1,72,256]{2,1,0:T(8,128)S(1)} %bitcast.19), channel_id=1, source_target_pairs={{0,8},{4,12},{8,0},{12,4},{1,9},{5,13},{9,1},{13,5},{2,10},{6,14},... | collective-permute-start | bytes 221192 | tf_op jit(solution)/shard_map/ppermute | solution.py:697
  23.4 5.2 %collective-permute-start.3 = (f32[2,72,256]{2,1,0:T(8,128)S(1)}, f32[2,72,256]{2,1,0:T(8,128)S(1)}, u32[]{:S(2)}, u32[]{:S(2)}) collective-permute-start(f32[2,72,256]{2,1,0:T(8,128)S(1)} %pad_maximum_fusion), channel_id=1, source_target_pairs={{0,4},{4,0},{8,12},{12,8},{1,5},{5,1},{9,13},{13,9},{2,6},{6,2},{1... | collective-permute-start | bytes 442376 | tf_op jit(solution)/shard_map/ppermute | solution.py:697
  32.1 3.6 %collective-permute-start.4 = (bf16[64,2560]{1,0:T(8,128)(2,1)S(1)}, bf16[64,2560]{1,0:T(8,128)(2,1)S(1)}, u32[]{:S(2)}, u32[]{:S(2)}) collective-permute-start(bf16[64,2560]{1,0:T(8,128)(2,1)S(1)} %get-tuple-element.105.rest_0_), channel_id=1, source_target_pairs={{0,1},{1,0},{2,3},{3,2},{4,5},{5,4},{6,7},{7,6},{8,9},{9,8},{10,11... | collective-permute-start | bytes 983048 | tf_op jit(solution)/shard_map/ppermute | solution.py:697
  32.2 3.5 %collective-permute-start.5 = (bf16[64,2560]{1,0:T(8,128)(2,1)S(1)}, bf16[64,2560]{1,0:T(8,128)(2,1)S(1)}, u32[]{:S(2)}, u32[]{:S(2)}) collective-permute-start(bf16[64,2560]{1,0:T(8,128)(2,1)S(1)} %get-tuple-element.111.rest_1_), channel_id=1, source_target_pairs={{0,1},{1,0},{2,3},{3,2},{4,5},{5,4},{6,7},{7,6},{8,9},{9,8},{10,11... | collective-permute-start | bytes 983048 | tf_op jit(solution)/shard_map/ppermute | solution.py:697
  40.2 2.2 %collective-permute-start.6 = (bf16[64,5248]{1,0:T(8,128)(2,1)S(1)}, bf16[64,5248]{1,0:T(8,128)(2,1)S(1)}, u32[]{:S(2)}, u32[]{:S(2)}) collective-permute-start(bf16[64,5248]{1,0:T(8,128)(2,1)S(1)} %get-tuple-element.77), channel_id=1, source_target_pairs={{0,1},{1,0},{2,3},{3,2},{4,5},{5,4},{6,7},{7,6},{8,9},{9,8},{10,11... | collective-permute-start | bytes 2015240 | tf_op jit(solution)/shard_map/ppermute | solution.py:697
  42.5 17.2 %collective-permute-start.7 = (bf16[64,5248]{1,0:T(8,128)(2,1)S(1)}, bf16[64,5248]{1,0:T(8,128)(2,1)S(1)}, u32[]{:S(2)}, u32[]{:S(2)}) collective-permute-start(bf16[64,5248]{1,0:T(8,128)(2,1)S(1)} %add_convert_fusion.1), channel_id=1, source_target_pairs={{0,2},{1,3},{2,0},{3,1},{4,6},{5,7},{6,4},{7,5},{8,10},{9,11},{10,... | collective-permute-start | bytes 2015240 | tf_op jit(solution)/shard_map/ppermute | solution.py:697
  43.8 6.8 %collective-permute-start.8 = (f32[1,72,256]{2,1,0:T(8,128)S(1)}, f32[1,72,256]{2,1,0:T(8,128)S(1)}, u32[]{:S(2)}, u32[]{:S(2)}) collective-permute-start(f32[1,72,256]{2,1,0:T(8,128)S(1)} %bitcast.21), channel_id=1, source_target_pairs={{0,8},{4,12},{8,0},{12,4},{1,9},{5,13},{9,1},{13,5},{2,10},{6,14},... | collective-permute-start | bytes 221192 | tf_op jit(solution)/shard_map/ppermute | solution.py:697
  50.7 5.2 %collective-permute-start.9 = (f32[2,72,256]{2,1,0:T(8,128)S(1)}, f32[2,72,256]{2,1,0:T(8,128)S(1)}, u32[]{:S(2)}, u32[]{:S(2)}) collective-permute-start(f32[2,72,256]{2,1,0:T(8,128)S(1)} %pad_maximum_fusion.1), channel_id=1, source_target_pairs={{0,4},{4,0},{8,12},{12,8},{1,5},{5,1},{9,13},{13,9},{2,6},{6,2},{1... | collective-permute-start | bytes 442376 | tf_op jit(solution)/shard_map/ppermute | solution.py:697
  60.3 3.4 %collective-permute-start.10 = (bf16[64,2560]{1,0:T(8,128)(2,1)S(1)}, bf16[64,2560]{1,0:T(8,128)(2,1)S(1)}, u32[]{:S(2)}, u32[]{:S(2)}) collective-permute-start(bf16[64,2560]{1,0:T(8,128)(2,1)S(1)} %get-tuple-element.101.rest_0_), channel_id=1, source_target_pairs={{0,1},{1,0},{2,3},{3,2},{4,5},{5,4},{6,7},{7,6},{8,9},{9,8},{10,11... | collective-permute-start | bytes 983048 | tf_op jit(solution)/shard_map/ppermute | solution.py:697
  60.4 3.3 %collective-permute-start.11 = (bf16[64,2560]{1,0:T(8,128)(2,1)S(1)}, bf16[64,2560]{1,0:T(8,128)(2,1)S(1)}, u32[]{:S(2)}, u32[]{:S(2)}) collective-permute-start(bf16[64,2560]{1,0:T(8,128)(2,1)S(1)} %get-tuple-element.110.rest_1_), channel_id=1, source_target_pairs={{0,1},{1,0},{2,3},{3,2},{4,5},{5,4},{6,7},{7,6},{8,9},{9,8},{10,11... | collective-permute-start | bytes 983048 | tf_op jit(solution)/shard_map/ppermute | solution.py:697
  68.4 2.2 %collective-permute-start.12 = (bf16[64,5248]{1,0:T(8,128)(2,1)S(1)}, bf16[64,5248]{1,0:T(8,128)(2,1)S(1)}, u32[]{:S(2)}, u32[]{:S(2)}) collective-permute-start(bf16[64,5248]{1,0:T(8,128)(2,1)S(1)} %get-tuple-element.89), channel_id=1, source_target_pairs={{0,1},{1,0},{2,3},{3,2},{4,5},{5,4},{6,7},{7,6},{8,9},{9,8},{10,11... | collective-permute-start | bytes 2015240 | tf_op jit(solution)/shard_map/ppermute | solution.py:697
  70.7 17.2 %collective-permute-start.13 = (bf16[64,5248]{1,0:T(8,128)(2,1)S(1)}, bf16[64,5248]{1,0:T(8,128)(2,1)S(1)}, u32[]{:S(2)}, u32[]{:S(2)}) collective-permute-start(bf16[64,5248]{1,0:T(8,128)(2,1)S(1)} %add_convert_fusion), channel_id=1, source_target_pairs={{0,2},{1,3},{2,0},{3,1},{4,6},{5,7},{6,4},{7,5},{8,10},{9,11},{10,... | collective-permute-start | bytes 2015240 | tf_op jit(solution)/shard_map/ppermute | solution.py:697
  71.3 7.2 %collective-permute-start.14 = (f32[1,72,256]{2,1,0:T(8,128)S(1)}, f32[1,72,256]{2,1,0:T(8,128)S(1)}, u32[]{:S(2)}, u32[]{:S(2)}) collective-permute-start(f32[1,72,256]{2,1,0:T(8,128)S(1)} %bitcast.23), channel_id=1, source_target_pairs={{0,8},{4,12},{8,0},{12,4},{1,9},{5,13},{9,1},{13,5},{2,10},{6,14},... | collective-permute-start | bytes 221192 | tf_op jit(solution)/shard_map/ppermute | solution.py:697
  78.5 5.2 %collective-permute-start.15 = (f32[2,72,256]{2,1,0:T(8,128)S(1)}, f32[2,72,256]{2,1,0:T(8,128)S(1)}, u32[]{:S(2)}, u32[]{:S(2)}) collective-permute-start(f32[2,72,256]{2,1,0:T(8,128)S(1)} %pad_maximum_fusion.2), channel_id=1, source_target_pairs={{0,4},{4,0},{8,12},{12,8},{1,5},{5,1},{9,13},{13,9},{2,6},{6,2},{1... | collective-permute-start | bytes 442376 | tf_op jit(solution)/shard_map/ppermute | solution.py:697
  89.5 3.3 %collective-permute-start.16 = (bf16[64,2560]{1,0:T(8,128)(2,1)S(1)}, bf16[64,2560]{1,0:T(8,128)(2,1)S(1)}, u32[]{:S(2)}, u32[]{:S(2)}) collective-permute-start(bf16[64,2560]{1,0:T(8,128)(2,1)S(1)} %get-tuple-element.99.rest_0_), channel_id=1, source_target_pairs={{0,1},{1,0},{2,3},{3,2},{4,5},{5,4},{6,7},{7,6},{8,9},{9,8},{10,11... | collective-permute-start | bytes 983048 | tf_op jit(solution)/shard_map/ppermute | solution.py:697
  89.5 3.3 %collective-permute-start.17 = (bf16[64,2560]{1,0:T(8,128)(2,1)S(1)}, bf16[64,2560]{1,0:T(8,128)(2,1)S(1)}, u32[]{:S(2)}, u32[]{:S(2)}) collective-permute-start(bf16[64,2560]{1,0:T(8,128)(2,1)S(1)} %get-tuple-element.109.rest_1_), channel_id=1, source_target_pairs={{0,1},{1,0},{2,3},{3,2},{4,5},{5,4},{6,7},{7,6},{8,9},{9,8},{10,11... | collective-permute-start | bytes 983048 | tf_op jit(solution)/shard_map/ppermute | solution.py:697

commit v4 on v3

--- a/solution.py
+++ b/solution.py
@@ -53,13 +53,12 @@
 FEW = 256
 LOW = 7
 
-COST, HIGH, RAMP, CAP, LOSS = range(5)
-BUS, TILES = range(2)
+COST, HIGH, RAMP, CAP, LOSS, BUS, TILES = range(7)
 
 
 def plan_kernel(
     chunks, quarter_tiles, kt,
-    mine, whole,
+    mine, pars,
     place, back, sorted_bus, ents, few,
 ):
     units = place.shape[0]
@@ -78,7 +77,7 @@
     def over_lane(mask, values):
         return jnp.sum(jnp.where(mask, values, 0.0), axis=1, keepdims=True)
 
-    bus = whole[BUS : BUS + 1].astype(F32)
+    bus = pars[BUS : BUS + 1]
     unit = lax.broadcasted_iota(jnp.int32, (1, units), 1).astype(F32)
     key = bus * units + unit
     ordered = jnp.zeros((1, units), F32)
@@ -101,8 +100,8 @@
         ).astype(BF16)
         sorted_bus[b] = jnp.broadcast_to(column(ordered[:, b * LANE : (b + 1) * LANE]), square)
 
-    row = whole[TILES : TILES + 1, :LANE]
-    col = whole[TILES : TILES + 1, LANE : 2 * LANE].astype(F32)
+    row = pars[TILES : TILES + 1, :LANE].astype(jnp.int32)
+    col = pars[TILES : TILES + 1, LANE : 2 * LANE]
     chunk = jnp.zeros_like(row)
     for d in range(1, chunks):
         chunk = chunk + (row >= d * quarter_tiles).astype(jnp.int32)
@@ -177,20 +176,21 @@
             copy.start()
             copy.wait()
 
-    def sweep(self, first, last, body):
+    def sweep(self, first, last, body, matrices=None):
+        matrices = self.compact if matrices is None else matrices
         lo, hi = self.few_held[START, first], self.few_held[START, last]
         held, more = self.few_held, self.ents_held
         sweep(
             lo,
             jnp.minimum(hi, self.kept),
-            lambda e, live: body(held[ROW, e], held[BLOCK, e], live, self.compact.at[e]),
+            lambda e, live: body(held[ROW, e], held[BLOCK, e], live, matrices.at[e], True),
         )
 
         def fetched(e, _):
             copy = pltpu.make_async_copy(self.spill.at[e - self.kept], self.stage, self.sems.at[1])
             copy.start()
             copy.wait()
-            body(more[ROW, e], more[BLOCK, e], None, self.stage)
+            body(more[ROW, e], more[BLOCK, e], None, self.stage, False)
             return 0
 
         lax.fori_loop(jnp.maximum(lo, self.kept), hi, fetched, 0)
@@ -258,7 +258,7 @@
     origin, spare = 2 * first * quarter_tiles, 2 * (last - first) * quarter_tiles
     blocks = picked.shape[0] - 1
 
-    def entry(row, m, live, matrix):
+    def entry(row, m, live, matrix, kept):
         row, m = pick(live, row - origin, spare), pick(live, m, blocks)
         total[:, lanes(row)] += mxu(picked[m], matrix[...], NN)
 
@@ -271,20 +271,20 @@
 
 
 def start_prices(bars, lines, quarter_tiles):
-    width = quarter_tiles * LANE
+    width = 2 * quarter_tiles * LANE
     for d, bar in enumerate(bars):
         lines[:, d * width : (d + 1) * width] = bar[...]
 
 
-def add_prices(lists, lines, total, quarter_tiles, first, last):
+def add_prices(lists, turned, lines, total, quarter_tiles, first, last):
     origin = first * quarter_tiles
     spare, blocks = (last - first) * quarter_tiles, total.shape[0] - 1
 
-    def entry(row, m, live, matrix):
+    def entry(row, m, live, matrix, kept):
         row, m = pick(live, row - origin, spare), pick(live, m, blocks)
-        total[m] += mxu(lines[:, lanes(row)], matrix[...], NT)
-
-    lists.sweep(first, last, entry)
+        total[m] += mxu(lines[:, lanes(row)], matrix[...], NN if kept else NT)
+
+    lists.sweep(first, last, entry, turned)
 
 
 def put_picked(z, picked):
@@ -366,11 +366,26 @@
     send_hours(z, own, sent)
 
 
+def turn_kernel(chunks, few, compact, turned, few_held, sem):
+    copy = pltpu.make_async_copy(few, few_held, sem)
+    copy.start()
+    square = (LANE, LANE)
+    eye = lax.broadcasted_iota(jnp.int32, square, 0) == lax.broadcasted_iota(jnp.int32, square, 1)
+    eye = jnp.where(eye, 1.0, 0.0).astype(BF16)
+    copy.wait()
+
+    def entry(e, live):
+        turned[e] = mxu(eye, compact[e], NT).astype(BF16)
+
+    sweep(jnp.int32(0), jnp.minimum(few_held[START, chunks], compact.shape[0] - SMALL), entry)
+
+
 def price_kernel(
     chunks, quarter_tiles, first, last, fresh,
-    few, ents, compact, spill, *rest,
+    few, ents, compact, spill, turned, *rest,
 ):
-    bars, rest = rest[: last - first], rest[last - first :]
+    count = (last - first) // 2
+    bars, rest = rest[:count], rest[count:]
     if not fresh:
         before, rest = rest[0], rest[1:]
     total, few_held, ents_held, stage, sems, lines = rest
@@ -378,18 +393,20 @@
     total[...] = jnp.zeros_like(total) if fresh else before[...]
     start_prices(bars, lines, quarter_tiles)
     lists.ready(chunks)
-    add_prices(lists, lines, total, quarter_tiles, first, last)
+    add_prices(lists, turned, lines, total, quarter_tiles, first, last)
 
 
 def step_kernel(
     chunks, quarter_tiles, balance_step, final,
-    few, ents, compact, spill, before, state, fixed, balance_dual, balances, rows, base, load_sum,
-    back, mine, *rest,
+    few, ents, compact, spill, turned, before, state, fixed, balance_dual, balances, rows, base,
+    load_sum, back, mine, *rest,
 ):
     start = 2
-    bars, rest = rest[: chunks - start], rest[chunks - start :]
+    bars, rest = rest[: chunks // 2 - 1], rest[chunks // 2 - 1 :]
     if final:
-        next_g, next_p, few_held, ents_held, stage, sems, lines, prices = rest
+        dual, next_g, next_p, line_dual, few_held, ents_held, stage, sems, lines, prices = rest
+        out = pltpu.make_async_copy(dual, line_dual, sems.at[2])
+        out.start()
     else:
         next_state, next_balance, *rest = rest
         outs, rest = rest[: chunks // 2 - 1], rest[chunks // 2 - 1 :]
@@ -400,7 +417,7 @@
     if not final:
         start_flows(base, total, quarter_tiles, 1, chunks // 2)
     lists.ready(chunks)
-    add_prices(lists, lines, prices, quarter_tiles, start, chunks)
+    add_prices(lists, turned, lines, prices, quarter_tiles, start, chunks)
     blocks = prices.shape[0] - 1
     price = jnp.concatenate([prices[m] for m in range(blocks)], axis=1)
     old = balance_dual[...]
@@ -414,6 +431,7 @@
         x = joined(mxu(split(z), back[...], NN))
         next_g[...] = x[:, :gens]
         next_p[...] = -x[:, gens:]
+        out.wait()
     else:
         next_state[...] = z
         next_balance[...] = new
@@ -533,32 +551,31 @@
     def like(*shape, dtype=F32):
         return jax.ShapeDtypeStruct(shape, dtype)
 
-    def placed(count, *parts):
+    def placed(*parts):
         total = 0
         for row, at, x in parts:
             before = row * units + at
-            total += jnp.pad(x, (before, count * units - before - x.shape[0]))
-        return total.reshape(count, units)
+            total += jnp.pad(x, (before, 8 * units - before - x.shape[0]))
+        return total
 
     pars = placed(
-        8,
         (COST, 0, gen_cost),
         (HIGH, 0, gen_max),
         (HIGH, gens, stor_power),
         (RAMP, 0, ramp_limit),
         (CAP, gens, stor_cap),
         (LOSS, gens, stor_loss),
-    )
-    whole = placed(
-        2, (BUS, 0, gen_bus), (BUS, gens, stor_bus), (TILES, 0, tile_row), (TILES, LANE, tile_col)
-    )
+    ) + placed(
+        (BUS, 0, gen_bus), (BUS, gens, stor_bus), (TILES, 0, tile_row), (TILES, LANE, tile_col)
+    ).astype(F32)
+    pars = pars.reshape(8, units)
 
     width = -(-(cap + SMALL) // LANE) * LANE
     where = lax.axis_index("tm").astype(jnp.int32).reshape(1)
     near_line = mine.astype(jnp.uint32) * lines
     far_line = (mine ^ (chunks // 2)).astype(jnp.uint32) * lines
-    whole, where, near_line, far_line = lax.optimization_barrier(
-        (whole, where, near_line, far_line)
+    pars, where, near_line, far_line = lax.optimization_barrier(
+        (pars, where, near_line, far_line)
     )
     mine_row = jnp.broadcast_to(mine.astype(jnp.int32), (1, LANE))
     place, back, sorted_bus, ents, few = pl.pallas_call(
@@ -575,7 +592,7 @@
         compiler_params=params(STEP_MIB),
         name="plan",
         cost_estimate=cost(3, 3 * 10**9),
-    )(mine_row, whole)
+    )(mine_row, pars)
 
     pair_out = (like(hours, 2 * lines + LANE, dtype=BF16),)
     step_out = pair_out * (chunks // 2 - 1)
@@ -614,6 +631,16 @@
         cost_estimate=cost(9),
     )
 
+    turn_call = pl.pallas_call(
+        functools.partial(turn_kernel, chunks),
+        out_shape=like(kept + SMALL, LANE, LANE, dtype=BF16),
+        in_specs=[vmem(), vmem()],
+        out_specs=vmem(),
+        scratch_shapes=[pltpu.SMEM((4, FEW), jnp.int32), pltpu.SemaphoreType.DMA],
+        compiler_params=params(STEP_MIB),
+        name="turn",
+        cost_estimate=cost(4),
+    )
     lower_call = pl.pallas_call(
         functools.partial(lower_kernel, chunks, quarter_tiles),
         out_shape=pair_out[0],
@@ -638,7 +665,7 @@
         return pl.pallas_call(
             functools.partial(price_kernel, chunks, quarter_tiles, first, last, fresh),
             out_shape=like(*price_shape),
-            in_specs=lists + [vmem()] * (last - first + (not fresh)),
+            in_specs=lists + [vmem()] * (1 + (last - first) // 2 + (not fresh)),
             out_specs=vmem(),
             scratch_shapes=staging + [line_scratch(last - first)],
             compiler_params=params(STEP_MIB),
@@ -651,15 +678,17 @@
     def step_call(final):
         scratch = staging + [line_scratch(chunks - tail), pltpu.VMEM(price_shape, F32)]
         if final:
-            shape = (like(hours, gens), like(hours, stores))
+            shape = (like(hours, gens), like(hours, stores), like(hours, lines))
+            out_specs = (vmem(), vmem(), hbm())
         else:
             shape = (like(hours, units), like(hours, 1)) + step_out
             scratch += flow_scratch(chunks // 2 - 1)
+            out_specs = (vmem(),) * len(shape)
         return pl.pallas_call(
             functools.partial(step_kernel, chunks, quarter_tiles, balance_step, final),
             out_shape=shape,
-            in_specs=lists + [vmem()] * (10 + chunks - tail),
-            out_specs=(vmem(),) * len(shape),
+            in_specs=lists + [vmem()] * (11 + (chunks - tail) // 2 + final),
+            out_specs=out_specs,
             scratch_shapes=scratch,
             compiler_params=params(STEP_MIB),
             name="step",
@@ -730,33 +759,40 @@
                     sums[d ^ bit] = sums[d ^ bit] + swap(sums[d].astype(BF16), bit).astype(F32)
         ready = sums[0].astype(BF16)
         got = swap(ready, half_way)
-        state, ready = lax.optimization_barrier((state, ready))
+        if iteration == 0:
+            whole_list, state, ready = lax.optimization_barrier((few, state, ready))
+            turned = turn_call(whole_list, compact)
+        else:
+            state, ready = lax.optimization_barrier((state, ready))
         heard = hear(hours_call(state, back)[None], spans)
         fixed, *duals = hourly_call(final)(
             where, state, unit_rows, pars, place, ramp_dual, state_dual,
             *[heard[j] for j in range(years)],
         )
-        got, fixed = lax.optimization_barrier((got, fixed))
+        if iteration == 0:
+            got, fixed, turned = lax.optimization_barrier((got, fixed, turned))
+        else:
+            got, fixed = lax.optimization_barrier((got, fixed))
         ours, theirs = ready.astype(F32), got.astype(F32)
         balances = ours[:, lines : lines + LANE] + theirs[:, lines : lines + LANE]
         near_dual, near = renew(
             near_dual, ours[:, :lines] + theirs[:, lines + LANE :], near_line
         )
         far_dual, far = renew(far_dual, ours[:, lines + LANE :] + theirs[:, :lines], far_line)
-        have = {0: (near, far)}
+        have = {0: jnp.concatenate([near, far], axis=1)}
         for bit in reversed(bits[:-1]):
             for d in list(have):
-                have[d | bit] = tuple(swap(x, bit) for x in have[d])
-        bars = [x for d in range(half_way) for x in have[d]]
-        prices = price_call(0, tail, True)(*held, *bars[:tail])
+                have[d | bit] = swap(have[d], bit)
+        bars = [have[d] for d in range(half_way)]
+        prices = price_call(0, tail, True)(*held, turned, bars[0])
         made = step_call(final)(
-            *held, prices, state, fixed, balance_dual, balances, unit_rows, base, load_sum, back,
-            mine_row, *bars[tail:],
+            *held, turned, prices, state, fixed, balance_dual, balances, unit_rows, base, load_sum, back,
+            mine_row, *bars[1:], *([near_dual] if final else []),
         )
         if not final:
             ramp_dual, state_dual = duals
             state, balance_dual, *made = made
-    return *made, near_dual
+    return made
 
 
 STEP_MIB = 16

time: 96.8 us -> 89.9 us (0.929)
  waiting for transfers between devices: 32.2 us -> 28.1 us
  Pallas kernels: 42.5 us -> 39.8 us
  other arithmetic: 5.01 us -> 3.58 us
    ppermute x18 -> x15, waiting for transfers between devices: 32.2 us -> 28.1 us  [swap(): return lax.ppermute(x, axis, [(i, i ^ bit) for i in range(size)])]
    pallas_call x3, Pallas kernels: 13.1 us -> 10.7 us  [shards(): step_call(final)]
    pallas_call x3 -> x4, Pallas kernels: 8.55 us -> 9.08 us  [the longest x3 5 us: shards(): prices = price_call(0, tail, True)(*held, turned, bars[0])]
    ppermute x18 -> x15, starting transfers between devices: 16 us -> 16.4 us  [swap(): return lax.ppermute(x, axis, [(i, i ^ bit) for i in range(size)])]
  transfers between devices with their start and end apart: 18 -> 15, of which waited for: 12 -> 14; matrix products, arithmetic and copies ran while one was open for 0% -> 1% of each run, Pallas kernels for 21% -> 23%
where the time goes in v4:
time: 89.9 us; the launch traced here: 89.3 us
  Pallas kernels  39.8 us (44%)
  waiting for transfers between devices  28.1 us (31%)
  starting transfers between devices  16.4 us (18%)
  other arithmetic  3.58 us (4%)
  between operations  1.19 us (1%)
    ppermute x15, waiting for transfers between devices, swap(): return lax.ppermute(x, axis, [(i, i ^ bit) for i in range(size)])  28.1 us
    ppermute x15, starting transfers between devices, swap(): return lax.ppermute(x, axis, [(i, i ^ bit) for i in range(size)])  16.4 us
    pallas_call x3, Pallas kernels, shards(): step_call(final)  10.7 us
    pallas_call x1, Pallas kernels, shards(): first_call(few, ents, pars, sorted_bus, load, ptdf_tiles, place, gen_star...  6.47 us
    pallas_call x3, Pallas kernels, shards(): hourly_call(final)  5.4 us
    pallas_call x3, Pallas kernels, shards(): made = [lower_call(*held, base, picked, balance), *made]  5.25 us
    pallas_call x3, Pallas kernels, shards(): prices = price_call(0, tail, True)(*held, turned, bars[0])  5 us
    pallas_call x1, Pallas kernels, shards(): turned = turn_call(whole_list, compact)  4.08 us
  transfers between devices with their start and end apart: 15, of which 14 were waited for; matrix products, arithmetic and copies ran while one was open for 1% of the time, Pallas kernels for 23%

profile of v4, /device:TPU:0, one launch (start us, length us, event | category | flops | bytes accessed | tf_op | source)
XLA Modules:
  0.0 89.3 jit_solution(4146200763464877118)
XLA Ops:
  1.6 2.1 %plan.1 = (bf16[896,896]{1,0:T(8,128)(2,1)S(1)}, bf16[896,896]{1,0:T(8,128)(2,1)S(1)}, f32[7,128,128]{2,1,0:T(8,128)S(1)}, s32[8,896]{1,0:T(8,128)S(1)}, s32[4,256]{1,0:T(4,128)S(1)}) custom-call(s32[1,128]{1,0:T(1,128)S(1)} %broadcast_in_dim.35.mine, f32[8,896]{1,0:T(8,128)S(1)} %reshape.16.pars), custom_call_target="tpu_custom_call" | custom-call | flops 3000000000 | bytes 9000000 | tf_op jit(solution)/shard_map/plan/pallas_call | solution.py:581
  3.7 6.5 %first.1 = (bf16[168,128,128]{2,1,0:T(8,128)(2,1)S(1)}, bf16[1500,128,128]{2,1,0:T(8,128)(2,1)}, f32[64,10368]{1,0:T(8,128)S(1)}, f32[64,1]{1,0:T(8,128)S(1)}, f...) custom-call(s32[4,256]{1,0:T(4,128)S(1)} %get-tuple-element.68.few, ...), custom_call_target="tpu_custom_call" | custom-call | bytes 27000000 | tf_op jit(solution)/shard_map/first/pallas_call | solution.py:739
  10.9 1.7 %lower.3 = bf16[64,5248]{1,0:T(8,128)(2,1)S(1)} custom-call(s32[4,256]{1,0:T(4,128)S(1)} %get-tuple-element.68.few, s32[8,896]{1,0:T(8,128)S(1)} %get-tuple-element.53.ents, bf16[168,128,128]{2,1,0:T(8,128)(2,1)S(1)} %get-tuple-element.56.compact, bf16[1500,128,128]{2,1,0:T(8,128)(2,1)} %get-tuple-element.57.spill, f32[64,10368]{1,0:T(8,128)S(1)} %get-tuple-element.58.base, ...), custom_call_target="tpu_custom_call" | custom-call | bytes 6000000 | tf_op jit(solution)/shard_map/lower/pallas_call | solution.py:754
  12.9 2.6 %collective-permute-start.1 = (bf16[64,5248]{1,0:T(8,128)(2,1)S(1)}, bf16[64,5248]{1,0:T(8,128)(2,1)S(1)}, u32[]{:S(2)}, u32[]{:S(2)}) collective-permute-start(bf16[64,5248]{1,0:T(8,128)(2,1)S(1)} %add_convert_fusion.2), channel_id=1, source_target_pairs={{0,2},{1,3},{2,0},{3,1},{4,6},{5,7},{6,4},{7,5},{8,10},{9,11},{10,... | collective-permute-start | bytes 2015240 | tf_op jit(solution)/shard_map/ppermute | solution.py:726
  15.8 2.7 %collective-permute-start.2 = (f32[1,72,256]{2,1,0:T(8,128)S(1)}, f32[1,72,256]{2,1,0:T(8,128)S(1)}, u32[]{:S(2)}, u32[]{:S(2)}) collective-permute-start(f32[1,72,256]{2,1,0:T(8,128)S(1)} %bitcast.19), channel_id=1, source_target_pairs={{0,8},{4,12},{8,0},{12,4},{1,9},{5,13},{9,1},{13,5},{2,10},{6,14},... | collective-permute-start | bytes 221192 | tf_op jit(solution)/shard_map/ppermute | solution.py:726
  18.4 4.1 %collective-permute-done.2 = f32[1,72,256]{2,1,0:T(8,128)S(1)} collective-permute-done((f32[1,72,256]{2,1,0:T(8,128)S(1)}, f32[1,72,256]{2,1,0:T(8,128)S(1)}, u32[]{:S(2)}, u32[]{:S(2)}) %collective-permute-start.2) | collective-permute-done | bytes 73760 | tf_op jit(solution)/shard_map/ppermute | solution.py:726
  23.3 4.1 %turn.1.turned = bf16[168,128,128]{2,1,0:T(8,128)(2,1)S(1)} custom-call(s32[4,256]{1,0:T(4,128)S(1)} %get-tuple-element.68.few, bf16[168,128,128]{2,1,0:T(8,128)(2,1)S(1)} %get-tuple-element.56.compact), custom_call_target="tpu_custom_call" | custom-call | bytes 12000000 | tf_op jit(solution)/shard_map/turn/pallas_call | solution.py:764
  27.8 1.8 %hourly.3 = (f32[64,896]{1,0:T(8,128)S(1)}, f32[72,896]{1,0:T(8,128)S(1)}, f32[32,8,256]{2,1,0:T(8,128)S(1)}) custom-call(s32[1]{0:T(128)} %bitcast.where, f32[64,896]{1,0:T(8,128)S(1)} %get-tuple-element.64.state, f32[8,896]{1,0:T(8,128)S(1)} %get-tuple-element.65.rows, f32[8,896]{1,0:T(8,128)S(1)} %reshape.16.pars, ...), custom_call_target="tpu_custom_call" | custom-call | bytes 7200000 | tf_op jit(solution)/shard_map/hourly/pallas_call | solution.py:768
  31.4 1.8 %price.3.before = f32[8,64,128]{2,1,0:T(8,128)S(1)} custom-call(s32[4,256]{1,0:T(4,128)S(1)} %get-tuple-element.68.few, s32[8,896]{1,0:T(8,128)S(1)} %get-tuple-element.53.ents, bf16[168,128,128]{2,1,0:T(8,128)(2,1)S(1)} %get-tuple-element.56.compact, bf16[1500,128,128]{2,1,0:T(8,128)(2,1)} %get-tuple-element.57.spill, ...), custom_call_target="tpu_custom_call" | custom-call | bytes 6000000 | tf_op jit(solution)/shard_map/price/pallas_call | solution.py:787
  33.5 3.7 %step.3 = (f32[64,896]{1,0:T(8,128)S(1)}, f32[64,1]{1,0:T(8,128)S(1)}, bf16[64,5248]{1,0:T(8,128)(2,1)S(1)}, bf16[64,128]{1,0:T(8,128)(2,1)S(1)}, bf16[8,64,128]{2,1,0:T(8,128)(2,1)S(1)}) custom-call(s32[4,256]{1,0:T(4,128)S(1)} %get-tuple-element.68.few, s32[8,896]{1,0:T(8,128)S(1)} %get-tuple-element.53.ents, ...), custom_call_target="tpu_custom_call" | custom-call | bytes 12000000 | tf_op jit(solution)/shard_map/step/pallas_call | solution.py:788
  37.3 1.7 %lower.4 = bf16[64,5248]{1,0:T(8,128)(2,1)S(1)} custom-call(s32[4,256]{1,0:T(4,128)S(1)} %get-tuple-element.68.few, s32[8,896]{1,0:T(8,128)S(1)} %get-tuple-element.53.ents, bf16[168,128,128]{2,1,0:T(8,128)(2,1)S(1)} %get-tuple-element.56.compact, bf16[1500,128,128]{2,1,0:T(8,128)(2,1)} %get-tuple-element.57.spill, f32[64,10368]{1,0:T(8,128)S(1)} %get-tuple-element.58.base, ...), custom_call_target="tpu_custom_call" | custom-call | bytes 6000000 | tf_op jit(solution)/shard_map/lower/pallas_call | solution.py:754
  39.5 1.7 %collective-permute-start.6 = (bf16[64,5248]{1,0:T(8,128)(2,1)S(1)}, bf16[64,5248]{1,0:T(8,128)(2,1)S(1)}, u32[]{:S(2)}, u32[]{:S(2)}) collective-permute-start(bf16[64,5248]{1,0:T(8,128)(2,1)S(1)} %add_convert_fusion.1), channel_id=1, source_target_pairs={{0,2},{1,3},{2,0},{3,1},{4,6},{5,7},{6,4},{7,5},{8,10},{9,11},{10,... | collective-permute-start | bytes 2015240 | tf_op jit(solution)/shard_map/ppermute | solution.py:726
  41.5 2.7 %collective-permute-start.7 = (f32[1,72,256]{2,1,0:T(8,128)S(1)}, f32[1,72,256]{2,1,0:T(8,128)S(1)}, u32[]{:S(2)}, u32[]{:S(2)}) collective-permute-start(f32[1,72,256]{2,1,0:T(8,128)S(1)} %bitcast.21), channel_id=1, source_target_pairs={{0,8},{4,12},{8,0},{12,4},{1,9},{5,13},{9,1},{13,5},{2,10},{6,14},... | collective-permute-start | bytes 221192 | tf_op jit(solution)/shard_map/ppermute | solution.py:726
  44.1 4.1 %collective-permute-done.7 = f32[1,72,256]{2,1,0:T(8,128)S(1)} collective-permute-done((f32[1,72,256]{2,1,0:T(8,128)S(1)}, f32[1,72,256]{2,1,0:T(8,128)S(1)}, u32[]{:S(2)}, u32[]{:S(2)}) %collective-permute-start.7) | collective-permute-done | bytes 73760 | tf_op jit(solution)/shard_map/ppermute | solution.py:726
  48.9 4.6 %collective-permute-done.8 = f32[2,72,256]{2,1,0:T(8,128)S(1)} collective-permute-done((f32[2,72,256]{2,1,0:T(8,128)S(1)}, f32[2,72,256]{2,1,0:T(8,128)S(1)}, u32[]{:S(2)}, u32[]{:S(2)}) %collective-permute-start.8) | collective-permute-done | bytes 147488 | tf_op jit(solution)/shard_map/ppermute | solution.py:726
  53.5 1.8 %hourly.4 = (f32[64,896]{1,0:T(8,128)S(1)}, f32[72,896]{1,0:T(8,128)S(1)}, f32[32,8,256]{2,1,0:T(8,128)S(1)}) custom-call(s32[1]{0:T(128)} %bitcast.where, f32[64,896]{1,0:T(8,128)S(1)} %get-tuple-element.81.state, f32[8,896]{1,0:T(8,128)S(1)} %get-tuple-element.65.rows, f32[8,896]{1,0:T(8,128)S(1)} %reshape.16.pars, ...), custom_call_target="tpu_custom_call" | custom-call | bytes 7200000 | tf_op jit(solution)/shard_map/hourly/pallas_call | solution.py:768
  57.5 1.6 %price.4.before = f32[8,64,128]{2,1,0:T(8,128)S(1)} custom-call(s32[4,256]{1,0:T(4,128)S(1)} %get-tuple-element.68.few, s32[8,896]{1,0:T(8,128)S(1)} %get-tuple-element.53.ents, bf16[168,128,128]{2,1,0:T(8,128)(2,1)S(1)} %get-tuple-element.56.compact, bf16[1500,128,128]{2,1,0:T(8,128)(2,1)} %get-tuple-element.57.spill, ...), custom_call_target="tpu_custom_call" | custom-call | bytes 6000000 | tf_op jit(solution)/shard_map/price/pallas_call | solution.py:787
  59.5 3.7 %step.4 = (f32[64,896]{1,0:T(8,128)S(1)}, f32[64,1]{1,0:T(8,128)S(1)}, bf16[64,5248]{1,0:T(8,128)(2,1)S(1)}, bf16[64,128]{1,0:T(8,128)(2,1)S(1)}, bf16[8,64,128]{2,1,0:T(8,128)(2,1)S(1)}) custom-call(s32[4,256]{1,0:T(4,128)S(1)} %get-tuple-element.68.few, s32[8,896]{1,0:T(8,128)S(1)} %get-tuple-element.53.ents, ...), custom_call_target="tpu_custom_call" | custom-call | bytes 12000000 | tf_op jit(solution)/shard_map/step/pallas_call | solution.py:788
  63.3 1.9 %lower.5 = bf16[64,5248]{1,0:T(8,128)(2,1)S(1)} custom-call(s32[4,256]{1,0:T(4,128)S(1)} %get-tuple-element.68.few, s32[8,896]{1,0:T(8,128)S(1)} %get-tuple-element.53.ents, bf16[168,128,128]{2,1,0:T(8,128)(2,1)S(1)} %get-tuple-element.56.compact, bf16[1500,128,128]{2,1,0:T(8,128)(2,1)} %get-tuple-element.57.spill, f32[64,10368]{1,0:T(8,128)S(1)} %get-tuple-element.58.base, ...), custom_call_target="tpu_custom_call" | custom-call | bytes 6000000 | tf_op jit(solution)/shard_map/lower/pallas_call | solution.py:754
  67.4 2.7 %collective-permute-start.12 = (f32[1,72,256]{2,1,0:T(8,128)S(1)}, f32[1,72,256]{2,1,0:T(8,128)S(1)}, u32[]{:S(2)}, u32[]{:S(2)}) collective-permute-start(f32[1,72,256]{2,1,0:T(8,128)S(1)} %bitcast.23), channel_id=1, source_target_pairs={{0,8},{4,12},{8,0},{12,4},{1,9},{5,13},{9,1},{13,5},{2,10},{6,14},... | collective-permute-start | bytes 221192 | tf_op jit(solution)/shard_map/ppermute | solution.py:726
  70.1 4.2 %collective-permute-done.12 = f32[1,72,256]{2,1,0:T(8,128)S(1)} collective-permute-done((f32[1,72,256]{2,1,0:T(8,128)S(1)}, f32[1,72,256]{2,1,0:T(8,128)S(1)}, u32[]{:S(2)}, u32[]{:S(2)}) %collective-permute-start.12) | collective-permute-done | bytes 73760 | tf_op jit(solution)/shard_map/ppermute | solution.py:726
  74.9 4.6 %collective-permute-done.13 = f32[2,72,256]{2,1,0:T(8,128)S(1)} collective-permute-done((f32[2,72,256]{2,1,0:T(8,128)S(1)}, f32[2,72,256]{2,1,0:T(8,128)S(1)}, u32[]{:S(2)}, u32[]{:S(2)}) %collective-permute-start.13) | collective-permute-done | bytes 147488 | tf_op jit(solution)/shard_map/ppermute | solution.py:726
  79.5 1.8 %hourly.5.fixed = f32[64,896]{1,0:T(8,128)S(1)} custom-call(s32[1]{0:T(128)} %bitcast.where, f32[64,896]{1,0:T(8,128)S(1)} %get-tuple-element.93.state, f32[8,896]{1,0:T(8,128)S(1)} %get-tuple-element.65.rows, f32[8,896]{1,0:T(8,128)S(1)} %reshape.16.pars, bf16[896,896]{1,0:T(8,128)(2,1)S(1)} %get-tuple-element.55.place, ...), custom_call_target="tpu_custom_call" | custom-call | bytes 7200000 | tf_op jit(solution)/shard_map/hourly/pallas_call | solution.py:768
  85.7 3.4 %step.5 = (f32[64,640]{1,0:T(8,128)}, f32[64,256]{1,0:T(8,128)}, f32[64,2560]{1,0:T(8,128)}) custom-call(s32[4,256]{1,0:T(4,128)S(1)} %get-tuple-element.68.few, s32[8,896]{1,0:T(8,128)S(1)} %get-tuple-element.53.ents, bf16[168,128,128]{2,1,0:T(8,128)(2,1)S(1)} %get-tuple-element.56.compact, bf16[1500,128,128]{2,1,0:T(8,128)(2,1)} %get-tuple-element.57.spill, ...), custom_call_target="tpu_custom_call" | custom-call | bytes 12000000 | tf_op jit(solution)/shard_map/step/pallas_call | solution.py:788
  (65 shorter events, 16.8 us)
Async XLA Ops:
  1.5 2.1 %copy-start = (bf16[116,128,128]{2,1,0:T(8,128)(2,1)S(1)}, bf16[116,128,128]{2,1,0:T(8,128)(2,1)}, u32[]{:S(2)}) copy-start(bf16[116,128,128]{2,1,0:T(8,128)(2,1)} %tiles.1) | copy-start | bytes 11403268
  1.5 2.2 %copy-start.1 = (bf16[64,4480]{1,0:T(8,128)(2,1)S(1)}, bf16[64,4480]{1,0:T(8,128)(2,1)}, u32[]{:S(2)}) copy-start(bf16[64,4480]{1,0:T(8,128)(2,1)} %load.1) | copy-start | bytes 1720324
  1.5 2.2 %copy-start.2 = (f32[64,640]{1,0:T(8,128)S(1)}, f32[64,640]{1,0:T(8,128)}, u32[]{:S(2)}) copy-start(f32[64,640]{1,0:T(8,128)} %generation.1) | copy-start | bytes 491524
  1.5 2.2 %copy-start.3 = (f32[64,256]{1,0:T(8,128)S(1)}, f32[64,256]{1,0:T(8,128)}, u32[]{:S(2)}) copy-start(f32[64,256]{1,0:T(8,128)} %charging.1) | copy-start | bytes 196612
  10.2 2.5 %collective-permute-start = (bf16[64,5248]{1,0:T(8,128)(2,1)S(1)}, bf16[64,5248]{1,0:T(8,128)(2,1)S(1)}, u32[]{:S(2)}, u32[]{:S(2)}) collective-permute-start(bf16[64,5248]{1,0:T(8,128)(2,1)S(1)} %get-tuple-element.61), channel_id=1, source_target_pairs={{0,1},{1,0},{2,3},{3,2},{4,5},{5,4},{6,7},{7,6},{8,9},{9,8},{10,11... | collective-permute-start | bytes 2015240 | tf_op jit(solution)/shard_map/ppermute | solution.py:726
  12.9 10.2 %copy-start.4 = (f32[10240]{0:T(1024)S(1)}, f32[10240]{0:T(1024)}, u32[]{:S(2)}) copy-start(f32[10240]{0:T(1024)} %param.29) | copy-start | bytes 122884
  12.9 18.0 %collective-permute-start.1 = (bf16[64,5248]{1,0:T(8,128)(2,1)S(1)}, bf16[64,5248]{1,0:T(8,128)(2,1)S(1)}, u32[]{:S(2)}, u32[]{:S(2)}) collective-permute-start(bf16[64,5248]{1,0:T(8,128)(2,1)S(1)} %add_convert_fusion.2), channel_id=1, source_target_pairs={{0,2},{1,3},{2,0},{3,1},{4,6},{5,7},{6,4},{7,5},{8,10},{9,11},{10,... | collective-permute-start | bytes 2015240 | tf_op jit(solution)/shard_map/ppermute | solution.py:726
  15.8 6.8 %collective-permute-start.2 = (f32[1,72,256]{2,1,0:T(8,128)S(1)}, f32[1,72,256]{2,1,0:T(8,128)S(1)}, u32[]{:S(2)}, u32[]{:S(2)}) collective-permute-start(f32[1,72,256]{2,1,0:T(8,128)S(1)} %bitcast.19), channel_id=1, source_target_pairs={{0,8},{4,12},{8,0},{12,4},{1,9},{5,13},{9,1},{13,5},{2,10},{6,14},... | collective-permute-start | bytes 221192 | tf_op jit(solution)/shard_map/ppermute | solution.py:726
  22.6 5.2 %collective-permute-start.3 = (f32[2,72,256]{2,1,0:T(8,128)S(1)}, f32[2,72,256]{2,1,0:T(8,128)S(1)}, u32[]{:S(2)}, u32[]{:S(2)}) collective-permute-start(f32[2,72,256]{2,1,0:T(8,128)S(1)} %pad_maximum_fusion.3), channel_id=1, source_target_pairs={{0,4},{4,0},{8,12},{12,8},{1,5},{5,1},{9,13},{13,9},{2,6},{6,2},{1... | collective-permute-start | bytes 442376 | tf_op jit(solution)/shard_map/ppermute | solution.py:726
  31.3 2.2 %collective-permute-start.4 = (bf16[64,5120]{1,0:T(8,128)(2,1)S(1)}, bf16[64,5120]{1,0:T(8,128)(2,1)S(1)}, u32[]{:S(2)}, u32[]{:S(2)}) collective-permute-start(bf16[64,5120]{1,0:T(8,128)(2,1)S(1)} %pad_maximum_fusion.rest_0_), channel_id=1, source_target_pairs={{0,1},{1,0},{2,3},{3,2},{4,5},{5,4},{6,7},{7,6},{8,9},{9,8},{10,11... | collective-permute-start | bytes 1966088 | tf_op jit(solution)/shard_map/ppermute | solution.py:726
  37.2 2.2 %collective-permute-start.5 = (bf16[64,5248]{1,0:T(8,128)(2,1)S(1)}, bf16[64,5248]{1,0:T(8,128)(2,1)S(1)}, u32[]{:S(2)}, u32[]{:S(2)}) collective-permute-start(bf16[64,5248]{1,0:T(8,128)(2,1)S(1)} %get-tuple-element.79), channel_id=1, source_target_pairs={{0,1},{1,0},{2,3},{3,2},{4,5},{5,4},{6,7},{7,6},{8,9},{9,8},{10,11... | collective-permute-start | bytes 2015240 | tf_op jit(solution)/shard_map/ppermute | solution.py:726
  39.5 17.2 %collective-permute-start.6 = (bf16[64,5248]{1,0:T(8,128)(2,1)S(1)}, bf16[64,5248]{1,0:T(8,128)(2,1)S(1)}, u32[]{:S(2)}, u32[]{:S(2)}) collective-permute-start(bf16[64,5248]{1,0:T(8,128)(2,1)S(1)} %add_convert_fusion.1), channel_id=1, source_target_pairs={{0,2},{1,3},{2,0},{3,1},{4,6},{5,7},{6,4},{7,5},{8,10},{9,11},{10,... | collective-permute-start | bytes 2015240 | tf_op jit(solution)/shard_map/ppermute | solution.py:726
  41.5 6.8 %collective-permute-start.7 = (f32[1,72,256]{2,1,0:T(8,128)S(1)}, f32[1,72,256]{2,1,0:T(8,128)S(1)}, u32[]{:S(2)}, u32[]{:S(2)}) collective-permute-start(f32[1,72,256]{2,1,0:T(8,128)S(1)} %bitcast.21), channel_id=1, source_target_pairs={{0,8},{4,12},{8,0},{12,4},{1,9},{5,13},{9,1},{13,5},{2,10},{6,14},... | collective-permute-start | bytes 221192 | tf_op jit(solution)/shard_map/ppermute | solution.py:726
  48.3 5.2 %collective-permute-start.8 = (f32[2,72,256]{2,1,0:T(8,128)S(1)}, f32[2,72,256]{2,1,0:T(8,128)S(1)}, u32[]{:S(2)}, u32[]{:S(2)}) collective-permute-start(f32[2,72,256]{2,1,0:T(8,128)S(1)} %pad_maximum_fusion.4), channel_id=1, source_target_pairs={{0,4},{4,0},{8,12},{12,8},{1,5},{5,1},{9,13},{13,9},{2,6},{6,2},{1... | collective-permute-start | bytes 442376 | tf_op jit(solution)/shard_map/ppermute | solution.py:726
  57.4 2.2 %collective-permute-start.9 = (bf16[64,5120]{1,0:T(8,128)(2,1)S(1)}, bf16[64,5120]{1,0:T(8,128)(2,1)S(1)}, u32[]{:S(2)}, u32[]{:S(2)}) collective-permute-start(bf16[64,5120]{1,0:T(8,128)(2,1)S(1)} %pad_maximum_fusion.1.rest_0_), channel_id=1, source_target_pairs={{0,1},{1,0},{2,3},{3,2},{4,5},{5,4},{6,7},{7,6},{8,9},{9,8},{10,11... | collective-permute-start | bytes 1966088 | tf_op jit(solution)/shard_map/ppermute | solution.py:726
  63.2 2.2 %collective-permute-start.10 = (bf16[64,5248]{1,0:T(8,128)(2,1)S(1)}, bf16[64,5248]{1,0:T(8,128)(2,1)S(1)}, u32[]{:S(2)}, u32[]{:S(2)}) collective-permute-start(bf16[64,5248]{1,0:T(8,128)(2,1)S(1)} %get-tuple-element.91), channel_id=1, source_target_pairs={{0,1},{1,0},{2,3},{3,2},{4,5},{5,4},{6,7},{7,6},{8,9},{9,8},{10,11... | collective-permute-start | bytes 2015240 | tf_op jit(solution)/shard_map/ppermute | solution.py:726
  65.6 17.2 %collective-permute-start.11 = (bf16[64,5248]{1,0:T(8,128)(2,1)S(1)}, bf16[64,5248]{1,0:T(8,128)(2,1)S(1)}, u32[]{:S(2)}, u32[]{:S(2)}) collective-permute-start(bf16[64,5248]{1,0:T(8,128)(2,1)S(1)} %add_convert_fusion), channel_id=1, source_target_pairs={{0,2},{1,3},{2,0},{3,1},{4,6},{5,7},{6,4},{7,5},{8,10},{9,11},{10,... | collective-permute-start | bytes 2015240 | tf_op jit(solution)/shard_map/ppermute | solution.py:726
  67.4 6.8 %collective-permute-start.12 = (f32[1,72,256]{2,1,0:T(8,128)S(1)}, f32[1,72,256]{2,1,0:T(8,128)S(1)}, u32[]{:S(2)}, u32[]{:S(2)}) collective-permute-start(f32[1,72,256]{2,1,0:T(8,128)S(1)} %bitcast.23), channel_id=1, source_target_pairs={{0,8},{4,12},{8,0},{12,4},{1,9},{5,13},{9,1},{13,5},{2,10},{6,14},... | collective-permute-start | bytes 221192 | tf_op jit(solution)/shard_map/ppermute | solution.py:726
  74.3 5.2 %collective-permute-start.13 = (f32[2,72,256]{2,1,0:T(8,128)S(1)}, f32[2,72,256]{2,1,0:T(8,128)S(1)}, u32[]{:S(2)}, u32[]{:S(2)}) collective-permute-start(f32[2,72,256]{2,1,0:T(8,128)S(1)} %pad_maximum_fusion.5), channel_id=1, source_target_pairs={{0,4},{4,0},{8,12},{12,8},{1,5},{5,1},{9,13},{13,9},{2,6},{6,2},{1... | collective-permute-start | bytes 442376 | tf_op jit(solution)/shard_map/ppermute | solution.py:726
  83.6 2.2 %collective-permute-start.14 = (bf16[64,5120]{1,0:T(8,128)(2,1)S(1)}, bf16[64,5120]{1,0:T(8,128)(2,1)S(1)}, u32[]{:S(2)}, u32[]{:S(2)}) collective-permute-start(bf16[64,5120]{1,0:T(8,128)(2,1)S(1)} %pad_maximum_fusion.2.rest_0_), channel_id=1, source_target_pairs={{0,1},{1,0},{2,3},{3,2},{4,5},{5,4},{6,7},{7,6},{8,9},{9,8},{10,11... | collective-permute-start | bytes 1966088 | tf_op jit(solution)/shard_map/ppermute | solution.py:726
